TPU v7x, 512 devices: a whole 4x8x8 slice. The times are simulated.
512 devices in a mesh: panel: 2 (over core), lat: 8 (over y), lon: 32 (over z, x).
Axes of the slice: x: 4, y: 8, z: 8, core: 2. Of those that a mesh axis runs over, the one named last changes fastest.
Arguments:
- fields: bfloat16 [2, 6, 24, 128, 4096], P('panel', None, None, 'lat', 'lon'), may hold values from -6 to 6
- departure_frac: float32 [2, 24, 128, 4096], P('panel', None, 'lat', 'lon'), may hold values from 0 to 1
- block_shift: int32 [2, 128, 32], P('panel', 'lat'), may hold values from 0 to 3, as said below
- level_mix: float32 [6, 24], replicated, may hold values from -2.5 to 2.5
- projection: float32 [24, 24], replicated, may hold values from -1.25 to 1.25
- mode_shift: float32 [24], replicated, may hold values from 0.02 to 2
- margin_cells: int32 [2, 8, 8192], P('panel', 'lat', 'lon'), may hold values from 0 to 2047, as said below
- margin_source: int32 [2, 8, 8192, 4], P('panel', 'lat', 'lon'), may hold values from 0 to 2047
- margin_weight: float32 [2, 8, 8192, 4], P('panel', 'lat', 'lon'), may hold values from 0.05 to 0.45
Outputs:
- advected: bfloat16 [2, 6, 24, 128, 4096], P('panel', None, None, 'lat', 'lon')
- solution: float32 [2, 24, 128, 4096], P('panel', None, 'lat', 'lon')
- residual: float32 [2, 24, 128, 4096], P('panel', None, 'lat', 'lon')
Inputs may be any that keep to these rules, and one draw needn't show every extreme that they name: Row r of panel p on lon device d takes its departure points 32 * block_shift[p, r, d] columns below its own. On every device the rows 2i and 2i + 1 of its block have values summing to at most 3, so the sum of block_shift + 1 over one device's 16 rows is at most 40, and some device reaches 40 in every draw. `margin_cells`: for each device, 256 distinct cell numbers row * 128 + column of its own block. `margin_source`: cell numbers row * 128 + column in the block of the device with the same lat and lon indices on the other panel.
All inputs are finite; a program needn't handle non-finite values.
Results may differ from a plain program's by a relative error of at most 0.0026.
Values may be sent and summed in bfloat16 or wider, within the bound.
No kernel may reach another device: no remote copies, remote signals or barrier semaphores. Data moves between devices by JAX's collectives and lax.ppermute only.
A program may use at most 64 MiB of HBM per device.

v0:
```python
import jax
import jax.numpy as jnp
from jax import lax
from jax.sharding import PartitionSpec as P

BW = 32
ITERS = 3


def padded_2(cells, sides, width):
    for axis, dim in sides:
        count = lax.axis_size(axis)
        ends = count - 1
        head = lax.slice_in_dim(cells, 0, width, axis=dim)
        tail = lax.slice_in_dim(cells, cells.shape[dim] - width, cells.shape[dim], axis=dim)
        cells = jnp.concatenate(
            [
                lax.ppermute(tail, axis, [(i, (i + 1) % count) for i in range(ends)]),
                cells,
                lax.ppermute(head, axis, [((i + 1) % count, i) for i in range(ends)]),
            ],
            axis=dim,
        )
    return cells


def from_behind(shard, axis, by):
    count = lax.axis_size(axis)
    pairs = [(i, i + by) for i in range(count) if 0 <= i + by < count]
    return lax.ppermute(shard, axis, pairs)


def partner(block, axis, bit):
    count = lax.axis_size(axis)
    route = []
    for low in range(count):
        high = low | 1 << bit
        if high != low and high < count:
            route += [(low, high), (high, low)]
    return lax.ppermute(block, axis, route)


def cubic_values(window, offset):
    width = offset.shape[-1]
    weight_a = -offset * (offset - 1.0) * (offset - 2.0) / 6.0
    weight_b = (offset + 1.0) * (offset - 1.0) * (offset - 2.0) / 2.0
    weight_c = -(offset + 1.0) * offset * (offset - 2.0) / 2.0
    weight_d = (offset + 1.0) * offset * (offset - 1.0) / 6.0
    total = weight_a * window[..., 0:width].astype(jnp.float32)
    total = total + weight_b * window[..., 1 : width + 1].astype(jnp.float32)
    total = total + weight_c * window[..., 2 : width + 2].astype(jnp.float32)
    return total + weight_d * window[..., 3 : width + 3].astype(jnp.float32)


def operate(field, mode_shift):
    padded = padded_2(field, (("lat", 2), ("lon", 3)), 1)
    beside = (
        padded[:, :, 2:, 1:-1]
        + padded[:, :, :-2, 1:-1]
        + padded[:, :, 1:-1, 2:]
        + padded[:, :, 1:-1, :-2]
    )
    return (4.0 + mode_shift[None, :, None, None]) * field - beside


def local_inner(left, right):
    return jnp.sum(left * right, axis=(0, 2, 3))


def expand(scalars):
    return scalars[None, :, None, None]


def per_device(
    fields,
    departure_frac,
    block_shift,
    level_mix,
    projection,
    mode_shift,
    margin_cells,
    margin_source,
    margin_weight,
):
    local_fields = fields[0]
    field_count, levels, row_count, column_count = local_fields.shape
    lon_index = lax.axis_index("lon")
    shift_table = block_shift[0]
    own_shift = lax.dynamic_index_in_dim(shift_table, lon_index, axis=1, keepdims=False)
    source_table = margin_source[0, 0].T
    weight_table = margin_weight[0, 0].T
    east_edge = from_behind(local_fields[..., :2], "lon", -1)
    western = from_behind(local_fields, "lon", 1)
    extended = jnp.concatenate([western, local_fields, east_edge], axis=3)
    starts = column_count - 1 - own_shift * BW

    def slice_window(strip, start):
        return lax.dynamic_slice_in_dim(strip, start, column_count + 3, axis=2)

    windows = jax.vmap(slice_window, in_axes=(2, 0), out_axes=2)(extended, starts)
    advected = cubic_values(windows, departure_frac[0]).astype(jnp.bfloat16)
    level_rhs = jnp.zeros((levels, row_count, column_count), jnp.float32)
    for field_index in range(field_count):
        level_rhs = level_rhs + level_mix[field_index][:, None, None] * advected[
            field_index
        ].astype(jnp.float32)
    flat_rhs = level_rhs.reshape(levels, row_count * column_count)
    partner_rhs = partner(flat_rhs.astype(jnp.bfloat16), "panel", 0).astype(flat_rhs.dtype)
    picked = partner_rhs[:, source_table]
    replaced = jnp.sum(picked * weight_table[None], axis=1)
    joined_rhs = flat_rhs.at[:, margin_cells[0, 0]].set(replaced)
    modal_rhs = jnp.dot(
        projection, joined_rhs, precision=lax.Precision.HIGHEST, preferred_element_type=jnp.float32
    )
    modal_rhs = modal_rhs.reshape(1, levels, row_count, column_count)
    solution = jnp.zeros_like(modal_rhs)
    residual = modal_rhs
    directions = [modal_rhs]
    images = [operate(modal_rhs, mode_shift)]
    norms = []
    for iteration in range(ITERS):
        along, square = lax.psum(
            (
                local_inner(residual, images[iteration]),
                local_inner(images[iteration], images[iteration]),
            ),
            ("panel", "lat", "lon"),
        )
        norms.append(square)
        ratio = along / square
        solution = solution + expand(ratio) * directions[iteration]
        residual = residual - expand(ratio) * images[iteration]
        if iteration + 1 < ITERS:
            fresh = operate(residual, mode_shift)
            crossed = lax.psum(
                jnp.stack([local_inner(fresh, image) for image in images]), ("panel", "lat", "lon")
            )
            direction, image_next = (residual, fresh)
            for earlier in range(iteration + 1):
                beta = -crossed[earlier] / norms[earlier]
                direction = direction + expand(beta) * directions[earlier]
                image_next = image_next + expand(beta) * images[earlier]
            directions.append(direction)
            images.append(image_next)
    return (advected[None], solution, residual)


def solution(mesh):
    in_specs = (
        P("panel", None, None, "lat", "lon"),
        P("panel", None, "lat", "lon"),
        P("panel", "lat", None),
        P(),
        P(),
        P(),
        P("panel", "lat", "lon"),
        P("panel", "lat", "lon", None),
        P("panel", "lat", "lon", None),
    )
    out_specs = (
        P("panel", None, None, "lat", "lon"),
        P("panel", None, "lat", "lon"),
        P("panel", None, "lat", "lon"),
    )
    return jax.shard_map(
        per_device, mesh=mesh, in_specs=in_specs, out_specs=out_specs, check_vma=False
    )
```

profile of v0, /device:TPU:1, one launch (start us, length us, event | category | flops | bytes accessed | tf_op | source)
XLA Modules:
  0.0 678.4 jit_solution(1686202782658851093)
XLA Ops:
  0.6 9.0 %copy.39 = bf16[1,6,24,16,128]{2,1,3,4,0:T(8,128)(2,1)} copy(bf16[1,6,24,16,128]{4,3,2,1,0:T(8,128)(2,1)} %param.9) | data formatting | bytes 1179648 | tf_op args[0]
  12.4 5.4 collective-permute-start
  25.8 9.0 %copy.42 = bf16[6,24,16,128]{1,0,2,3:T(8,128)(2,1)} copy(bf16[6,24,16,128]{3,2,1,0:T(8,128)(2,1)} %collective-permute-done) | data formatting | bytes 1179648 | tf_op jit(solution)/shard_map/ppermute | solution.py:30
  34.8 8.0 %maximum_bitcast_fusion = bf16[16,6,24,258]{2,1,0,3:T(8,128)(2,1)} fusion(bf16[6,24,16,2]{1,0,2,3:T(8,128)(2,1)S(1)} %copy.43, bf16[6,24,16,128]{1,0,2,3:T(8,128)(2,1)} %bitcast.80, bf16[6,24,16,128]{1,0,2,3:T(8,128)(2,1)} %copy.42), kind=kLoop, calls=%fused_computation.3 | loop fusion | flops 1188864 | bytes 2377728 | tf_op jit(solution)/shard_map/vmap()/transpose | solution.py:98
  42.8 7.4 %gather_fusion.1 = bf16[16,6,24,131]{2,1,3,0:T(8,128)(2,1)} fusion(bf16[16,6,24,258]{2,1,0,3:T(8,128)(2,1)} %maximum_bitcast_fusion, s32[16]{0:T(128)S(1)} %or_bitcast_fusion), kind=kCustom, calls=%fused_computation.1 | custom fusion | bytes 1207552 | tf_op jit(solution)/shard_map/vmap()/gather | solution.py:98
  50.1 9.3 %add_convert_fusion = bf16[6,24,16,128]{1,0,3,2:T(8,128)(2,1)S(1)} fusion(bf16[6,24,16,131]{1,0,3,2:T(8,128)(2,1)} %bitcast.77, f32[24,16,128]{0,2,1:T(8,128)S(1)} %copy.46, f32[24,16,128]{0,2,1:T(8,128)S(1)} %copy.45, f32[24,16,128]{0,2,1:T(8,128)S(1)} %copy.44, f32[24,16,128]{0,2,1:T(8,128)} %copy.38), kind=kLoop, calls=%fused_computation.4 | loop fusion | flops 3538944 | bytes 3735552 | tf_op jit(solution)/shard_map/convert_element_type | solution.py:101
  59.5 7.0 %slice_convert_fusion.5 = (f32[1,24,16,128]{1,0,3,2:T(1,128)S(1)}, f32[1,24,16,128]{1,0,3,2:T(1,128)S(1)}, f32[1,24,16,128]{1,0,3,2:T(1,128)S(1)}, f32[1,24,16,1...) fusion(bf16[6,24,16,128]{1,0,3,2:T(8,128)(2,1)S(1)} %add_convert_fusion), kind=kLoop, calls=%fused_computation.11 | loop fusion | flops 294912 | bytes 1769472 | tf_op jit(solution)/shard_map/convert_element_type | solution.py:106
  68.1 8.7 %collective-permute-start.2 = (bf16[24,2048]{0,1:T(8,128)(2,1)S(1)}, bf16[24,2048]{0,1:T(8,128)(2,1)S(1)}, u32[]{:S(2)}, u32[]{:S(2)}) collective-permute-start(bf16[24,2048]{0,1:T(8,128)(2,1)S(1)} %get-tuple-element.40), channel_id=1, source_target_pairs={{0,256},{256,0},{1,257},{257,1},{2,258},{258,2},{3,259},{259,3},{4... | collective-permute-start | bytes 294920 | tf_op jit(solution)/shard_map/ppermute | solution.py:40
  79.4 5.3 gather_fusion
  85.9 3.4 scatter_fusion
  92.9 4.0 collective-permute-start.4
  102.5 3.2 collective-permute-done.6
  105.8 3.9 collective-permute-done.5
  111.0 112.3 %all-reduce.3 = (f32[24]{0:T(128)S(1)}, f32[24]{0:T(128)S(1)}) all-reduce(f32[24]{0:T(128)S(1)} %get-tuple-element.25, f32[24]{0:T(128)S(1)} %get-tuple-element.24), channel_id=1, replica_groups=mesh['panel'=2,'lat'=8,'lon'=32] {'panel','lat','lon'}, use_global_device_ids=true, to_apply=%region_3.4 | all-reduce | flops 48 | bytes 384 | tf_op jit(solution)/shard_map/psum | solution.py:122
  226.3 4.0 collective-permute-start.8
  237.4 3.8 collective-permute-done.9
  243.9 103.7 %psum.58 = f32[1,24]{1,0:T(1,128)} all-reduce(f32[1,24]{1,0:T(1,128)} %bitcast.100), channel_id=1, replica_groups=mesh['panel'=2,'lat'=8,'lon'=32] {'panel','lat','lon'}, use_global_device_ids=true, to_apply=%region_7.8 | all-reduce | flops 24 | bytes 192 | tf_op jit(solution)/shard_map/psum | solution.py:135
  351.3 95.0 %all-reduce.2 = (f32[24]{0:T(128)}, f32[24]{0:T(128)}) all-reduce(f32[24]{0:T(128)} %get-tuple-element.23, f32[24]{0:T(128)} %get-tuple-element.22), channel_id=1, replica_groups=mesh['panel'=2,'lat'=8,'lon'=32] {'panel','lat','lon'}, use_global_device_ids=true, to_apply=%region_9.10 | all-reduce | flops 48 | bytes 384 | tf_op jit(solution)/shard_map/psum | solution.py:122
  449.4 4.0 collective-permute-start.12
  455.7 4.4 collective-permute-start.14
  461.4 10.5 %fusion.36 = bf16[1,6,24,16,128]{2,1,4,3,0:T(8,128)(2,1)} fusion(bf16[6,24,16,131]{1,0,3,2:T(8,128)(2,1)} %bitcast.78, f32[24,16,128]{0,2,1:T(8,128)S(1)} %copy.46, f32[24,16,128]{0,2,1:T(8,128)S(1)} %copy.45, f32[24,16,128]{0,2,1:T(8,128)S(1)} %copy.44, f32[24,16,128]{0,2,1:T(8,128)} %copy.38), kind=kLoop, calls=%fused_computation.110 | loop fusion | flops 3538944 | bytes 3735552 | tf_op jit(solution)/shard_map/broadcast_in_dim | solution.py:145
  471.9 4.6 copy.47
  479.0 99.8 %psum.61 = f32[2,24]{1,0:T(2,128)S(1)} all-reduce(f32[2,24]{1,0:T(2,128)S(1)} %pad_maximum_fusion.27), channel_id=1, replica_groups=mesh['panel'=2,'lat'=8,'lon'=32] {'panel','lat','lon'}, use_global_device_ids=true, to_apply=%region_14.15 | all-reduce | flops 48 | bytes 384 | tf_op jit(solution)/shard_map/psum | solution.py:135
  581.2 95.3 %all-reduce.1 = (f32[24]{0:T(128)S(1)}, f32[24]{0:T(128)S(1)}) all-reduce(f32[24]{0:T(128)S(1)} %get-tuple-element.19, f32[24]{0:T(128)S(1)} %get-tuple-element.18), channel_id=1, replica_groups=mesh['panel'=2,'lat'=8,'lon'=32] {'panel','lat','lon'}, use_global_device_ids=true, to_apply=%region_16.17 | all-reduce | flops 48 | bytes 384 | tf_op jit(solution)/shard_map/psum | solution.py:122
  (101 shorter events, 56.4 us)
Async XLA Ops:
  0.6 88.7 %copy-start = (f32[24,24]{1,0:T(8,128)S(1)}, f32[24,24]{1,0:T(8,128)}, u32[]{:S(2)}) copy-start(f32[24,24]{1,0:T(8,128)} %param.13) | copy-start | bytes 6916
  11.1 13.8 %collective-permute-start.1 = (bf16[6,24,16,2]{1,2,3,0:T(8,128)(2,1)}, bf16[6,24,16,2]{1,2,3,0:T(8,128)(2,1)}, u32[]{:S(2)}, u32[]{:S(2)}) collective-permute-start(bf16[6,24,16,2]{1,2,3,0:T(8,128)(2,1)} %copy.41), channel_id=1, source_target_pairs={{1,0},{2,1},{3,2},{4,3},{5,4},{6,5},{7,6},{8,7},{9,8},{10,9},{11,1... | collective-permute-start | bytes 27656 | tf_op jit(solution)/shard_map/ppermute | solution.py:30
  12.4 13.3 %collective-permute-start = (bf16[6,24,16,128]{3,2,1,0:T(8,128)(2,1)}, bf16[6,24,16,128]{3,2,1,0:T(8,128)(2,1)}, u32[]{:S(2)}, u32[]{:S(2)}) collective-permute-start(bf16[6,24,16,128]{3,2,1,0:T(8,128)(2,1)} %bitcast.94), channel_id=1, source_target_pairs={{0,1},{1,2},{2,3},{3,4},{4,5},{5,6},{6,7},{7,8},{8,9},{9,10},{10,1... | collective-permute-start | bytes 1769480 | tf_op jit(solution)/shard_map/ppermute | solution.py:30
  59.4 7.1 %copy-start.6 = (f32[24]{0:T(128)S(1)}, f32[24]{0:T(128)}, u32[]{:S(2)}) copy-start(f32[24]{0:T(128)} %get-tuple-element.66) | copy-start | bytes 292
  59.5 7.1 %copy-start.7 = (f32[24]{0:T(128)S(1)}, f32[24]{0:T(128)}, u32[]{:S(2)}) copy-start(f32[24]{0:T(128)} %get-tuple-element.67) | copy-start | bytes 292
  59.5 7.1 %copy-start.8 = (f32[24]{0:T(128)S(1)}, f32[24]{0:T(128)}, u32[]{:S(2)}) copy-start(f32[24]{0:T(128)} %get-tuple-element.68) | copy-start | bytes 292
  59.5 7.1 %copy-start.9 = (f32[24]{0:T(128)S(1)}, f32[24]{0:T(128)}, u32[]{:S(2)}) copy-start(f32[24]{0:T(128)} %get-tuple-element.69) | copy-start | bytes 292
  59.5 17.4 %copy-start.15 = (s32[1,1,256]{2,1,0:T(1,128)S(1)}, s32[1,1,256]{2,1,0:T(1,128)}, u32[]{:S(2)}) copy-start(s32[1,1,256]{2,1,0:T(1,128)} %param.15) | copy-start | bytes 3076
  59.5 19.9 %copy-start.4 = (s32[1024]{0:T(1024)S(1)}, s32[1024]{0:T(1024)}, u32[]{:S(2)}) copy-start(s32[1024]{0:T(1024)} %broadcast_clamp_fusion) | copy-start | bytes 12292
  59.5 25.1 %copy-start.5 = (f32[1,1,256,4]{2,3,1,0:T(4,128)S(1)}, f32[1,1,256,4]{2,3,1,0:T(4,128)}, u32[]{:S(2)}) copy-start(f32[1,1,256,4]{2,3,1,0:T(4,128)} %param.17) | copy-start | bytes 12292
  66.6 36.0 %copy-start.17 = (f32[24]{0:T(128)S(1)}, f32[24]{0:T(128)}, u32[]{:S(2)}) copy-start(f32[24]{0:T(128)} %param.14) | copy-start | bytes 292
  68.1 10.3 %collective-permute-start.2 = (bf16[24,2048]{0,1:T(8,128)(2,1)S(1)}, bf16[24,2048]{0,1:T(8,128)(2,1)S(1)}, u32[]{:S(2)}, u32[]{:S(2)}) collective-permute-start(bf16[24,2048]{0,1:T(8,128)(2,1)S(1)} %get-tuple-element.40), channel_id=1, source_target_pairs={{0,256},{256,0},{1,257},{257,1},{2,258},{258,2},{3,259},{259,3},{4... | collective-permute-start | bytes 294920 | tf_op jit(solution)/shard_map/ppermute | solution.py:40
  91.6 5.3 collective-permute-start.3
  92.9 4.8 collective-permute-start.4
  97.9 7.8 %collective-permute-start.6 = (f32[1,24,18,1]{3,2,1,0:T(8,128)S(1)}, f32[1,24,18,1]{3,2,1,0:T(8,128)S(1)}, u32[]{:S(2)}, u32[]{:S(2)}) collective-permute-start(f32[1,24,18,1]{3,2,1,0:T(8,128)S(1)} %get-tuple-element.53), channel_id=1, source_target_pairs={{0,1},{1,2},{2,3},{3,4},{4,5},{5,6},{6,7},{7,8},{8,9},{9,10},{10,1... | collective-permute-start | bytes 5192 | tf_op jit(solution)/shard_map/ppermute | solution.py:18
  101.0 8.6 %collective-permute-start.5 = (f32[1,24,18,1]{3,2,1,0:T(8,128)S(1)}, f32[1,24,18,1]{3,2,1,0:T(8,128)S(1)}, u32[]{:S(2)}, u32[]{:S(2)}) collective-permute-start(f32[1,24,18,1]{3,2,1,0:T(8,128)S(1)} %get-tuple-element.52), channel_id=1, source_target_pairs={{1,0},{2,1},{3,2},{4,3},{5,4},{6,5},{7,6},{8,7},{9,8},{10,9},{11,1... | collective-permute-start | bytes 5192 | tf_op jit(solution)/shard_map/ppermute | solution.py:20
  225.0 5.3 collective-permute-start.7
  226.3 4.8 collective-permute-start.8
  231.3 6.2 collective-permute-start.10
  233.0 8.3 %collective-permute-start.9 = (f32[1,24,18,1]{3,2,1,0:T(8,128)S(1)}, f32[1,24,18,1]{3,2,1,0:T(8,128)S(1)}, u32[]{:S(2)}, u32[]{:S(2)}) collective-permute-start(f32[1,24,18,1]{3,2,1,0:T(8,128)S(1)} %get-tuple-element.50), channel_id=1, source_target_pairs={{1,0},{2,1},{3,2},{4,3},{5,4},{6,5},{7,6},{8,7},{9,8},{10,9},{11,1... | collective-permute-start | bytes 5192 | tf_op jit(solution)/shard_map/ppermute | solution.py:20
  448.1 5.3 collective-permute-start.11
  449.4 4.8 collective-permute-start.12
  455.7 20.7 %collective-permute-start.14 = (f32[1,24,18,1]{3,2,1,0:T(8,128)}, f32[1,24,18,1]{3,2,1,0:T(8,128)}, u32[]{:S(2)}, u32[]{:S(2)}) collective-permute-start(f32[1,24,18,1]{3,2,1,0:T(8,128)} %get-tuple-element.49), channel_id=1, source_target_pairs={{0,1},{1,2},{2,3},{3,4},{4,5},{5,6},{6,7},{7,8},{8,9},{9,10},{10,1... | collective-permute-start | bytes 5192 | tf_op jit(solution)/shard_map/ppermute | solution.py:18
  460.1 16.3 %collective-permute-start.13 = (f32[1,24,18,1]{3,2,1,0:T(8,128)}, f32[1,24,18,1]{3,2,1,0:T(8,128)}, u32[]{:S(2)}, u32[]{:S(2)}) collective-permute-start(f32[1,24,18,1]{3,2,1,0:T(8,128)} %get-tuple-element.48), channel_id=1, source_target_pairs={{1,0},{2,1},{3,2},{4,3},{5,4},{6,5},{7,6},{8,7},{9,8},{10,9},{11,1... | collective-permute-start | bytes 5192 | tf_op jit(solution)/shard_map/ppermute | solution.py:20
  (9 other events, 24.5 us)
where the time goes:
time: 680 us; the launch traced here: 678 us
  blocking collectives  506 us (74%)
  other arithmetic  58.7 us (9%)
  local copies, waits for them, and re-layouts  47.7 us (7%)
  starting transfers between devices  44.5 us (7%)
  waiting for transfers between devices  18 us (3%)
    psum x3, blocking collectives, per_device(): lax.psum((local_inner(residual, images[iteration]), local_inner(images[it...  303 us
    psum x2, blocking collectives, per_device(): lax.psum(jnp.stack([local_inner(fresh, image) for image in images]), ('pa...  203 us
    ppermute x6, starting transfers between devices, padded_2(): lax.ppermute(tail, axis, [(i, (i + 1) % count) for i in range(ends)])  21.1 us
    unnamed x40, local copies, waits for them, and re-layouts  15.4 us
  transfers between devices with their start and end apart: 15, of which 8 were waited for; matrix products, arithmetic and copies ran while one was open for 3% of the time, Pallas kernels for 0%

commit v1 on v0

v1 whole, which is shorter than its diff:
```python
import jax
import jax.numpy as jnp
from jax import lax
from jax.experimental import pallas as pl
from jax.experimental.pallas import tpu as pltpu
from jax.sharding import PartitionSpec as P

F32 = jnp.float32
BF16 = jnp.bfloat16
NF = 6
LEV = 24
ROWS = 16
COLS = 128
G = 3
OV = 256
VMEM_LIMIT = 48 * 1024 * 1024


def lane_iota(shape):
    return lax.broadcasted_iota(jnp.int32, shape, len(shape) - 1)


def roll_lanes(x, by):
    by = by % COLS
    if by == 0:
        return x
    return pltpu.roll(x, by, x.ndim - 1)


def params():
    return pltpu.CompilerParams(vmem_limit_bytes=VMEM_LIMIT)


def pack_east_kernel(fields_ref, out_ref):
    lane = lane_iota((ROWS, COLS))
    acc = jnp.zeros((ROWS, COLS), F32)
    for f in range(NF):
        for l8 in range(8):
            i = f * 8 + l8
            x = roll_lanes(fields_ref[f, l8].astype(F32), 2 * i)
            acc = jnp.where((lane >> 1) == i, x, acc)
    out_ref[0] = acc.astype(BF16)


def pack_east(fields):
    return pl.pallas_call(
        pack_east_kernel,
        grid=(G,),
        in_specs=[pl.BlockSpec((NF, 8, ROWS, COLS), lambda g: (0, g, 0, 0))],
        out_specs=pl.BlockSpec((1, ROWS, COLS), lambda g: (g, 0, 0)),
        out_shape=jax.ShapeDtypeStruct((G, ROWS, COLS), BF16),
        compiler_params=params(),
        name="pack_east",
    )(fields)


def advect_kernel(mix_ref, shift_ref, frac_ref, fields_ref, west_ref, east_ref, adv_ref, rhs_ref, half_ref):
    g = pl.program_id(0)
    lon = lax.axis_index("lon")
    table = shift_ref[...]
    own = jnp.sum(jnp.where(lane_iota(table.shape) == lon, table, 0), axis=1, keepdims=True)
    shift = jnp.broadcast_to(own, (ROWS, COLS))
    lane = lane_iota((ROWS, COLS))
    odd = (shift & 1) == 1
    two = (shift & 2) == 2

    def turn(x, sign):
        x = jnp.where(odd, roll_lanes(x, 32 * sign), x)
        return jnp.where(two, roll_lanes(x, 64), x)

    def beyond(j):
        at = ((lane - j + 32 * shift) & (COLS - 1)) - 32 * shift + j
        return (at < 0) | (at >= COLS)

    taps = (-1, 0, 1, 2)
    masks = [beyond(j) for j in taps]
    edge = lane < 2
    east = east_ref[0].astype(F32)
    for l8 in range(8):
        t = turn(frac_ref[l8], -1)
        tm1, tm2, tp1 = t - 1.0, t - 2.0, t + 1.0
        weights = (
            -t * tm1 * tm2 * (1.0 / 6.0),
            tp1 * tm1 * tm2 * 0.5,
            -tp1 * t * tm2 * 0.5,
            tp1 * t * tm1 * (1.0 / 6.0),
        )
        total = jnp.zeros((ROWS, COLS), F32)
        for f in range(NF):
            own_row = fields_ref[f, l8].astype(F32)
            other = jnp.where(edge, roll_lanes(east, -2 * (f * 8 + l8)), west_ref[f, l8].astype(F32))
            acc = None
            for j, mask, weight in zip(taps, masks, weights):
                term = weight * roll_lanes(jnp.where(mask, other, own_row), -j)
                acc = term if acc is None else acc + term
            rounded = acc.astype(BF16)
            acc = rounded.astype(F32)
            adv_ref[f, l8] = turn(acc, 1).astype(BF16)
            total = total + mix_ref[f, g * 8 + l8] * acc
        rhs_ref[0, pl.ds(l8, ROWS, stride=8), :] = turn(total, 1)
    half_ref[0] = rhs_ref[0].astype(BF16)


def advect(mix, shift, frac, fields, west, east):
    block = pl.BlockSpec((NF, 8, ROWS, COLS), lambda g: (0, g, 0, 0))
    group = pl.BlockSpec((1, 128, COLS), lambda g: (g, 0, 0))
    return pl.pallas_call(
        advect_kernel,
        grid=(G,),
        in_specs=[
            pl.BlockSpec(memory_space=pltpu.SMEM),
            pl.BlockSpec((ROWS, 32), lambda g: (0, 0)),
            pl.BlockSpec((8, ROWS, COLS), lambda g: (g, 0, 0)),
            block,
            block,
            pl.BlockSpec((1, ROWS, COLS), lambda g: (g, 0, 0)),
        ],
        out_specs=[block, group, group],
        out_shape=[
            jax.ShapeDtypeStruct((NF, LEV, ROWS, COLS), BF16),
            jax.ShapeDtypeStruct((G, 128, COLS), F32),
            jax.ShapeDtypeStruct((G, 128, COLS), BF16),
        ],
        compiler_params=params(),
        name="advect",
    )(mix, shift, frac, fields, west, east)


def split3(x):
    a = x.astype(BF16)
    rest = x - a.astype(F32)
    b = rest.astype(BF16)
    c = (rest - b.astype(F32)).astype(BF16)
    return a, b, c


def margin_kernel(rhs_ref, both_ref, cells_ref, source_ref, weight_ref, proj_ref, b_ref, top_ref, bottom_ref):
    other = 1 - lax.axis_index("panel")
    src = jnp.concatenate([source_ref[q : q + 1, :] for q in range(4)], axis=1)
    wgt = jnp.concatenate([weight_ref[q : q + 1, :] for q in range(4)], axis=1)
    src_col = jnp.broadcast_to(src & 127, (128, 4 * OV))
    pick = jnp.where(lax.broadcasted_iota(jnp.int32, (128, 4 * OV), 0) == src_col, 1.0, 0.0).astype(BF16)
    src_row = jnp.broadcast_to(src >> 7, (8, 4 * OV))
    wgt = jnp.broadcast_to(wgt, (8, 4 * OV))
    cells = cells_ref[...]
    cell_col = jnp.broadcast_to(cells & 127, (128, OV))
    place = jnp.where(lax.broadcasted_iota(jnp.int32, (128, OV), 0) == cell_col, 1.0, 0.0).astype(BF16)
    cell_row = jnp.broadcast_to(cells >> 7, (128, OV))
    in_row = (lax.broadcasted_iota(jnp.int32, (128, OV), 0) >> 3) == cell_row
    nt = (((1,), (1,)), ((), ()))
    covered = lax.dot_general(jnp.where(in_row, 1.0, 0.0).astype(BF16), place, nt, preferred_element_type=F32) > 0.5
    joined = []
    for lb in range(G):
        cols = jnp.dot(both_ref[other, lb], pick, preferred_element_type=F32)
        rep = jnp.zeros((8, 4 * OV), F32)
        for r in range(ROWS):
            rep = rep + jnp.where(src_row == r, wgt, 0.0) * cols[8 * r : 8 * r + 8, :]
        rep = rep[:, :OV] + rep[:, OV : 2 * OV] + rep[:, 2 * OV : 3 * OV] + rep[:, 3 * OV :]
        spread = jnp.where(in_row, jnp.concatenate([rep] * ROWS, axis=0), 0.0)
        values = None
        for part in split3(spread):
            value = lax.dot_general(part, place, nt, preferred_element_type=F32)
            values = value if values is None else values + value
        joined.append(jnp.where(covered, values, rhs_ref[lb]))
    levels = jnp.concatenate(
        [jnp.concatenate([joined[lb][8 * r : 8 * r + 8] for lb in range(G)], axis=0) for r in range(ROWS)], axis=1
    )
    modal = jnp.dot(proj_ref[...], levels, precision=lax.Precision.HIGHEST, preferred_element_type=F32)
    for lb in range(G):
        for r in range(ROWS):
            tile = modal[8 * lb : 8 * lb + 8, COLS * r : COLS * r + COLS]
            b_ref[lb, 8 * r : 8 * r + 8, :] = tile
            if r < 3:
                top_ref[lb, 8 * r : 8 * r + 8, :] = tile
            if r >= ROWS - 3:
                s = r - (ROWS - 3)
                bottom_ref[lb, 8 * s : 8 * s + 8, :] = tile


def margin(rhs, both, cells, source, weight, proj):
    return pl.pallas_call(
        margin_kernel,
        out_shape=[
            jax.ShapeDtypeStruct((G, 128, COLS), F32),
            jax.ShapeDtypeStruct((G, 24, COLS), F32),
            jax.ShapeDtypeStruct((G, 24, COLS), F32),
        ],
        compiler_params=params(),
        name="margin",
    )(rhs, both, cells, source, weight, proj)


def pack_columns_kernel(b_ref, north_ref, south_ref, out_ref):
    lane = lane_iota((8, COLS))
    for lb in range(G):
        acc = jnp.zeros((8, COLS), F32)
        for i in range(20):
            j = i - 2
            if j < 0:
                row = north_ref[lb, 8 * (j + 3) : 8 * (j + 3) + 8, :]
            elif j >= ROWS:
                row = south_ref[lb, 8 * (j - ROWS) : 8 * (j - ROWS) + 8, :]
            else:
                row = b_ref[lb, 8 * j : 8 * j + 8, :]
            here = ((lane - 6 * i + 3) & 127) < 6
            acc = jnp.where(here, roll_lanes(row, 6 * i), acc)
        out_ref[lb] = acc


def pack_columns(b, north, south):
    return pl.pallas_call(
        pack_columns_kernel,
        out_shape=jax.ShapeDtypeStruct((G, 8, COLS), F32),
        compiler_params=params(),
        name="pack_columns",
    )(b, north, south)


def images_kernel(shift_ref, b_ref, north_ref, south_ref, fwest_ref, feast_ref, c_ref, u1_ref, u2_ref, s_ref):
    lat, lon = lax.axis_index("lat"), lax.axis_index("lon")
    one = jnp.float32(1.0)
    zero = jnp.float32(0.0)
    has_n = jnp.where(lat > 0, one, zero)
    has_s = jnp.where(lat < lax.axis_size("lat") - 1, one, zero)
    has_w = jnp.where(lon > 0, one, zero)
    has_e = jnp.where(lon < lax.axis_size("lon") - 1, one, zero)
    lane = lane_iota((8, COLS))
    first, last = lane == 0, lane == COLS - 1
    side = jnp.where(lane < 64, has_e, has_w)
    from_east = ((lane % 6) < 3) & (lane < 120)

    def line(main, ext):
        return roll_lanes(jnp.where(last, ext, main), 1) + roll_lanes(jnp.where(first, ext, main), -1)

    def row_scale(j):
        return has_n if j < 0 else has_s if j >= ROWS else None

    sums_out = jnp.zeros((8, COLS), F32)
    for lb in range(G):
        diag = lane_iota((8, LEV)) == (lax.broadcasted_iota(jnp.int32, (8, LEV), 0) + 8 * lb)
        a = 4.0 + jnp.sum(jnp.where(diag, jnp.broadcast_to(shift_ref[...], (8, LEV)), 0.0), axis=1, keepdims=True)
        a = jnp.broadcast_to(a, (8, COLS))
        packed = jnp.where(from_east, feast_ref[lb], fwest_ref[lb])

        def b_main(j):
            if j < 0:
                return north_ref[lb, 8 * (j + 3) : 8 * (j + 3) + 8, :]
            if j >= ROWS:
                return south_ref[lb, 8 * (j - ROWS) : 8 * (j - ROWS) + 8, :]
            return b_ref[lb, 8 * j : 8 * j + 8, :]

        bm = {j: b_main(j) for j in (-3, -2)}
        bx = {-2: packed}
        cm, cx, um, ux = {}, {}, {}, {}
        sums = [jnp.zeros((8, COLS), F32) for _ in range(8)]
        for j in range(-2, ROWS + 4):
            if j <= ROWS + 1:
                bm[j + 1] = b_main(j + 1)
                if j + 1 <= ROWS + 1:
                    bx[j + 1] = roll_lanes(packed, -6 * (j + 3))
                value = a * bm[j] - (bm[j - 1] + bm[j + 1] + line(bm[j], bx[j]))
                scale = row_scale(j)
                cm[j] = value if scale is None else value * scale
                if -1 <= j <= ROWS:
                    value = (a * bx[j] - (bx[j - 1] + bx[j + 1] + line(bx[j], bm[j]))) * side
                    cx[j] = value if scale is None else value * scale
                if 0 <= j < ROWS:
                    c_ref[lb, 8 * j : 8 * j + 8, :] = cm[j]
            i = j - 1
            if -1 <= i <= ROWS:
                value = 0.25 * (cm[i - 1] + cm[i + 1] + line(cm[i], cx[i]))
                scale = row_scale(i)
                um[i] = value if scale is None else value * scale
                if 0 <= i < ROWS:
                    ux[i] = 0.25 * (cx[i - 1] + cx[i + 1] + line(cx[i], cm[i])) * side
                    u1_ref[lb, 8 * i : 8 * i + 8, :] = um[i]
            i = j - 2
            if 0 <= i < ROWS:
                u2 = 0.5 * (um[i - 1] + um[i + 1] + line(um[i], ux[i])) - cm[i]
                u2_ref[lb, 8 * i : 8 * i + 8, :] = u2
                b, c, u1 = b_main(i), cm[i], um[i]
                pairs = ((b, c), (b, u1), (b, u2), (c, c), (c, u1), (u1, u1), (u1, u2), (u2, u2))
                sums = [s + x * y for s, (x, y) in zip(sums, pairs)]
        for q in range(8):
            total = jnp.sum(sums[q], axis=1, keepdims=True)
            sums_out = jnp.where(lane == 8 * lb + q, total, sums_out)
    s_ref[...] = sums_out


def images(mode_shift, b, north, south, from_west, from_east):
    full = jax.ShapeDtypeStruct((G, 128, COLS), F32)
    return pl.pallas_call(
        images_kernel,
        out_shape=[full, full, full, jax.ShapeDtypeStruct((8, COLS), F32)],
        compiler_params=params(),
        name="images",
    )(mode_shift, b, north, south, from_west, from_east)


def iterate_kernel(shift_ref, s_ref, b_ref, c_ref, u1_ref, u2_ref, sol_ref, res_ref):
    lane = lane_iota((8, COLS))
    sums = s_ref[...]
    for lb in range(G):
        diag = lane_iota((8, LEV)) == (lax.broadcasted_iota(jnp.int32, (8, LEV), 0) + 8 * lb)
        a = 4.0 + jnp.sum(jnp.where(diag, jnp.broadcast_to(shift_ref[...], (8, LEV)), 0.0), axis=1, keepdims=True)
        a = jnp.broadcast_to(a, (8, COLS))

        def inner(q):
            value = jnp.sum(jnp.where(lane == 8 * lb + q, sums, 0.0), axis=1, keepdims=True)
            return jnp.broadcast_to(value, (8, COLS))

        bc, bu1, bu2, cc, cu1, u1u1, u1u2, u2u2 = [inner(q) for q in range(8)]
        cu2 = 2.0 * u1u1 - cc
        l10 = cu1 / cc
        l20 = cu2 / cc
        d1 = u1u1 - l10 * cu1
        e1 = u1u2 - l10 * cu2
        l21 = e1 / d1
        d2 = u2u2 - l20 * cu2 - l21 * e1
        z0 = bc
        z1 = bu1 - l10 * z0
        z2 = bu2 - l20 * z0 - l21 * z1
        y2 = z2 / d2
        y1 = z1 / d1 - l21 * y2
        y0 = z0 / cc - l10 * y1 - l20 * y2
        for r in range(ROWS):
            rows = slice(8 * r, 8 * r + 8)
            b, c, u1, u2 = b_ref[lb, rows, :], c_ref[lb, rows, :], u1_ref[lb, rows, :], u2_ref[lb, rows, :]
            v1 = 0.25 * (a * b - c)
            v2 = 0.5 * (a * v1 - u1) - b
            at = pl.ds(lb * 128 + r, 8, stride=ROWS)
            sol_ref[at, :] = y0 * b + y1 * v1 + y2 * v2
            res_ref[at, :] = b - y0 * c - y1 * u1 - y2 * u2


def iterate(mode_shift, sums, b, c, u1, u2):
    out = jax.ShapeDtypeStruct((LEV * ROWS, COLS), F32)
    return pl.pallas_call(
        iterate_kernel,
        out_shape=[out, out],
        compiler_params=params(),
        name="iterate",
    )(mode_shift, sums, b, c, u1, u2)


def send(block, axis, by):
    count = lax.axis_size(axis)
    return lax.ppermute(block, axis, [(i, i + by) for i in range(count) if 0 <= i + by < count])


def groups_of_lon(count):
    along_x = [[4 * z + x for x in range(4)] for z in range(count // 4)]
    along_z = [[4 * z + x for z in range(count // 4)] for x in range(4)]
    return along_x, along_z


def reduced(sums):
    along_x, along_z = groups_of_lon(lax.axis_size("lon"))
    sums = lax.psum(sums, "panel")
    sums = lax.psum(sums, "lon", axis_index_groups=along_x)
    sums = lax.psum(sums, "lat")
    return lax.psum(sums, "lon", axis_index_groups=along_z)


def per_device(fields, frac, shift, mix, proj, mode_shift, cells, source, weight):
    fields = fields[0]
    west = send(fields, "lon", 1)
    east = send(pack_east(fields), "lon", -1)
    adv, rhs, half = advect(mix, shift[0], frac[0], fields, west, east)
    both = lax.all_gather(half, "panel")
    b, top, bottom = margin(rhs, both, cells[0], source[0, 0].T, weight[0, 0].T, proj)
    north = send(bottom, "lat", 1)
    south = send(top, "lat", -1)
    columns = pack_columns(b, north, south)
    from_west = send(columns, "lon", 1)
    from_east = send(columns, "lon", -1)
    shifts = mode_shift.reshape(1, LEV)
    c, u1, u2, sums = images(shifts, b, north, south, from_west, from_east)
    sol, res = iterate(shifts, reduced(sums), b, c, u1, u2)
    shape = (1, LEV, ROWS, COLS)
    return adv[None], sol.reshape(shape), res.reshape(shape)


def solution(mesh):
    wide = P("panel", None, None, "lat", "lon")
    flat = P("panel", None, "lat", "lon")
    table = P("panel", "lat", "lon", None)
    in_specs = (wide, flat, P("panel", "lat", None), P(), P(), P(), P("panel", "lat", "lon"), table, table)
    return jax.shard_map(per_device, mesh=mesh, in_specs=in_specs, out_specs=(wide, flat, flat), check_vma=False)
```

time: 680 us -> 111 us (0.16)
  the two profiles are of different devices: /device:TPU:1 before, /device:TPU:2 now
where the time goes in v1:
time: 111 us
  blocking collectives  58.8 us (53%)
  starting transfers between devices  19.8 us (18%)
  Pallas kernels  16.8 us (15%)
  waiting for transfers between devices  12.7 us (11%)
  local copies, waits for them, and re-layouts  1.79 us (2%)
    psum x1, blocking collectives, reduced(): return lax.psum(sums, 'lon', axis_index_groups=along_z)  26.4 us
    ppermute x6, starting transfers between devices, send(): lax.ppermute(block, axis, [(i, i + by) for i in range(count) if 0 <= i +...  19.8 us
    psum x1, blocking collectives, reduced(): sums = lax.psum(sums, 'lat')  18.1 us
    ppermute x6, waiting for transfers between devices, send(): lax.ppermute(block, axis, [(i, i + by) for i in range(count) if 0 <= i +...  12.7 us
    pallas_call x1, Pallas kernels, advect(): pl.pallas_call(advect_kernel, grid=(G,), in_specs=[pl.BlockSpec(memory_sp...  11.7 us
    psum x1, blocking collectives, reduced(): sums = lax.psum(sums, 'lon', axis_index_groups=along_x)  9.87 us
    psum x1, blocking collectives, reduced(): sums = lax.psum(sums, 'panel')  2.46 us
    pallas_call x1, Pallas kernels, images(): pl.pallas_call(images_kernel, out_shape=[full, full, full, jax.ShapeDtype...  2.22 us
  transfers between devices with their start and end apart: 6, of which 5 were waited for; matrix products, arithmetic and copies ran while one was open for 0% of the time, Pallas kernels for 0%

profile of v1, /device:TPU:2, one launch (start us, length us, event | category | flops | bytes accessed | tf_op | source)
XLA Modules:
  0.0 110.6 jit_solution(1760479455625292238)
XLA Ops:
  0.6 3.4 %collective-permute-start = (bf16[6,24,16,128]{3,2,1,0:T(8,128)(2,1)}, bf16[6,24,16,128]{3,2,1,0:T(8,128)(2,1)S(1)}, u32[]{:S(2)}, u32[]{:S(2)}) collective-permute-start(bf16[6,24,16,128]{3,2,1,0:T(8,128)(2,1)} %bitcast.15), channel_id=1, source_target_pairs={{0,1},{1,2},{2,3},{3,4},{4,5},{5,6},{6,7},{7,8},{8,9},{9,10},{10,1... | collective-permute-start | bytes 1769480 | tf_op jit(solution)/shard_map/ppermute | solution.py:348
  4.0 1.1 copy-done
  5.1 0.5 pack_east.1
  5.6 5.8 %collective-permute-start.1 = (bf16[3,16,128]{2,1,0:T(8,128)(2,1)S(1)}, bf16[3,16,128]{2,1,0:T(8,128)(2,1)S(1)}, u32[]{:S(2)}, u32[]{:S(2)}) collective-permute-start(bf16[3,16,128]{2,1,0:T(8,128)(2,1)S(1)} %pack_east.1), channel_id=1, source_target_pairs={{1,0},{2,1},{3,2},{4,3},{5,4},{6,5},{7,6},{8,7},{9,8},{10,9},{11,1... | collective-permute-start | bytes 36872 | tf_op jit(solution)/shard_map/ppermute | solution.py:348
  11.3 1.4 %collective-permute-done.1.east_ref = bf16[3,16,128]{2,1,0:T(8,128)(2,1)S(1)} collective-permute-done((bf16[3,16,128]{2,1,0:T(8,128)(2,1)S(1)}, bf16[3,16,128]{2,1,0:T(8,128)(2,1)S(1)}, u32[]{:S(2)}, u32[]{:S(2)}) %collective-permute-start.1) | collective-permute-done | bytes 12320 | tf_op jit(solution)/shard_map/ppermute | solution.py:348
  12.7 5.1 %collective-permute-done.west_ref = bf16[6,24,16,128]{3,2,1,0:T(8,128)(2,1)S(1)} collective-permute-done((bf16[6,24,16,128]{3,2,1,0:T(8,128)(2,1)}, bf16[6,24,16,128]{3,2,1,0:T(8,128)(2,1)S(1)}, u32[]{:S(2)}, u32[]{:S(2)}) %collective-permute-start) | collective-permute-done | bytes 589856 | tf_op jit(solution)/shard_map/ppermute | solution.py:348
  17.8 11.7 %advect.1 = (bf16[6,24,16,128]{3,2,1,0:T(8,128)(2,1)}, f32[3,128,128]{2,1,0:T(8,128)S(1)}, bf16[3,128,128]{2,1,0:T(8,128)(2,1)S(1)}) custom-call(f32[6,24]{1,0:T(8,128)S(1)} %copy-done.4, s32[16,32]{1,0:T(8,128)S(1)} %bitcast.20, f32[24,16,128]{2,1,0:T(8,128)S(1)} %bitcast.19, bf16[6,24,16,128]{3,2,1,0:T(8,128)(2,1)S(1)} %bitcast.17, ...), custom_call_target="tpu_custom_call" | custom-call | tf_op jit(solution)/shard_map/advect/pallas_call | solution.py:107
  29.5 2.1 %all-gather = bf16[6,128,128]{2,1,0:T(8,128)(2,1)S(1)} all-gather(bf16[3,128,128]{2,1,0:T(8,128)(2,1)S(1)} %get-tuple-element.17), channel_id=2, replica_groups=mesh['panel'=2,'lat'=8,'lon'=32] {'panel'}, dimensions={0}, use_global_device_ids=true | all-gather | bytes 294912 | tf_op jit(solution)/shard_map/all_gather | solution.py:370
  31.6 0.7 copy-done.6
  32.3 1.3 %margin.1 = (f32[3,128,128]{2,1,0:T(8,128)S(1)}, f32[3,24,128]{2,1,0:T(8,128)S(1)}, f32[3,24,128]{2,1,0:T(8,128)S(1)}) custom-call(f32[3,128,128]{2,1,0:T(8,128)S(1)} %get-tuple-element.16.rhs_ref, bf16[2,3,128,128]{3,2,1,0:T(8,128)(2,1)S(1)} %bitcast.18, s32[1,256]{1,0:T(1,128)S(1)} %bitcast.25, s32[4,256]{1,0:T(4,128)S(1)} %bitcast.21, ...), custom_call_target="tpu_custom_call" | custom-call | tf_op jit(solution)/shard_map/margin/pallas_call | solution.py:181
  33.6 3.5 %collective-permute-start.2 = (f32[3,24,128]{2,1,0:T(8,128)S(1)}, f32[3,24,128]{2,1,0:T(8,128)S(1)}, u32[]{:S(2)}, u32[]{:S(2)}) collective-permute-start(f32[3,24,128]{2,1,0:T(8,128)S(1)} %get-tuple-element.19), channel_id=1, source_target_pairs={{0,32},{32,64},{64,96},{96,128},{128,160},{160,192},{192,224},{1,3... | collective-permute-start | bytes 110600 | tf_op jit(solution)/shard_map/ppermute | solution.py:348
  37.1 1.3 %collective-permute-start.3 = (f32[3,24,128]{2,1,0:T(8,128)S(1)}, f32[3,24,128]{2,1,0:T(8,128)S(1)}, u32[]{:S(2)}, u32[]{:S(2)}) collective-permute-start(f32[3,24,128]{2,1,0:T(8,128)S(1)} %get-tuple-element.20), channel_id=1, source_target_pairs={{32,0},{64,32},{96,64},{128,96},{160,128},{192,160},{224,192},{33,... | collective-permute-start | bytes 110600 | tf_op jit(solution)/shard_map/ppermute | solution.py:348
  38.4 0.3 collective-permute-done.2.north_ref
  38.7 4.2 %collective-permute-done.3.south_ref = f32[3,24,128]{2,1,0:T(8,128)S(1)} collective-permute-done((f32[3,24,128]{2,1,0:T(8,128)S(1)}, f32[3,24,128]{2,1,0:T(8,128)S(1)}, u32[]{:S(2)}, u32[]{:S(2)}) %collective-permute-start.3) | collective-permute-done | bytes 36896 | tf_op jit(solution)/shard_map/ppermute | solution.py:348
  42.9 0.1 pack_columns.1
  43.1 1.9 %collective-permute-start.5 = (f32[3,8,128]{2,1,0:T(8,128)S(1)}, f32[3,8,128]{2,1,0:T(8,128)S(1)}, u32[]{:S(2)}, u32[]{:S(2)}) collective-permute-start(f32[3,8,128]{2,1,0:T(8,128)S(1)} %pack_columns.1), channel_id=1, source_target_pairs={{1,0},{2,1},{3,2},{4,3},{5,4},{6,5},{7,6},{8,7},{9,8},{10,9},{11,1... | collective-permute-start | bytes 36872 | tf_op jit(solution)/shard_map/ppermute | solution.py:348
  45.0 3.9 %collective-permute-start.4 = (f32[3,8,128]{2,1,0:T(8,128)S(1)}, f32[3,8,128]{2,1,0:T(8,128)S(1)}, u32[]{:S(2)}, u32[]{:S(2)}) collective-permute-start(f32[3,8,128]{2,1,0:T(8,128)S(1)} %pack_columns.1), channel_id=1, source_target_pairs={{0,1},{1,2},{2,3},{3,4},{4,5},{5,6},{6,7},{7,8},{8,9},{9,10},{10,1... | collective-permute-start | bytes 36872 | tf_op jit(solution)/shard_map/ppermute | solution.py:348
  48.9 1.6 %collective-permute-done.4.fwest_ref = f32[3,8,128]{2,1,0:T(8,128)S(1)} collective-permute-done((f32[3,8,128]{2,1,0:T(8,128)S(1)}, f32[3,8,128]{2,1,0:T(8,128)S(1)}, u32[]{:S(2)}, u32[]{:S(2)}) %collective-permute-start.4) | collective-permute-done | bytes 12320 | tf_op jit(solution)/shard_map/ppermute | solution.py:348
  50.6 2.2 %images.1 = (f32[3,128,128]{2,1,0:T(8,128)S(1)}, f32[3,128,128]{2,1,0:T(8,128)S(1)}, f32[3,128,128]{2,1,0:T(8,128)S(1)}, f32[8,128]{1,0:T(8,128)S(1)}) custom-call(f32[1,24]{1,0:T(1,128)S(1)} %bitcast.23, f32[3,128,128]{2,1,0:T(8,128)S(1)} %get-tuple-element.18.b_ref, f32[3,24,128]{2,1,0:T(8,128)S(1)} %collective-permute-done.2.north_ref, ...), custom_call_target="tpu_custom_call" | custom-call | tf_op jit(solution)/shard_map/images/pallas_call | solution.py:292
  52.8 2.5 %psum.28 = f32[8,128]{1,0:T(8,128)S(1)} all-reduce(f32[8,128]{1,0:T(8,128)S(1)} %get-tuple-element.21), channel_id=1, replica_groups=mesh['panel'=2,'lat'=8,'lon'=32] {'panel'}, use_global_device_ids=true, to_apply=%region_0.0 | all-reduce | flops 1024 | bytes 8192 | tf_op jit(solution)/shard_map/psum | solution.py:359
  55.3 9.9 %psum.29 = f32[8,128]{1,0:T(8,128)S(1)} all-reduce(f32[8,128]{1,0:T(8,128)S(1)} %psum.28), channel_id=1, replica_groups={{0,1,2,3},{4,5,6,7},{8,9,10,11},{12,13,14,15},{16,17,18,19},{20,21,22,2..., use_global_device_ids=true, to_apply=%region_1.0 | all-reduce | flops 1024 | bytes 8192 | tf_op jit(solution)/shard_map/psum | solution.py:360
  65.2 18.1 %psum.30 = f32[8,128]{1,0:T(8,128)S(1)} all-reduce(f32[8,128]{1,0:T(8,128)S(1)} %psum.29), channel_id=1, replica_groups=mesh['panel'=2,'lat'=8,'lon'=32] {'lat'}, use_global_device_ids=true, to_apply=%region_2.0 | all-reduce | flops 1024 | bytes 8192 | tf_op jit(solution)/shard_map/psum | solution.py:361
  83.2 26.4 %psum.31.s_ref = f32[8,128]{1,0:T(8,128)S(1)} all-reduce(f32[8,128]{1,0:T(8,128)S(1)} %psum.30), channel_id=1, replica_groups={{0,4,8,12,16,20,24,28},{1,5,9,13,17,21,25,29},{2,6,10,14,18,22,26,30},{..., use_global_device_ids=true, to_apply=%region_3.0 | all-reduce | flops 1024 | bytes 8192 | tf_op jit(solution)/shard_map/psum | solution.py:362
  109.6 1.0 iterate.1
  (17 shorter events, 0.1 us)
Async XLA Ops:
  0.6 17.2 %collective-permute-start = (bf16[6,24,16,128]{3,2,1,0:T(8,128)(2,1)}, bf16[6,24,16,128]{3,2,1,0:T(8,128)(2,1)S(1)}, u32[]{:S(2)}, u32[]{:S(2)}) collective-permute-start(bf16[6,24,16,128]{3,2,1,0:T(8,128)(2,1)} %bitcast.15), channel_id=1, source_target_pairs={{0,1},{1,2},{2,3},{3,4},{4,5},{5,6},{6,7},{7,8},{8,9},{9,10},{10,1... | collective-permute-start | bytes 1769480 | tf_op jit(solution)/shard_map/ppermute | solution.py:348
  4.0 1.1 copy-start
  5.1 12.7 %copy-start.1 = (f32[1,24,16,128]{3,2,1,0:T(8,128)S(1)}, f32[1,24,16,128]{3,2,1,0:T(8,128)}, u32[]{:S(2)}) copy-start(f32[1,24,16,128]{3,2,1,0:T(8,128)} %param.10) | copy-start | bytes 589828
  5.1 12.7 %copy-start.3 = (s32[1,16,32]{2,1,0:T(8,128)S(1)}, s32[1,16,32]{2,1,0:T(8,128)}, u32[]{:S(2)}) copy-start(s32[1,16,32]{2,1,0:T(8,128)} %param.11) | copy-start | bytes 6148
  5.1 12.7 %copy-start.4 = (f32[6,24]{1,0:T(8,128)S(1)}, f32[6,24]{1,0:T(8,128)}, u32[]{:S(2)}) copy-start(f32[6,24]{1,0:T(8,128)} %mix_ref.1) | copy-start | bytes 1732
  5.6 7.1 %collective-permute-start.1 = (bf16[3,16,128]{2,1,0:T(8,128)(2,1)S(1)}, bf16[3,16,128]{2,1,0:T(8,128)(2,1)S(1)}, u32[]{:S(2)}, u32[]{:S(2)}) collective-permute-start(bf16[3,16,128]{2,1,0:T(8,128)(2,1)S(1)} %pack_east.1), channel_id=1, source_target_pairs={{1,0},{2,1},{3,2},{4,3},{5,4},{6,5},{7,6},{8,7},{9,8},{10,9},{11,1... | collective-permute-start | bytes 36872 | tf_op jit(solution)/shard_map/ppermute | solution.py:348
  29.5 2.1 %copy-start.2 = (f32[24,24]{1,0:T(8,128)S(1)}, f32[24,24]{1,0:T(8,128)}, u32[]{:S(2)}) copy-start(f32[24,24]{1,0:T(8,128)} %proj_ref.1) | copy-start | bytes 6916
  31.6 0.7 copy-start.6
  31.6 0.7 copy-start.5
  31.6 0.7 copy-start.8
  33.6 5.1 %collective-permute-start.2 = (f32[3,24,128]{2,1,0:T(8,128)S(1)}, f32[3,24,128]{2,1,0:T(8,128)S(1)}, u32[]{:S(2)}, u32[]{:S(2)}) collective-permute-start(f32[3,24,128]{2,1,0:T(8,128)S(1)} %get-tuple-element.19), channel_id=1, source_target_pairs={{0,32},{32,64},{64,96},{96,128},{128,160},{160,192},{192,224},{1,3... | collective-permute-start | bytes 110600 | tf_op jit(solution)/shard_map/ppermute | solution.py:348
  37.1 5.9 %collective-permute-start.3 = (f32[3,24,128]{2,1,0:T(8,128)S(1)}, f32[3,24,128]{2,1,0:T(8,128)S(1)}, u32[]{:S(2)}, u32[]{:S(2)}) collective-permute-start(f32[3,24,128]{2,1,0:T(8,128)S(1)} %get-tuple-element.20), channel_id=1, source_target_pairs={{32,0},{64,32},{96,64},{128,96},{160,128},{192,160},{224,192},{33,... | collective-permute-start | bytes 110600 | tf_op jit(solution)/shard_map/ppermute | solution.py:348
  43.1 7.5 %copy-start.7 = (f32[24]{0:T(128)S(1)}, f32[24]{0:T(128)}, u32[]{:S(2)}) copy-start(f32[24]{0:T(128)} %param.14) | copy-start | bytes 292
  43.1 5.9 %collective-permute-start.5 = (f32[3,8,128]{2,1,0:T(8,128)S(1)}, f32[3,8,128]{2,1,0:T(8,128)S(1)}, u32[]{:S(2)}, u32[]{:S(2)}) collective-permute-start(f32[3,8,128]{2,1,0:T(8,128)S(1)} %pack_columns.1), channel_id=1, source_target_pairs={{1,0},{2,1},{3,2},{4,3},{5,4},{6,5},{7,6},{8,7},{9,8},{10,9},{11,1... | collective-permute-start | bytes 36872 | tf_op jit(solution)/shard_map/ppermute | solution.py:348
  45.0 5.6 %collective-permute-start.4 = (f32[3,8,128]{2,1,0:T(8,128)S(1)}, f32[3,8,128]{2,1,0:T(8,128)S(1)}, u32[]{:S(2)}, u32[]{:S(2)}) collective-permute-start(f32[3,8,128]{2,1,0:T(8,128)S(1)} %pack_columns.1), channel_id=1, source_target_pairs={{0,1},{1,2},{2,3},{3,4},{4,5},{5,6},{6,7},{7,8},{8,9},{9,10},{10,1... | collective-permute-start | bytes 36872 | tf_op jit(solution)/shard_map/ppermute | solution.py:348

commit v2 on v1

--- a/solution.py
+++ b/solution.py
@@ -54,6 +54,10 @@
     )(fields)
 
 
+def half_mask(mask):
+    return jnp.where(mask, 1, 0).astype(jnp.int16) == jnp.int16(1)
+
+
 def advect_kernel(mix_ref, shift_ref, frac_ref, fields_ref, west_ref, east_ref, adv_ref, rhs_ref, half_ref):
     g = pl.program_id(0)
     lon = lax.axis_index("lon")
@@ -61,10 +65,11 @@
     own = jnp.sum(jnp.where(lane_iota(table.shape) == lon, table, 0), axis=1, keepdims=True)
     shift = jnp.broadcast_to(own, (ROWS, COLS))
     lane = lane_iota((ROWS, COLS))
-    odd = (shift & 1) == 1
-    two = (shift & 2) == 2
-
-    def turn(x, sign):
+    odd, two = (shift & 1) == 1, (shift & 2) == 2
+    odd16, two16 = half_mask(odd), half_mask(two)
+    edge16 = half_mask(lane < 2)
+
+    def turn(x, sign, odd, two):
         x = jnp.where(odd, roll_lanes(x, 32 * sign), x)
         return jnp.where(two, roll_lanes(x, 64), x)
 
@@ -73,11 +78,13 @@
         return (at < 0) | (at >= COLS)
 
     taps = (-1, 0, 1, 2)
-    masks = [beyond(j) for j in taps]
-    edge = lane < 2
-    east = east_ref[0].astype(F32)
+    masks = [half_mask(beyond(j)) for j in taps]
+    source = lax.broadcasted_iota(jnp.int32, (COLS, COLS), 0)
+    target = lax.broadcasted_iota(jnp.int32, (COLS, COLS), 1)
+    shifts = [jnp.where(source == ((target + j) & (COLS - 1)), 1.0, 0.0).astype(BF16) for j in taps]
+    east = east_ref[0]
     for l8 in range(8):
-        t = turn(frac_ref[l8], -1)
+        t = turn(frac_ref[l8], -1, odd, two)
         tm1, tm2, tp1 = t - 1.0, t - 2.0, t + 1.0
         weights = (
             -t * tm1 * tm2 * (1.0 / 6.0),
@@ -85,19 +92,27 @@
             -tp1 * t * tm2 * 0.5,
             tp1 * t * tm1 * (1.0 / 6.0),
         )
+        chosen = [[] for _ in taps]
+        for f in range(NF):
+            other = jnp.where(edge16, roll_lanes(east, -2 * (f * 8 + l8)), west_ref[f, l8])
+            for n, mask in enumerate(masks):
+                chosen[n].append(jnp.where(mask, other, fields_ref[f, l8]))
+        moved = []
+        for j, parts, matrix in zip(taps, chosen, shifts):
+            if j == 0:
+                moved.append([part.astype(F32) for part in parts])
+            else:
+                wide = jnp.dot(jnp.concatenate(parts, axis=0), matrix, preferred_element_type=F32)
+                moved.append([wide[ROWS * f : ROWS * f + ROWS] for f in range(NF)])
         total = jnp.zeros((ROWS, COLS), F32)
         for f in range(NF):
-            own_row = fields_ref[f, l8].astype(F32)
-            other = jnp.where(edge, roll_lanes(east, -2 * (f * 8 + l8)), west_ref[f, l8].astype(F32))
-            acc = None
-            for j, mask, weight in zip(taps, masks, weights):
-                term = weight * roll_lanes(jnp.where(mask, other, own_row), -j)
-                acc = term if acc is None else acc + term
+            acc = weights[0] * moved[0][f]
+            for n in range(1, 4):
+                acc = acc + weights[n] * moved[n][f]
             rounded = acc.astype(BF16)
-            acc = rounded.astype(F32)
-            adv_ref[f, l8] = turn(acc, 1).astype(BF16)
-            total = total + mix_ref[f, g * 8 + l8] * acc
-        rhs_ref[0, pl.ds(l8, ROWS, stride=8), :] = turn(total, 1)
+            adv_ref[f, l8] = turn(rounded, 1, odd16, two16)
+            total = total + mix_ref[f, g * 8 + l8] * rounded.astype(F32)
+        rhs_ref[0, pl.ds(l8, ROWS, stride=8), :] = turn(total, 1, odd, two)
     half_ref[0] = rhs_ref[0].astype(BF16)
 
 
@@ -284,22 +299,30 @@
         for q in range(8):
             total = jnp.sum(sums[q], axis=1, keepdims=True)
             sums_out = jnp.where(lane == 8 * lb + q, total, sums_out)
-    s_ref[...] = sums_out
-
-
-def images(mode_shift, b, north, south, from_west, from_east):
+    for n in range(s_ref.shape[0]):
+        s_ref[n] = sums_out
+
+
+def images(mode_shift, b, north, south, from_west, from_east, copies):
     full = jax.ShapeDtypeStruct((G, 128, COLS), F32)
     return pl.pallas_call(
         images_kernel,
-        out_shape=[full, full, full, jax.ShapeDtypeStruct((8, COLS), F32)],
+        out_shape=[full, full, full, jax.ShapeDtypeStruct((copies, 8, COLS), F32)],
         compiler_params=params(),
         name="images",
     )(mode_shift, b, north, south, from_west, from_east)
 
 
+def sum_copies(ref):
+    parts = [ref[n] for n in range(ref.shape[0])]
+    while len(parts) > 1:
+        parts = [parts[n] + parts[n + 1] for n in range(0, len(parts), 2)]
+    return parts[0]
+
+
 def iterate_kernel(shift_ref, s_ref, b_ref, c_ref, u1_ref, u2_ref, sol_ref, res_ref):
     lane = lane_iota((8, COLS))
-    sums = s_ref[...]
+    sums = sum_copies(s_ref)
     for lb in range(G):
         diag = lane_iota((8, LEV)) == (lax.broadcasted_iota(jnp.int32, (8, LEV), 0) + 8 * lb)
         a = 4.0 + jnp.sum(jnp.where(diag, jnp.broadcast_to(shift_ref[...], (8, LEV)), 0.0), axis=1, keepdims=True)
@@ -348,18 +371,19 @@
     return lax.ppermute(block, axis, [(i, i + by) for i in range(count) if 0 <= i + by < count])
 
 
-def groups_of_lon(count):
-    along_x = [[4 * z + x for x in range(4)] for z in range(count // 4)]
-    along_z = [[4 * z + x for z in range(count // 4)] for x in range(4)]
-    return along_x, along_z
-
-
-def reduced(sums):
-    along_x, along_z = groups_of_lon(lax.axis_size("lon"))
-    sums = lax.psum(sums, "panel")
-    sums = lax.psum(sums, "lon", axis_index_groups=along_x)
-    sums = lax.psum(sums, "lat")
-    return lax.psum(sums, "lon", axis_index_groups=along_z)
+def relay_kernel(in_ref, out_ref):
+    total = sum_copies(in_ref)
+    for n in range(out_ref.shape[0]):
+        out_ref[n] = total
+
+
+def relay(parts, copies):
+    return pl.pallas_call(
+        relay_kernel,
+        out_shape=jax.ShapeDtypeStruct((copies, 8, COLS), F32),
+        compiler_params=params(),
+        name="relay",
+    )(parts)
 
 
 def per_device(fields, frac, shift, mix, proj, mode_shift, cells, source, weight):
@@ -375,8 +399,12 @@
     from_west = send(columns, "lon", 1)
     from_east = send(columns, "lon", -1)
     shifts = mode_shift.reshape(1, LEV)
-    c, u1, u2, sums = images(shifts, b, north, south, from_west, from_east)
-    sol, res = iterate(shifts, reduced(sums), b, c, u1, u2)
+    count = lax.axis_size("lon")
+    rest = lax.axis_size("panel") * lax.axis_size("lat")
+    c, u1, u2, sums = images(shifts, b, north, south, from_west, from_east, count)
+    sums = relay(lax.all_to_all(sums, "lon", 0, 0), rest)
+    sums = lax.all_to_all(sums, ("panel", "lat"), 0, 0)
+    sol, res = iterate(shifts, sums, b, c, u1, u2)
     shape = (1, LEV, ROWS, COLS)
     return adv[None], sol.reshape(shape), res.reshape(shape)
 

time: 111 us -> 89.3 us (0.80)
  the two profiles are of different devices: /device:TPU:2 before, /device:TPU:1 now
where the time goes in v2:
time: 89.3 us; the launch traced here: 88.9 us
  blocking collectives  51.8 us (58%)
  starting transfers between devices  15.7 us (18%)
  waiting for transfers between devices  10.3 us (12%)
  Pallas kernels  8.53 us (10%)
  local copies, waits for them, and re-layouts  1.8 us (2%)
    all_to_all x1, blocking collectives, per_device(): sums = relay(lax.all_to_all(sums, 'lon', 0, 0), rest)  26.7 us
    all_to_all x1, blocking collectives, per_device(): sums = lax.all_to_all(sums, ('panel', 'lat'), 0, 0)  18.5 us
    ppermute x6, starting transfers between devices, send(): lax.ppermute(block, axis, [(i, i + by) for i in range(count) if 0 <= i +...  15.7 us
    ppermute x6, waiting for transfers between devices, send(): lax.ppermute(block, axis, [(i, i + by) for i in range(count) if 0 <= i +...  10.3 us
    all_gather x1, blocking collectives, per_device(): both = lax.all_gather(half, 'panel')  6.57 us
    pallas_call x1, Pallas kernels, advect(): pl.pallas_call(advect_kernel, grid=(G,), in_specs=[pl.BlockSpec(memory_sp...  3.4 us
    pallas_call x1, Pallas kernels, images(): pl.pallas_call(images_kernel, out_shape=[full, full, full, jax.ShapeDtype...  2.23 us
    unnamed x18, local copies, waits for them, and re-layouts  1.8 us
  transfers between devices with their start and end apart: 6, of which 4 were waited for; matrix products, arithmetic and copies ran while one was open for 0% of the time, Pallas kernels for 1%

profile of v2, /device:TPU:1, one launch (start us, length us, event | category | flops | bytes accessed | tf_op | source)
XLA Modules:
  0.0 88.9 jit_solution(5208824339471826511)
XLA Ops:
  0.6 4.0 %collective-permute-start = (bf16[6,24,16,128]{3,2,1,0:T(8,128)(2,1)}, bf16[6,24,16,128]{3,2,1,0:T(8,128)(2,1)S(1)}, u32[]{:S(2)}, u32[]{:S(2)}) collective-permute-start(bf16[6,24,16,128]{3,2,1,0:T(8,128)(2,1)} %bitcast.15), channel_id=1, source_target_pairs={{0,1},{1,2},{2,3},{3,4},{4,5},{5,6},{6,7},{7,8},{8,9},{9,10},{10,1... | collective-permute-start | bytes 1769480 | tf_op jit(solution)/shard_map/ppermute | solution.py:371
  4.6 1.1 %copy-done = bf16[1,6,24,16,128]{4,3,2,1,0:T(8,128)(2,1)S(1)} copy-done((bf16[1,6,24,16,128]{4,3,2,1,0:T(8,128)(2,1)S(1)}, bf16[1,6,24,16,128]{4,3,2,1,0:T(8,128)(2,1)}, u32[]{:S(2)}) %copy-start) | copy-done | bytes 589848
  5.7 0.5 pack_east.1
  6.2 1.3 %collective-permute-start.1 = (bf16[3,16,128]{2,1,0:T(8,128)(2,1)S(1)}, bf16[3,16,128]{2,1,0:T(8,128)(2,1)S(1)}, u32[]{:S(2)}, u32[]{:S(2)}) collective-permute-start(bf16[3,16,128]{2,1,0:T(8,128)(2,1)S(1)} %pack_east.1), channel_id=1, source_target_pairs={{1,0},{2,1},{3,2},{4,3},{5,4},{6,5},{7,6},{8,7},{9,8},{10,9},{11,1... | collective-permute-start | bytes 36872 | tf_op jit(solution)/shard_map/ppermute | solution.py:371
  7.5 3.1 %collective-permute-done.1.east_ref = bf16[3,16,128]{2,1,0:T(8,128)(2,1)S(1)} collective-permute-done((bf16[3,16,128]{2,1,0:T(8,128)(2,1)S(1)}, bf16[3,16,128]{2,1,0:T(8,128)(2,1)S(1)}, u32[]{:S(2)}, u32[]{:S(2)}) %collective-permute-start.1) | collective-permute-done | bytes 12320 | tf_op jit(solution)/shard_map/ppermute | solution.py:371
  10.6 3.0 %collective-permute-done.west_ref = bf16[6,24,16,128]{3,2,1,0:T(8,128)(2,1)S(1)} collective-permute-done((bf16[6,24,16,128]{3,2,1,0:T(8,128)(2,1)}, bf16[6,24,16,128]{3,2,1,0:T(8,128)(2,1)S(1)}, u32[]{:S(2)}, u32[]{:S(2)}) %collective-permute-start) | collective-permute-done | bytes 589856 | tf_op jit(solution)/shard_map/ppermute | solution.py:371
  13.6 3.4 %advect.1 = (bf16[6,24,16,128]{3,2,1,0:T(8,128)(2,1)}, f32[3,128,128]{2,1,0:T(8,128)S(1)}, bf16[3,128,128]{2,1,0:T(8,128)(2,1)S(1)}) custom-call(f32[6,24]{1,0:T(8,128)S(1)} %copy-done.4, s32[16,32]{1,0:T(8,128)S(1)} %bitcast.20, f32[24,16,128]{2,1,0:T(8,128)S(1)} %bitcast.19, bf16[6,24,16,128]{3,2,1,0:T(8,128)(2,1)S(1)} %bitcast.17, ...), custom_call_target="tpu_custom_call" | custom-call | tf_op jit(solution)/shard_map/advect/pallas_call | solution.py:122
  17.0 6.6 %all-gather = bf16[6,128,128]{2,1,0:T(8,128)(2,1)S(1)} all-gather(bf16[3,128,128]{2,1,0:T(8,128)(2,1)S(1)} %get-tuple-element.17), channel_id=2, replica_groups=mesh['panel'=2,'lat'=8,'lon'=32] {'panel'}, dimensions={0}, use_global_device_ids=true | all-gather | bytes 294912 | tf_op jit(solution)/shard_map/all_gather | solution.py:394
  23.6 0.7 copy-done.6
  24.2 0.0 copy-done.5
  24.2 0.0 copy-done.8
  24.3 1.3 %margin.1 = (f32[3,128,128]{2,1,0:T(8,128)S(1)}, f32[3,24,128]{2,1,0:T(8,128)S(1)}, f32[3,24,128]{2,1,0:T(8,128)S(1)}) custom-call(f32[3,128,128]{2,1,0:T(8,128)S(1)} %get-tuple-element.16.rhs_ref, bf16[2,3,128,128]{3,2,1,0:T(8,128)(2,1)S(1)} %bitcast.18, s32[1,256]{1,0:T(1,128)S(1)} %bitcast.25, s32[4,256]{1,0:T(4,128)S(1)} %bitcast.21, ...), custom_call_target="tpu_custom_call" | custom-call | tf_op jit(solution)/shard_map/margin/pallas_call | solution.py:196
  25.6 3.2 %collective-permute-start.2 = (f32[3,24,128]{2,1,0:T(8,128)S(1)}, f32[3,24,128]{2,1,0:T(8,128)S(1)}, u32[]{:S(2)}, u32[]{:S(2)}) collective-permute-start(f32[3,24,128]{2,1,0:T(8,128)S(1)} %get-tuple-element.19), channel_id=1, source_target_pairs={{0,32},{32,64},{64,96},{96,128},{128,160},{160,192},{192,224},{1,3... | collective-permute-start | bytes 110600 | tf_op jit(solution)/shard_map/ppermute | solution.py:371
  28.8 1.3 %collective-permute-start.3 = (f32[3,24,128]{2,1,0:T(8,128)S(1)}, f32[3,24,128]{2,1,0:T(8,128)S(1)}, u32[]{:S(2)}, u32[]{:S(2)}) collective-permute-start(f32[3,24,128]{2,1,0:T(8,128)S(1)} %get-tuple-element.20), channel_id=1, source_target_pairs={{32,0},{64,32},{96,64},{128,96},{160,128},{192,160},{224,192},{33,... | collective-permute-start | bytes 110600 | tf_op jit(solution)/shard_map/ppermute | solution.py:371
  30.1 3.4 %collective-permute-done.3.south_ref = f32[3,24,128]{2,1,0:T(8,128)S(1)} collective-permute-done((f32[3,24,128]{2,1,0:T(8,128)S(1)}, f32[3,24,128]{2,1,0:T(8,128)S(1)}, u32[]{:S(2)}, u32[]{:S(2)}) %collective-permute-start.3) | collective-permute-done | bytes 36896 | tf_op jit(solution)/shard_map/ppermute | solution.py:371
  33.5 0.1 pack_columns.1
  33.6 0.0 copy-start.7
  33.6 1.3 %collective-permute-start.5 = (f32[3,8,128]{2,1,0:T(8,128)S(1)}, f32[3,8,128]{2,1,0:T(8,128)S(1)}, u32[]{:S(2)}, u32[]{:S(2)}) collective-permute-start(f32[3,8,128]{2,1,0:T(8,128)S(1)} %pack_columns.1), channel_id=1, source_target_pairs={{1,0},{2,1},{3,2},{4,3},{5,4},{6,5},{7,6},{8,7},{9,8},{10,9},{11,1... | collective-permute-start | bytes 36872 | tf_op jit(solution)/shard_map/ppermute | solution.py:371
  34.9 4.7 %collective-permute-start.4 = (f32[3,8,128]{2,1,0:T(8,128)S(1)}, f32[3,8,128]{2,1,0:T(8,128)S(1)}, u32[]{:S(2)}, u32[]{:S(2)}) collective-permute-start(f32[3,8,128]{2,1,0:T(8,128)S(1)} %pack_columns.1), channel_id=1, source_target_pairs={{0,1},{1,2},{2,3},{3,4},{4,5},{5,6},{6,7},{7,8},{8,9},{9,10},{10,1... | collective-permute-start | bytes 36872 | tf_op jit(solution)/shard_map/ppermute | solution.py:371
  39.6 0.8 collective-permute-done.4.fwest_ref
  40.4 2.2 %images.1 = (f32[3,128,128]{2,1,0:T(8,128)S(1)}, f32[3,128,128]{2,1,0:T(8,128)S(1)}, f32[3,128,128]{2,1,0:T(8,128)S(1)}, f32[32,8,128]{2,1,0:T(8,128)S(1)}) custom-call(f32[1,24]{1,0:T(1,128)S(1)} %bitcast.23, f32[3,128,128]{2,1,0:T(8,128)S(1)} %get-tuple-element.18.b_ref, f32[3,24,128]{2,1,0:T(8,128)S(1)} %collective-permute-done.2.north_ref, ...), custom_call_target="tpu_custom_call" | custom-call | tf_op jit(solution)/shard_map/images/pallas_call | solution.py:308
  42.6 26.7 %all_to_all.10.in_ref = f32[32,8,128]{2,1,0:T(8,128)S(1)} all-to-all(f32[32,8,128]{2,1,0:T(8,128)S(1)} %get-tuple-element.21), channel_id=1, replica_groups=mesh['panel'=2,'lat'=8,'lon'=32] {'lon'}, dimensions={0} | all-to-all | bytes 262144 | tf_op jit(solution)/shard_map/all_to_all | solution.py:405
  69.3 18.5 %all_to_all.11.s_ref = f32[16,8,128]{2,1,0:T(8,128)S(1)} all-to-all(f32[16,8,128]{2,1,0:T(8,128)S(1)} %relay.1), channel_id=1, replica_groups=mesh['panel'=2,'lat'=8,'lon'=32] {'panel','lat'}, dimensions={0} | all-to-all | bytes 131072 | tf_op jit(solution)/shard_map/all_to_all | solution.py:406
  87.9 1.0 %iterate.1 = (f32[384,128]{1,0:T(8,128)}, f32[384,128]{1,0:T(8,128)}) custom-call(f32[1,24]{1,0:T(1,128)S(1)} %bitcast.24, f32[16,8,128]{2,1,0:T(8,128)S(1)} %all_to_all.11.s_ref, f32[3,128,128]{2,1,0:T(8,128)S(1)} %get-tuple-element.18.b_ref, f32[3,128,128]{2,1,0:T(8,128)S(1)} %get-tuple-element.22.c_ref, f32[3,128,128]{2,1,0:T(8,128)S(1)} %get-tuple-element.23.u1_ref, ...), custom_call_target="tpu_custom_call" | custom-call | tf_op jit(solution)/shard_map/iterate/pallas_call | solution.py:361
  (16 shorter events, 0.0 us)
Async XLA Ops:
  0.6 12.9 %collective-permute-start = (bf16[6,24,16,128]{3,2,1,0:T(8,128)(2,1)}, bf16[6,24,16,128]{3,2,1,0:T(8,128)(2,1)S(1)}, u32[]{:S(2)}, u32[]{:S(2)}) collective-permute-start(bf16[6,24,16,128]{3,2,1,0:T(8,128)(2,1)} %bitcast.15), channel_id=1, source_target_pairs={{0,1},{1,2},{2,3},{3,4},{4,5},{5,6},{6,7},{7,8},{8,9},{9,10},{10,1... | collective-permute-start | bytes 1769480 | tf_op jit(solution)/shard_map/ppermute | solution.py:371
  4.6 1.1 %copy-start = (bf16[1,6,24,16,128]{4,3,2,1,0:T(8,128)(2,1)S(1)}, bf16[1,6,24,16,128]{4,3,2,1,0:T(8,128)(2,1)}, u32[]{:S(2)}) copy-start(bf16[1,6,24,16,128]{4,3,2,1,0:T(8,128)(2,1)} %param.9) | copy-start | bytes 1769476
  5.7 7.9 %copy-start.1 = (f32[1,24,16,128]{3,2,1,0:T(8,128)S(1)}, f32[1,24,16,128]{3,2,1,0:T(8,128)}, u32[]{:S(2)}) copy-start(f32[1,24,16,128]{3,2,1,0:T(8,128)} %param.10) | copy-start | bytes 589828
  5.7 7.9 %copy-start.3 = (s32[1,16,32]{2,1,0:T(8,128)S(1)}, s32[1,16,32]{2,1,0:T(8,128)}, u32[]{:S(2)}) copy-start(s32[1,16,32]{2,1,0:T(8,128)} %param.11) | copy-start | bytes 6148
  5.7 7.9 %copy-start.4 = (f32[6,24]{1,0:T(8,128)S(1)}, f32[6,24]{1,0:T(8,128)}, u32[]{:S(2)}) copy-start(f32[6,24]{1,0:T(8,128)} %mix_ref.1) | copy-start | bytes 1732
  6.2 4.4 %collective-permute-start.1 = (bf16[3,16,128]{2,1,0:T(8,128)(2,1)S(1)}, bf16[3,16,128]{2,1,0:T(8,128)(2,1)S(1)}, u32[]{:S(2)}, u32[]{:S(2)}) collective-permute-start(bf16[3,16,128]{2,1,0:T(8,128)(2,1)S(1)} %pack_east.1), channel_id=1, source_target_pairs={{1,0},{2,1},{3,2},{4,3},{5,4},{6,5},{7,6},{8,7},{9,8},{10,9},{11,1... | collective-permute-start | bytes 36872 | tf_op jit(solution)/shard_map/ppermute | solution.py:371
  17.0 6.6 %copy-start.2 = (f32[24,24]{1,0:T(8,128)S(1)}, f32[24,24]{1,0:T(8,128)}, u32[]{:S(2)}) copy-start(f32[24,24]{1,0:T(8,128)} %proj_ref.1) | copy-start | bytes 6916
  23.5 0.7 copy-start.6
  23.5 0.7 copy-start.5
  23.5 0.7 copy-start.8
  25.6 4.5 %collective-permute-start.2 = (f32[3,24,128]{2,1,0:T(8,128)S(1)}, f32[3,24,128]{2,1,0:T(8,128)S(1)}, u32[]{:S(2)}, u32[]{:S(2)}) collective-permute-start(f32[3,24,128]{2,1,0:T(8,128)S(1)} %get-tuple-element.19), channel_id=1, source_target_pairs={{0,32},{32,64},{64,96},{96,128},{128,160},{160,192},{192,224},{1,3... | collective-permute-start | bytes 110600 | tf_op jit(solution)/shard_map/ppermute | solution.py:371
  28.8 4.7 %collective-permute-start.3 = (f32[3,24,128]{2,1,0:T(8,128)S(1)}, f32[3,24,128]{2,1,0:T(8,128)S(1)}, u32[]{:S(2)}, u32[]{:S(2)}) collective-permute-start(f32[3,24,128]{2,1,0:T(8,128)S(1)} %get-tuple-element.20), channel_id=1, source_target_pairs={{32,0},{64,32},{96,64},{128,96},{160,128},{192,160},{224,192},{33,... | collective-permute-start | bytes 110600 | tf_op jit(solution)/shard_map/ppermute | solution.py:371
  33.6 6.8 %copy-start.7 = (f32[24]{0:T(128)S(1)}, f32[24]{0:T(128)}, u32[]{:S(2)}) copy-start(f32[24]{0:T(128)} %param.14) | copy-start | bytes 292
  33.6 6.0 %collective-permute-start.5 = (f32[3,8,128]{2,1,0:T(8,128)S(1)}, f32[3,8,128]{2,1,0:T(8,128)S(1)}, u32[]{:S(2)}, u32[]{:S(2)}) collective-permute-start(f32[3,8,128]{2,1,0:T(8,128)S(1)} %pack_columns.1), channel_id=1, source_target_pairs={{1,0},{2,1},{3,2},{4,3},{5,4},{6,5},{7,6},{8,7},{9,8},{10,9},{11,1... | collective-permute-start | bytes 36872 | tf_op jit(solution)/shard_map/ppermute | solution.py:371
  34.9 5.5 %collective-permute-start.4 = (f32[3,8,128]{2,1,0:T(8,128)S(1)}, f32[3,8,128]{2,1,0:T(8,128)S(1)}, u32[]{:S(2)}, u32[]{:S(2)}) collective-permute-start(f32[3,8,128]{2,1,0:T(8,128)S(1)} %pack_columns.1), channel_id=1, source_target_pairs={{0,1},{1,2},{2,3},{3,4},{4,5},{5,6},{6,7},{7,8},{8,9},{9,10},{10,1... | collective-permute-start | bytes 36872 | tf_op jit(solution)/shard_map/ppermute | solution.py:371

commit v3 on v2

--- a/solution.py
+++ b/solution.py
@@ -31,40 +31,92 @@
     return pltpu.CompilerParams(vmem_limit_bytes=VMEM_LIMIT)
 
 
-def pack_east_kernel(fields_ref, out_ref):
+def own_shift(shift_ref, lon):
+    table = shift_ref[...]
+    own = jnp.sum(jnp.where(lane_iota(table.shape) == lon, table, 0), axis=1, keepdims=True)
+    return jnp.broadcast_to(own, (ROWS, COLS))
+
+
+def half_mask(mask):
+    return jnp.where(mask, 1, 0).astype(jnp.int16) == jnp.int16(1)
+
+
+def lane_matrix(rule):
+    source = lax.broadcasted_iota(jnp.int32, (COLS, COLS), 0)
+    target = lax.broadcasted_iota(jnp.int32, (COLS, COLS), 1)
+    return jnp.where(rule(source, target), 1.0, 0.0).astype(BF16)
+
+
+def mirrored(source, target):
+    return (target >= 32) & (source == jnp.where((target >> 5) == 2, target, (target + 64) & (COLS - 1)))
+
+
+def pack_kernel(shift_ref, fields_ref, west_ref, east_ref, scratch):
+    shift = own_shift(shift_ref, lax.axis_index("lon") + 1)
     lane = lane_iota((ROWS, COLS))
+    low = (lax.broadcasted_iota(jnp.int32, (ROWS, COLS), 0) & 1) == 0
+    block = lane >= COLS - 32 * shift
+    single = lane == COLS - 1 - 32 * shift
+    masks = [half_mask(m & row) for row in (low, ~low) for m in (block, single)]
+    matrix = jnp.concatenate(
+        [
+            lane_matrix(lambda s, t: s == t),
+            lane_matrix(lambda s, t: ((s & 31) == 31) & (t == 31)),
+            lane_matrix(mirrored),
+            lane_matrix(lambda s, t: ((s & 31) == 31) & (t == 30)),
+        ],
+        axis=0,
+    )
+    zero = jnp.zeros((ROWS, COLS), BF16)
     acc = jnp.zeros((ROWS, COLS), F32)
-    for f in range(NF):
-        for l8 in range(8):
+    for l8 in range(8):
+        parts = [
+            jnp.concatenate([jnp.where(m, fields_ref[f, l8], zero) for m in masks], axis=1) for f in range(NF)
+        ]
+        scratch[l8] = jnp.dot(jnp.concatenate(parts, axis=0), matrix, preferred_element_type=F32)
+        pairs = scratch[l8, pl.ds(0, 8 * NF, stride=2), :] + scratch[l8, pl.ds(1, 8 * NF, stride=2), :]
+        pairs = pairs.astype(BF16)
+        for n in range(NF // 2):
+            west_ref[n, l8] = pairs[ROWS * n : ROWS * n + ROWS]
+        for f in range(NF):
             i = f * 8 + l8
             x = roll_lanes(fields_ref[f, l8].astype(F32), 2 * i)
             acc = jnp.where((lane >> 1) == i, x, acc)
-    out_ref[0] = acc.astype(BF16)
-
-
-def pack_east(fields):
-    return pl.pallas_call(
-        pack_east_kernel,
+    east_ref[0] = acc.astype(BF16)
+
+
+def pack(shift, fields):
+    return pl.pallas_call(
+        pack_kernel,
         grid=(G,),
-        in_specs=[pl.BlockSpec((NF, 8, ROWS, COLS), lambda g: (0, g, 0, 0))],
-        out_specs=pl.BlockSpec((1, ROWS, COLS), lambda g: (g, 0, 0)),
-        out_shape=jax.ShapeDtypeStruct((G, ROWS, COLS), BF16),
-        compiler_params=params(),
-        name="pack_east",
-    )(fields)
-
-
-def half_mask(mask):
-    return jnp.where(mask, 1, 0).astype(jnp.int16) == jnp.int16(1)
-
-
-def advect_kernel(mix_ref, shift_ref, frac_ref, fields_ref, west_ref, east_ref, adv_ref, rhs_ref, half_ref):
+        in_specs=[
+            pl.BlockSpec((ROWS, 32), lambda g: (0, 0)),
+            pl.BlockSpec((NF, 8, ROWS, COLS), lambda g: (0, g, 0, 0)),
+        ],
+        out_specs=[
+            pl.BlockSpec((NF // 2, 8, ROWS, COLS), lambda g: (0, g, 0, 0)),
+            pl.BlockSpec((1, ROWS, COLS), lambda g: (g, 0, 0)),
+        ],
+        out_shape=[
+            jax.ShapeDtypeStruct((NF // 2, LEV, ROWS, COLS), BF16),
+            jax.ShapeDtypeStruct((G, ROWS, COLS), BF16),
+        ],
+        scratch_shapes=[pltpu.VMEM((8, NF * ROWS, COLS), F32)],
+        compiler_params=params(),
+        name="pack",
+    )(shift, fields)
+
+
+def advect_kernel(mix_ref, shift_ref, frac_ref, fields_ref, west_ref, east_ref, adv_ref, rhs_ref, half_ref, scratch):
     g = pl.program_id(0)
-    lon = lax.axis_index("lon")
-    table = shift_ref[...]
-    own = jnp.sum(jnp.where(lane_iota(table.shape) == lon, table, 0), axis=1, keepdims=True)
-    shift = jnp.broadcast_to(own, (ROWS, COLS))
+    shift = own_shift(shift_ref, lax.axis_index("lon"))
     lane = lane_iota((ROWS, COLS))
+    low = (lax.broadcasted_iota(jnp.int32, (ROWS, COLS), 0) & 1) == 0
+    swap16 = half_mask(~low & ((lane >> 5) != 2))
+    single16 = half_mask(lane == jnp.where(low, 31, 30))
+    single_at = jnp.concatenate([lane == ((COLS - 32 * shift) & (COLS - 1))] * NF, axis=0)
+    single_to = lane_matrix(lambda s, t: ((s == 30) | (s == 31)) & ((t & 31) == 0))
+    zero = jnp.zeros((ROWS, COLS), BF16)
     odd, two = (shift & 1) == 1, (shift & 2) == 2
     odd16, two16 = half_mask(odd), half_mask(two)
     edge16 = half_mask(lane < 2)
@@ -79,9 +131,7 @@
 
     taps = (-1, 0, 1, 2)
     masks = [half_mask(beyond(j)) for j in taps]
-    source = lax.broadcasted_iota(jnp.int32, (COLS, COLS), 0)
-    target = lax.broadcasted_iota(jnp.int32, (COLS, COLS), 1)
-    shifts = [jnp.where(source == ((target + j) & (COLS - 1)), 1.0, 0.0).astype(BF16) for j in taps]
+    shifts = [lane_matrix(lambda s, t, j=j: s == ((t + j) & (COLS - 1))) for j in taps]
     east = east_ref[0]
     for l8 in range(8):
         t = turn(frac_ref[l8], -1, odd, two)
@@ -92,9 +142,17 @@
             -tp1 * t * tm2 * 0.5,
             tp1 * t * tm1 * (1.0 / 6.0),
         )
+        shared = jnp.concatenate([west_ref[n, l8] for n in range(NF // 2)], axis=0).astype(F32)
+        scratch[l8, pl.ds(0, 8 * NF, stride=2), :] = shared
+        scratch[l8, pl.ds(1, 8 * NF, stride=2), :] = shared
+        west = scratch[l8].astype(BF16)
         chosen = [[] for _ in taps]
+        singles = []
         for f in range(NF):
-            other = jnp.where(edge16, roll_lanes(east, -2 * (f * 8 + l8)), west_ref[f, l8])
+            other = west[ROWS * f : ROWS * f + ROWS]
+            singles.append(jnp.where(single16, other, zero))
+            other = jnp.where(swap16, roll_lanes(other, 64), other)
+            other = jnp.where(edge16, roll_lanes(east, -2 * (f * 8 + l8)), other)
             for n, mask in enumerate(masks):
                 chosen[n].append(jnp.where(mask, other, fields_ref[f, l8]))
         moved = []
@@ -103,6 +161,9 @@
                 moved.append([part.astype(F32) for part in parts])
             else:
                 wide = jnp.dot(jnp.concatenate(parts, axis=0), matrix, preferred_element_type=F32)
+                if j == -1:
+                    column = jnp.dot(jnp.concatenate(singles, axis=0), single_to, preferred_element_type=F32)
+                    wide = jnp.where(single_at, column, wide)
                 moved.append([wide[ROWS * f : ROWS * f + ROWS] for f in range(NF)])
         total = jnp.zeros((ROWS, COLS), F32)
         for f in range(NF):
@@ -127,7 +188,7 @@
             pl.BlockSpec((ROWS, 32), lambda g: (0, 0)),
             pl.BlockSpec((8, ROWS, COLS), lambda g: (g, 0, 0)),
             block,
-            block,
+            pl.BlockSpec((NF // 2, 8, ROWS, COLS), lambda g: (0, g, 0, 0)),
             pl.BlockSpec((1, ROWS, COLS), lambda g: (g, 0, 0)),
         ],
         out_specs=[block, group, group],
@@ -136,6 +197,7 @@
             jax.ShapeDtypeStruct((G, 128, COLS), F32),
             jax.ShapeDtypeStruct((G, 128, COLS), BF16),
         ],
+        scratch_shapes=[pltpu.VMEM((8, NF * ROWS, COLS), F32)],
         compiler_params=params(),
         name="advect",
     )(mix, shift, frac, fields, west, east)
@@ -388,8 +450,9 @@
 
 def per_device(fields, frac, shift, mix, proj, mode_shift, cells, source, weight):
     fields = fields[0]
-    west = send(fields, "lon", 1)
-    east = send(pack_east(fields), "lon", -1)
+    west, east = pack(shift[0], fields)
+    west = send(west, "lon", 1)
+    east = send(east, "lon", -1)
     adv, rhs, half = advect(mix, shift[0], frac[0], fields, west, east)
     both = lax.all_gather(half, "panel")
     b, top, bottom = margin(rhs, both, cells[0], source[0, 0].T, weight[0, 0].T, proj)

time: 89.3 us -> 88.9 us (level)
  waiting for transfers between devices: 10.3 us -> 7.34 us
  blocking collectives: 51.8 us -> 54.6 us
  starting transfers between devices: 15.7 us -> 13.1 us
  Pallas kernels: 8.53 us -> 10.1 us
    ppermute x6, waiting for transfers between devices: 10.3 us -> 7.34 us  [send(): lax.ppermute(block, axis, [(i, i + by) for i in range(count) if 0 <= i +...]
    ppermute x6, starting transfers between devices: 15.7 us -> 13.1 us  [send(): lax.ppermute(block, axis, [(i, i + by) for i in range(count) if 0 <= i +...]
    all_to_all x1, blocking collectives: 26.7 us -> 28.6 us  [per_device(): sums = relay(lax.all_to_all(sums, 'lon', 0, 0), rest)]
    pallas_call x1, Pallas kernels: 0.45 us -> 1.65 us  [pack(): pl.pallas_call(pack_kernel, grid=(G,), in_specs=[pl.BlockSpec((ROWS, 32),...]
  transfers between devices with their start and end apart: 6 -> 6, of which waited for: 4 -> 3; matrix products, arithmetic and copies ran while one was open for 0% -> 0% of each run, Pallas kernels for 1% -> 0%
where the time goes in v3:
time: 88.9 us; the launch traced here: 88.4 us
  blocking collectives  54.6 us (61%)
  starting transfers between devices  13.1 us (15%)
  Pallas kernels  10.1 us (11%)
  waiting for transfers between devices  7.34 us (8%)
  local copies, waits for them, and re-layouts  2.48 us (3%)
    all_to_all x1, blocking collectives, per_device(): sums = relay(lax.all_to_all(sums, 'lon', 0, 0), rest)  28.6 us
    all_to_all x1, blocking collectives, per_device(): sums = lax.all_to_all(sums, ('panel', 'lat'), 0, 0)  18.9 us
    ppermute x6, starting transfers between devices, send(): lax.ppermute(block, axis, [(i, i + by) for i in range(count) if 0 <= i +...  13.1 us
    ppermute x6, waiting for transfers between devices, send(): lax.ppermute(block, axis, [(i, i + by) for i in range(count) if 0 <= i +...  7.34 us
    all_gather x1, blocking collectives, per_device(): both = lax.all_gather(half, 'panel')  7.09 us
    pallas_call x1, Pallas kernels, advect(): pl.pallas_call(advect_kernel, grid=(G,), in_specs=[pl.BlockSpec(memory_sp...  3.75 us
    unnamed x18, local copies, waits for them, and re-layouts  2.48 us
    pallas_call x1, Pallas kernels, images(): pl.pallas_call(images_kernel, out_shape=[full, full, full, jax.ShapeDtype...  2.23 us
  transfers between devices with their start and end apart: 6, of which 3 were waited for; matrix products, arithmetic and copies ran while one was open for 0% of the time, Pallas kernels for 0%

profile of v3, /device:TPU:1, one launch (start us, length us, event | category | flops | bytes accessed | tf_op | source)
XLA Modules:
  0.0 88.4 jit_solution(7774959168075702723)
XLA Ops:
  0.6 1.1 %copy-done = bf16[1,6,24,16,128]{4,3,2,1,0:T(8,128)(2,1)S(1)} copy-done((bf16[1,6,24,16,128]{4,3,2,1,0:T(8,128)(2,1)S(1)}, bf16[1,6,24,16,128]{4,3,2,1,0:T(8,128)(2,1)}, u32[]{:S(2)}) %copy-start) | copy-done | bytes 589848
  1.7 0.7 copy-done.2
  2.4 1.6 %pack.1 = (bf16[3,24,16,128]{3,2,1,0:T(8,128)(2,1)S(1)}, bf16[3,16,128]{2,1,0:T(8,128)(2,1)S(1)}) custom-call(s32[16,32]{1,0:T(8,128)S(1)} %bitcast.19, bf16[6,24,16,128]{3,2,1,0:T(8,128)(2,1)S(1)} %bitcast.15), custom_call_target="tpu_custom_call" | custom-call | tf_op jit(solution)/shard_map/pack/pallas_call | solution.py:89
  4.1 0.0 copy-start.4
  4.1 4.0 %collective-permute-start = (bf16[3,24,16,128]{3,2,1,0:T(8,128)(2,1)S(1)}, bf16[3,24,16,128]{3,2,1,0:T(8,128)(2,1)S(1)}, u32[]{:S(2)}, u32[]{:S(2)}) collective-permute-start(bf16[3,24,16,128]{3,2,1,0:T(8,128)(2,1)S(1)} %get-tuple-element.17), channel_id=1, source_target_pairs={{0,1},{1,2},{2,3},{3,4},{4,5},{5,6},{6,7},{7,8},{8,9},{9,10},{10,1... | collective-permute-start | bytes 884744 | tf_op jit(solution)/shard_map/ppermute | solution.py:433
  8.0 1.3 %collective-permute-start.1 = (bf16[3,16,128]{2,1,0:T(8,128)(2,1)S(1)}, bf16[3,16,128]{2,1,0:T(8,128)(2,1)S(1)}, u32[]{:S(2)}, u32[]{:S(2)}) collective-permute-start(bf16[3,16,128]{2,1,0:T(8,128)(2,1)S(1)} %get-tuple-element.18), channel_id=1, source_target_pairs={{1,0},{2,1},{3,2},{4,3},{5,4},{6,5},{7,6},{8,7},{9,8},{10,9},{11,1... | collective-permute-start | bytes 36872 | tf_op jit(solution)/shard_map/ppermute | solution.py:433
  9.3 3.1 %collective-permute-done.1.east_ref = bf16[3,16,128]{2,1,0:T(8,128)(2,1)S(1)} collective-permute-done((bf16[3,16,128]{2,1,0:T(8,128)(2,1)S(1)}, bf16[3,16,128]{2,1,0:T(8,128)(2,1)S(1)}, u32[]{:S(2)}, u32[]{:S(2)}) %collective-permute-start.1) | collective-permute-done | bytes 12320 | tf_op jit(solution)/shard_map/ppermute | solution.py:433
  12.5 3.8 %advect.1 = (bf16[6,24,16,128]{3,2,1,0:T(8,128)(2,1)}, f32[3,128,128]{2,1,0:T(8,128)S(1)}, bf16[3,128,128]{2,1,0:T(8,128)(2,1)S(1)}) custom-call(f32[6,24]{1,0:T(8,128)S(1)} %copy-done.4, s32[16,32]{1,0:T(8,128)S(1)} %bitcast.20, f32[24,16,128]{2,1,0:T(8,128)S(1)} %bitcast.18, bf16[6,24,16,128]{3,2,1,0:T(8,128)(2,1)S(1)} %bitcast.16, ...), custom_call_target="tpu_custom_call" | custom-call | tf_op jit(solution)/shard_map/advect/pallas_call | solution.py:183
  16.2 7.1 %all-gather = bf16[6,128,128]{2,1,0:T(8,128)(2,1)S(1)} all-gather(bf16[3,128,128]{2,1,0:T(8,128)(2,1)S(1)} %get-tuple-element.21), channel_id=2, replica_groups=mesh['panel'=2,'lat'=8,'lon'=32] {'panel'}, dimensions={0}, use_global_device_ids=true | all-gather | bytes 294912 | tf_op jit(solution)/shard_map/all_gather | solution.py:457
  23.3 0.7 copy-done.6
  24.0 0.0 copy-done.5
  24.0 0.0 copy-done.8
  24.0 1.3 %margin.1 = (f32[3,128,128]{2,1,0:T(8,128)S(1)}, f32[3,24,128]{2,1,0:T(8,128)S(1)}, f32[3,24,128]{2,1,0:T(8,128)S(1)}) custom-call(f32[3,128,128]{2,1,0:T(8,128)S(1)} %get-tuple-element.20.rhs_ref, bf16[2,3,128,128]{3,2,1,0:T(8,128)(2,1)S(1)} %bitcast.17, s32[1,256]{1,0:T(1,128)S(1)} %bitcast.25, s32[4,256]{1,0:T(4,128)S(1)} %bitcast.21, ...), custom_call_target="tpu_custom_call" | custom-call | tf_op jit(solution)/shard_map/margin/pallas_call | solution.py:258
  25.4 1.3 %collective-permute-start.2 = (f32[3,24,128]{2,1,0:T(8,128)S(1)}, f32[3,24,128]{2,1,0:T(8,128)S(1)}, u32[]{:S(2)}, u32[]{:S(2)}) collective-permute-start(f32[3,24,128]{2,1,0:T(8,128)S(1)} %get-tuple-element.23), channel_id=1, source_target_pairs={{0,32},{32,64},{64,96},{96,128},{128,160},{160,192},{192,224},{1,3... | collective-permute-start | bytes 110600 | tf_op jit(solution)/shard_map/ppermute | solution.py:433
  26.7 1.3 %collective-permute-start.3 = (f32[3,24,128]{2,1,0:T(8,128)S(1)}, f32[3,24,128]{2,1,0:T(8,128)S(1)}, u32[]{:S(2)}, u32[]{:S(2)}) collective-permute-start(f32[3,24,128]{2,1,0:T(8,128)S(1)} %get-tuple-element.24), channel_id=1, source_target_pairs={{32,0},{64,32},{96,64},{128,96},{160,128},{192,160},{224,192},{33,... | collective-permute-start | bytes 110600 | tf_op jit(solution)/shard_map/ppermute | solution.py:433
  28.0 3.4 %collective-permute-done.3.south_ref = f32[3,24,128]{2,1,0:T(8,128)S(1)} collective-permute-done((f32[3,24,128]{2,1,0:T(8,128)S(1)}, f32[3,24,128]{2,1,0:T(8,128)S(1)}, u32[]{:S(2)}, u32[]{:S(2)}) %collective-permute-start.3) | collective-permute-done | bytes 36896 | tf_op jit(solution)/shard_map/ppermute | solution.py:433
  31.4 0.1 pack_columns.1
  31.5 1.3 %collective-permute-start.5 = (f32[3,8,128]{2,1,0:T(8,128)S(1)}, f32[3,8,128]{2,1,0:T(8,128)S(1)}, u32[]{:S(2)}, u32[]{:S(2)}) collective-permute-start(f32[3,8,128]{2,1,0:T(8,128)S(1)} %pack_columns.1), channel_id=1, source_target_pairs={{1,0},{2,1},{3,2},{4,3},{5,4},{6,5},{7,6},{8,7},{9,8},{10,9},{11,1... | collective-permute-start | bytes 36872 | tf_op jit(solution)/shard_map/ppermute | solution.py:433
  32.8 4.0 %collective-permute-start.4 = (f32[3,8,128]{2,1,0:T(8,128)S(1)}, f32[3,8,128]{2,1,0:T(8,128)S(1)}, u32[]{:S(2)}, u32[]{:S(2)}) collective-permute-start(f32[3,8,128]{2,1,0:T(8,128)S(1)} %pack_columns.1), channel_id=1, source_target_pairs={{0,1},{1,2},{2,3},{3,4},{4,5},{5,6},{6,7},{7,8},{8,9},{9,10},{10,1... | collective-permute-start | bytes 36872 | tf_op jit(solution)/shard_map/ppermute | solution.py:433
  36.8 0.8 collective-permute-done.4.fwest_ref
  37.6 2.2 %images.1 = (f32[3,128,128]{2,1,0:T(8,128)S(1)}, f32[3,128,128]{2,1,0:T(8,128)S(1)}, f32[3,128,128]{2,1,0:T(8,128)S(1)}, f32[32,8,128]{2,1,0:T(8,128)S(1)}) custom-call(f32[1,24]{1,0:T(1,128)S(1)} %bitcast.23, f32[3,128,128]{2,1,0:T(8,128)S(1)} %get-tuple-element.22.b_ref, f32[3,24,128]{2,1,0:T(8,128)S(1)} %collective-permute-done.2.north_ref, ...), custom_call_target="tpu_custom_call" | custom-call | tf_op jit(solution)/shard_map/images/pallas_call | solution.py:370
  39.8 28.6 %all_to_all.10.in_ref = f32[32,8,128]{2,1,0:T(8,128)S(1)} all-to-all(f32[32,8,128]{2,1,0:T(8,128)S(1)} %get-tuple-element.25), channel_id=1, replica_groups=mesh['panel'=2,'lat'=8,'lon'=32] {'lon'}, dimensions={0} | all-to-all | bytes 262144 | tf_op jit(solution)/shard_map/all_to_all | solution.py:468
  68.5 18.9 %all_to_all.11.s_ref = f32[16,8,128]{2,1,0:T(8,128)S(1)} all-to-all(f32[16,8,128]{2,1,0:T(8,128)S(1)} %relay.1), channel_id=1, replica_groups=mesh['panel'=2,'lat'=8,'lon'=32] {'panel','lat'}, dimensions={0} | all-to-all | bytes 131072 | tf_op jit(solution)/shard_map/all_to_all | solution.py:469
  87.4 1.0 %iterate.1 = (f32[384,128]{1,0:T(8,128)}, f32[384,128]{1,0:T(8,128)}) custom-call(f32[1,24]{1,0:T(1,128)S(1)} %bitcast.24, f32[16,8,128]{2,1,0:T(8,128)S(1)} %all_to_all.11.s_ref, f32[3,128,128]{2,1,0:T(8,128)S(1)} %get-tuple-element.22.b_ref, f32[3,128,128]{2,1,0:T(8,128)S(1)} %get-tuple-element.26.c_ref, f32[3,128,128]{2,1,0:T(8,128)S(1)} %get-tuple-element.27.u1_ref, ...), custom_call_target="tpu_custom_call" | custom-call | tf_op jit(solution)/shard_map/iterate/pallas_call | solution.py:423
  (16 shorter events, 0.0 us)
Async XLA Ops:
  0.6 1.1 %copy-start = (bf16[1,6,24,16,128]{4,3,2,1,0:T(8,128)(2,1)S(1)}, bf16[1,6,24,16,128]{4,3,2,1,0:T(8,128)(2,1)}, u32[]{:S(2)}) copy-start(bf16[1,6,24,16,128]{4,3,2,1,0:T(8,128)(2,1)} %param.9) | copy-start | bytes 1769476
  1.7 0.7 copy-start.2
  2.4 10.1 %copy-start.1 = (f32[1,24,16,128]{3,2,1,0:T(8,128)S(1)}, f32[1,24,16,128]{3,2,1,0:T(8,128)}, u32[]{:S(2)}) copy-start(f32[1,24,16,128]{3,2,1,0:T(8,128)} %param.10) | copy-start | bytes 589828
  4.1 8.4 %copy-start.4 = (f32[6,24]{1,0:T(8,128)S(1)}, f32[6,24]{1,0:T(8,128)}, u32[]{:S(2)}) copy-start(f32[6,24]{1,0:T(8,128)} %mix_ref.1) | copy-start | bytes 1732
  4.1 8.4 %collective-permute-start = (bf16[3,24,16,128]{3,2,1,0:T(8,128)(2,1)S(1)}, bf16[3,24,16,128]{3,2,1,0:T(8,128)(2,1)S(1)}, u32[]{:S(2)}, u32[]{:S(2)}) collective-permute-start(bf16[3,24,16,128]{3,2,1,0:T(8,128)(2,1)S(1)} %get-tuple-element.17), channel_id=1, source_target_pairs={{0,1},{1,2},{2,3},{3,4},{4,5},{5,6},{6,7},{7,8},{8,9},{9,10},{10,1... | collective-permute-start | bytes 884744 | tf_op jit(solution)/shard_map/ppermute | solution.py:433
  8.0 4.4 %collective-permute-start.1 = (bf16[3,16,128]{2,1,0:T(8,128)(2,1)S(1)}, bf16[3,16,128]{2,1,0:T(8,128)(2,1)S(1)}, u32[]{:S(2)}, u32[]{:S(2)}) collective-permute-start(bf16[3,16,128]{2,1,0:T(8,128)(2,1)S(1)} %get-tuple-element.18), channel_id=1, source_target_pairs={{1,0},{2,1},{3,2},{4,3},{5,4},{6,5},{7,6},{8,7},{9,8},{10,9},{11,1... | collective-permute-start | bytes 36872 | tf_op jit(solution)/shard_map/ppermute | solution.py:433
  16.2 7.1 %copy-start.3 = (f32[24,24]{1,0:T(8,128)S(1)}, f32[24,24]{1,0:T(8,128)}, u32[]{:S(2)}) copy-start(f32[24,24]{1,0:T(8,128)} %proj_ref.1) | copy-start | bytes 6916
  23.3 0.7 copy-start.6
  23.3 0.7 copy-start.5
  23.3 0.7 copy-start.8
  25.4 2.6 %collective-permute-start.2 = (f32[3,24,128]{2,1,0:T(8,128)S(1)}, f32[3,24,128]{2,1,0:T(8,128)S(1)}, u32[]{:S(2)}, u32[]{:S(2)}) collective-permute-start(f32[3,24,128]{2,1,0:T(8,128)S(1)} %get-tuple-element.23), channel_id=1, source_target_pairs={{0,32},{32,64},{64,96},{96,128},{128,160},{160,192},{192,224},{1,3... | collective-permute-start | bytes 110600 | tf_op jit(solution)/shard_map/ppermute | solution.py:433
  26.7 4.7 %collective-permute-start.3 = (f32[3,24,128]{2,1,0:T(8,128)S(1)}, f32[3,24,128]{2,1,0:T(8,128)S(1)}, u32[]{:S(2)}, u32[]{:S(2)}) collective-permute-start(f32[3,24,128]{2,1,0:T(8,128)S(1)} %get-tuple-element.24), channel_id=1, source_target_pairs={{32,0},{64,32},{96,64},{128,96},{160,128},{192,160},{224,192},{33,... | collective-permute-start | bytes 110600 | tf_op jit(solution)/shard_map/ppermute | solution.py:433
  31.5 6.1 %copy-start.7 = (f32[24]{0:T(128)S(1)}, f32[24]{0:T(128)}, u32[]{:S(2)}) copy-start(f32[24]{0:T(128)} %param.14) | copy-start | bytes 292
  31.5 5.3 %collective-permute-start.5 = (f32[3,8,128]{2,1,0:T(8,128)S(1)}, f32[3,8,128]{2,1,0:T(8,128)S(1)}, u32[]{:S(2)}, u32[]{:S(2)}) collective-permute-start(f32[3,8,128]{2,1,0:T(8,128)S(1)} %pack_columns.1), channel_id=1, source_target_pairs={{1,0},{2,1},{3,2},{4,3},{5,4},{6,5},{7,6},{8,7},{9,8},{10,9},{11,1... | collective-permute-start | bytes 36872 | tf_op jit(solution)/shard_map/ppermute | solution.py:433
  32.8 4.8 %collective-permute-start.4 = (f32[3,8,128]{2,1,0:T(8,128)S(1)}, f32[3,8,128]{2,1,0:T(8,128)S(1)}, u32[]{:S(2)}, u32[]{:S(2)}) collective-permute-start(f32[3,8,128]{2,1,0:T(8,128)S(1)} %pack_columns.1), channel_id=1, source_target_pairs={{0,1},{1,2},{2,3},{3,4},{4,5},{5,6},{6,7},{7,8},{8,9},{9,10},{10,1... | collective-permute-start | bytes 36872 | tf_op jit(solution)/shard_map/ppermute | solution.py:433

commit v4 on v3

--- a/solution.py
+++ b/solution.py
@@ -51,7 +51,30 @@
     return (target >= 32) & (source == jnp.where((target >> 5) == 2, target, (target + 64) & (COLS - 1)))
 
 
-def pack_kernel(shift_ref, fields_ref, west_ref, east_ref, scratch):
+def pack_east_kernel(fields_ref, out_ref):
+    lane = lane_iota((ROWS, COLS))
+    acc = jnp.zeros((ROWS, COLS), F32)
+    for f in range(NF):
+        for l8 in range(8):
+            i = f * 8 + l8
+            x = roll_lanes(fields_ref[f, l8].astype(F32), 2 * i)
+            acc = jnp.where((lane >> 1) == i, x, acc)
+    out_ref[0] = acc.astype(BF16)
+
+
+def pack_east(fields):
+    return pl.pallas_call(
+        pack_east_kernel,
+        grid=(G,),
+        in_specs=[pl.BlockSpec((NF, 8, ROWS, COLS), lambda g: (0, g, 0, 0))],
+        out_specs=pl.BlockSpec((1, ROWS, COLS), lambda g: (g, 0, 0)),
+        out_shape=jax.ShapeDtypeStruct((G, ROWS, COLS), BF16),
+        compiler_params=params(),
+        name="pack_east",
+    )(fields)
+
+
+def pack_kernel(shift_ref, fields_ref, west_ref, scratch):
     shift = own_shift(shift_ref, lax.axis_index("lon") + 1)
     lane = lane_iota((ROWS, COLS))
     low = (lax.broadcasted_iota(jnp.int32, (ROWS, COLS), 0) & 1) == 0
@@ -68,7 +91,6 @@
         axis=0,
     )
     zero = jnp.zeros((ROWS, COLS), BF16)
-    acc = jnp.zeros((ROWS, COLS), F32)
     for l8 in range(8):
         parts = [
             jnp.concatenate([jnp.where(m, fields_ref[f, l8], zero) for m in masks], axis=1) for f in range(NF)
@@ -78,11 +100,6 @@
         pairs = pairs.astype(BF16)
         for n in range(NF // 2):
             west_ref[n, l8] = pairs[ROWS * n : ROWS * n + ROWS]
-        for f in range(NF):
-            i = f * 8 + l8
-            x = roll_lanes(fields_ref[f, l8].astype(F32), 2 * i)
-            acc = jnp.where((lane >> 1) == i, x, acc)
-    east_ref[0] = acc.astype(BF16)
 
 
 def pack(shift, fields):
@@ -93,14 +110,8 @@
             pl.BlockSpec((ROWS, 32), lambda g: (0, 0)),
             pl.BlockSpec((NF, 8, ROWS, COLS), lambda g: (0, g, 0, 0)),
         ],
-        out_specs=[
-            pl.BlockSpec((NF // 2, 8, ROWS, COLS), lambda g: (0, g, 0, 0)),
-            pl.BlockSpec((1, ROWS, COLS), lambda g: (g, 0, 0)),
-        ],
-        out_shape=[
-            jax.ShapeDtypeStruct((NF // 2, LEV, ROWS, COLS), BF16),
-            jax.ShapeDtypeStruct((G, ROWS, COLS), BF16),
-        ],
+        out_specs=pl.BlockSpec((NF // 2, 8, ROWS, COLS), lambda g: (0, g, 0, 0)),
+        out_shape=jax.ShapeDtypeStruct((NF // 2, LEV, ROWS, COLS), BF16),
         scratch_shapes=[pltpu.VMEM((8, NF * ROWS, COLS), F32)],
         compiler_params=params(),
         name="pack",
@@ -203,6 +214,13 @@
     )(mix, shift, frac, fields, west, east)
 
 
+SLOTS = 20
+
+
+def slot_of_lane():
+    return ((lane_iota((8, COLS)) + 3) & (COLS - 1)) // 6
+
+
 def split3(x):
     a = x.astype(BF16)
     rest = x - a.astype(F32)
@@ -211,21 +229,54 @@
     return a, b, c
 
 
-def margin_kernel(rhs_ref, both_ref, cells_ref, source_ref, weight_ref, proj_ref, b_ref, top_ref, bottom_ref):
-    other = 1 - lax.axis_index("panel")
+def tables_kernel(
+    cells_ref, source_ref, weight_ref, proj_ref, pick_ref, place_ref, in_row_ref, covered_ref, src_row_ref, wgt_ref, proj_out_ref
+):
+    proj_out_ref[...] = proj_ref[...]
     src = jnp.concatenate([source_ref[q : q + 1, :] for q in range(4)], axis=1)
     wgt = jnp.concatenate([weight_ref[q : q + 1, :] for q in range(4)], axis=1)
-    src_col = jnp.broadcast_to(src & 127, (128, 4 * OV))
-    pick = jnp.where(lax.broadcasted_iota(jnp.int32, (128, 4 * OV), 0) == src_col, 1.0, 0.0).astype(BF16)
-    src_row = jnp.broadcast_to(src >> 7, (8, 4 * OV))
-    wgt = jnp.broadcast_to(wgt, (8, 4 * OV))
+    wide = (COLS, 4 * OV)
+    col = jnp.broadcast_to(src & (COLS - 1), wide)
+    pick_ref[...] = jnp.where(lax.broadcasted_iota(jnp.int32, wide, 0) == col, 1.0, 0.0).astype(BF16)
+    src_row_ref[...] = jnp.broadcast_to(src >> 7, (8, 4 * OV))
+    wgt_ref[...] = jnp.broadcast_to(wgt, (8, 4 * OV))
     cells = cells_ref[...]
-    cell_col = jnp.broadcast_to(cells & 127, (128, OV))
-    place = jnp.where(lax.broadcasted_iota(jnp.int32, (128, OV), 0) == cell_col, 1.0, 0.0).astype(BF16)
-    cell_row = jnp.broadcast_to(cells >> 7, (128, OV))
-    in_row = (lax.broadcasted_iota(jnp.int32, (128, OV), 0) >> 3) == cell_row
+    sub = lax.broadcasted_iota(jnp.int32, (128, OV), 0)
+    place = jnp.where(sub == jnp.broadcast_to(cells & (COLS - 1), (128, OV)), 1.0, 0.0).astype(BF16)
+    place_ref[...] = place
+    in_row = jnp.where((sub >> 3) == jnp.broadcast_to(cells >> 7, (128, OV)), 1.0, 0.0).astype(BF16)
+    in_row_ref[...] = in_row
     nt = (((1,), (1,)), ((), ()))
-    covered = lax.dot_general(jnp.where(in_row, 1.0, 0.0).astype(BF16), place, nt, preferred_element_type=F32) > 0.5
+    covered_ref[...] = lax.dot_general(in_row, place, nt, preferred_element_type=F32)
+
+
+def tables(cells, source, weight, proj):
+    return pl.pallas_call(
+        tables_kernel,
+        out_shape=[
+            jax.ShapeDtypeStruct((COLS, 4 * OV), BF16),
+            jax.ShapeDtypeStruct((128, OV), BF16),
+            jax.ShapeDtypeStruct((128, OV), BF16),
+            jax.ShapeDtypeStruct((128, COLS), F32),
+            jax.ShapeDtypeStruct((8, 4 * OV), jnp.int32),
+            jax.ShapeDtypeStruct((8, 4 * OV), F32),
+            jax.ShapeDtypeStruct((LEV, LEV), F32),
+        ],
+        compiler_params=params(),
+        cost_estimate=pl.CostEstimate(flops=4_000_000, bytes_accessed=500_000, transcendentals=0),
+        name="tables",
+    )(cells, source, weight, proj)
+
+
+def margin_kernel(
+    rhs_ref, both_ref, pick_ref, place_ref, in_row_ref, covered_ref, src_row_ref, wgt_ref, proj_ref, b_ref, slots_ref
+):
+    other = 1 - lax.axis_index("panel")
+    pick, place = pick_ref[...], place_ref[...]
+    src_row, wgt = src_row_ref[...], wgt_ref[...]
+    in_row = in_row_ref[...].astype(F32)
+    covered = covered_ref[...] > 0.5
+    nt = (((1,), (1,)), ((), ()))
     joined = []
     for lb in range(G):
         cols = jnp.dot(both_ref[other, lb], pick, preferred_element_type=F32)
@@ -233,7 +284,7 @@
         for r in range(ROWS):
             rep = rep + jnp.where(src_row == r, wgt, 0.0) * cols[8 * r : 8 * r + 8, :]
         rep = rep[:, :OV] + rep[:, OV : 2 * OV] + rep[:, 2 * OV : 3 * OV] + rep[:, 3 * OV :]
-        spread = jnp.where(in_row, jnp.concatenate([rep] * ROWS, axis=0), 0.0)
+        spread = in_row * jnp.concatenate([rep] * ROWS, axis=0)
         values = None
         for part in split3(spread):
             value = lax.dot_general(part, place, nt, preferred_element_type=F32)
@@ -247,53 +298,57 @@
         for r in range(ROWS):
             tile = modal[8 * lb : 8 * lb + 8, COLS * r : COLS * r + COLS]
             b_ref[lb, 8 * r : 8 * r + 8, :] = tile
-            if r < 3:
-                top_ref[lb, 8 * r : 8 * r + 8, :] = tile
-            if r >= ROWS - 3:
-                s = r - (ROWS - 3)
-                bottom_ref[lb, 8 * s : 8 * s + 8, :] = tile
-
-
-def margin(rhs, both, cells, source, weight, proj):
+    lat, lon = lax.axis_index("lat"), lax.axis_index("lon")
+    place_in_square = 2 * (lat & 1) + (lon & 1)
+    for lb in range(G):
+        slots_ref[place_in_square ^ 2, lb] = b_ref[lb, pl.ds(pl.multiple_of(8 * 13 * (1 - (lat & 1)), 8), 24), :]
+        acc = jnp.zeros((8, COLS), F32)
+        for i in range(SLOTS):
+            r = (i - 2) % ROWS
+            acc = jnp.where(slot_of_lane() == i, roll_lanes(b_ref[lb, 8 * r : 8 * r + 8, :], 6 * i), acc)
+        slots_ref[place_in_square ^ 1, lb, 0:8, :] = acc
+        slots_ref[place_in_square ^ 3, lb, 0:8, :] = acc
+
+
+def margin(rhs, both, lists):
     return pl.pallas_call(
         margin_kernel,
         out_shape=[
             jax.ShapeDtypeStruct((G, 128, COLS), F32),
-            jax.ShapeDtypeStruct((G, 24, COLS), F32),
-            jax.ShapeDtypeStruct((G, 24, COLS), F32),
+            jax.ShapeDtypeStruct((4, G, 24, COLS), F32),
         ],
         compiler_params=params(),
         name="margin",
-    )(rhs, both, cells, source, weight, proj)
-
-
-def pack_columns_kernel(b_ref, north_ref, south_ref, out_ref):
-    lane = lane_iota((8, COLS))
+    )(rhs, both, *lists)
+
+
+def second_kernel(b_ref, first_ref, got_ref, out_ref):
+    lat, lon = lax.axis_index("lat"), lax.axis_index("lon")
+    here = 2 * (lat & 1) + (lon & 1)
+    there = 3 - here
+    even = jnp.broadcast_to(lat & 1, (8, COLS)) == 0
+    slot = slot_of_lane()
     for lb in range(G):
-        acc = jnp.zeros((8, COLS), F32)
-        for i in range(20):
-            j = i - 2
-            if j < 0:
-                row = north_ref[lb, 8 * (j + 3) : 8 * (j + 3) + 8, :]
-            elif j >= ROWS:
-                row = south_ref[lb, 8 * (j - ROWS) : 8 * (j - ROWS) + 8, :]
-            else:
-                row = b_ref[lb, 8 * j : 8 * j + 8, :]
-            here = ((lane - 6 * i + 3) & 127) < 6
-            acc = jnp.where(here, roll_lanes(row, 6 * i), acc)
-        out_ref[lb] = acc
-
-
-def pack_columns(b, north, south):
-    return pl.pallas_call(
-        pack_columns_kernel,
-        out_shape=jax.ShapeDtypeStruct((G, 8, COLS), F32),
-        compiler_params=params(),
-        name="pack_columns",
-    )(b, north, south)
-
-
-def images_kernel(shift_ref, b_ref, north_ref, south_ref, fwest_ref, feast_ref, c_ref, u1_ref, u2_ref, s_ref):
+        out_ref[there ^ 2, lb, 0:24, :] = b_ref[lb, pl.ds(pl.multiple_of(8 * 13 * (lat & 1), 8), 24), :]
+        out_ref[there ^ 2, lb, 24:32, :] = got_ref[here ^ 1, lb, 0:8, :]
+        own = first_ref[here ^ 1, lb, 0:8, :]
+        out_ref[there ^ 3, lb, 24:32, :] = own
+        row = [got_ref[here ^ 2, lb, 8 * n : 8 * n + 8, :] for n in range(3)]
+        with_south = jnp.where(slot == 18, roll_lanes(row[0], 6 * 18), jnp.where(slot == 19, roll_lanes(row[1], 6 * 19), own))
+        with_north = jnp.where(slot == 0, row[1], jnp.where(slot == 1, roll_lanes(row[2], 6), own))
+        out_ref[there ^ 1, lb, 24:32, :] = jnp.where(even, with_south, with_north)
+
+
+def second(b, first, got):
+    return pl.pallas_call(
+        second_kernel,
+        out_shape=jax.ShapeDtypeStruct((4, G, 32, COLS), F32),
+        compiler_params=params(),
+        name="second",
+    )(b, first, got)
+
+
+def images_kernel(shift_ref, b_ref, first_ref, second_ref, c_ref, u1_ref, u2_ref, s_ref):
     lat, lon = lax.axis_index("lat"), lax.axis_index("lon")
     one = jnp.float32(1.0)
     zero = jnp.float32(0.0)
@@ -304,7 +359,17 @@
     lane = lane_iota((8, COLS))
     first, last = lane == 0, lane == COLS - 1
     side = jnp.where(lane < 64, has_e, has_w)
+    here = 2 * (lat & 1) + (lon & 1)
+    there = 3 - here
+    lat_even = jnp.broadcast_to(lat & 1, (8, COLS)) == 0
+    slot = slot_of_lane()
     from_east = ((lane % 6) < 3) & (lane < 120)
+    north_slot, south_slot = slot < 2, (slot == 18) | (slot == 19)
+    inside = jnp.where(from_east, has_e, has_w)
+    inside = jnp.where(north_slot, inside * has_n, jnp.where(south_slot, inside * has_s, inside)) > 0.5
+    first_side = (lat_even & south_slot) | (~lat_even & north_slot)
+    second_side = (lat_even & north_slot) | (~lat_even & south_slot)
+    east_first = jnp.where(from_east, 1, 0) == jnp.broadcast_to(1 - (lon & 1), (8, COLS))
 
     def line(main, ext):
         return roll_lanes(jnp.where(last, ext, main), 1) + roll_lanes(jnp.where(first, ext, main), -1)
@@ -317,14 +382,20 @@
         diag = lane_iota((8, LEV)) == (lax.broadcasted_iota(jnp.int32, (8, LEV), 0) + 8 * lb)
         a = 4.0 + jnp.sum(jnp.where(diag, jnp.broadcast_to(shift_ref[...], (8, LEV)), 0.0), axis=1, keepdims=True)
         a = jnp.broadcast_to(a, (8, COLS))
-        packed = jnp.where(from_east, feast_ref[lb], fwest_ref[lb])
+        near = jnp.where(first_side, first_ref[here ^ 3, lb, 0:8, :], first_ref[here ^ 1, lb, 0:8, :])
+        near = jnp.where(second_side, second_ref[there ^ 2, lb, 24:32, :], near)
+        far = jnp.where(second_side, second_ref[there ^ 3, lb, 24:32, :], second_ref[there ^ 1, lb, 24:32, :])
+        packed = jnp.where(inside, jnp.where(east_first, near, far), 0.0)
 
         def b_main(j):
+            if 0 <= j < ROWS:
+                return b_ref[lb, 8 * j : 8 * j + 8, :]
+            n = j + 3 if j < 0 else j - ROWS
+            rows = slice(8 * n, 8 * n + 8)
+            one, two = first_ref[here ^ 2, lb, rows, :], second_ref[there ^ 2, lb, rows, :]
             if j < 0:
-                return north_ref[lb, 8 * (j + 3) : 8 * (j + 3) + 8, :]
-            if j >= ROWS:
-                return south_ref[lb, 8 * (j - ROWS) : 8 * (j - ROWS) + 8, :]
-            return b_ref[lb, 8 * j : 8 * j + 8, :]
+                return jnp.where(has_n > 0.5, jnp.where(lat_even, two, one), 0.0)
+            return jnp.where(has_s > 0.5, jnp.where(lat_even, one, two), 0.0)
 
         bm = {j: b_main(j) for j in (-3, -2)}
         bx = {-2: packed}
@@ -361,18 +432,23 @@
         for q in range(8):
             total = jnp.sum(sums[q], axis=1, keepdims=True)
             sums_out = jnp.where(lane == 8 * lb + q, total, sums_out)
+    sub = lax.broadcasted_iota(jnp.int32, (8, COLS), 0)
+    spread = jnp.zeros((8, COLS), F32)
+    for m in range(4):
+        spread = jnp.where((sub & 3) == m, roll_lanes(sums_out, 32 * m), spread)
+    folded = jnp.concatenate([jnp.sum(spread[4 * h : 4 * h + 4], axis=0, keepdims=True) for h in range(2)], axis=0)
     for n in range(s_ref.shape[0]):
-        s_ref[n] = sums_out
-
-
-def images(mode_shift, b, north, south, from_west, from_east, copies):
+        s_ref[n] = folded
+
+
+def images(mode_shift, b, got_first, got_second, copies):
     full = jax.ShapeDtypeStruct((G, 128, COLS), F32)
     return pl.pallas_call(
         images_kernel,
-        out_shape=[full, full, full, jax.ShapeDtypeStruct((copies, 8, COLS), F32)],
+        out_shape=[full, full, full, jax.ShapeDtypeStruct((copies, 2, COLS), F32)],
         compiler_params=params(),
         name="images",
-    )(mode_shift, b, north, south, from_west, from_east)
+    )(mode_shift, b, got_first, got_second)
 
 
 def sum_copies(ref):
@@ -384,7 +460,12 @@
 
 def iterate_kernel(shift_ref, s_ref, b_ref, c_ref, u1_ref, u2_ref, sol_ref, res_ref):
     lane = lane_iota((8, COLS))
-    sums = sum_copies(s_ref)
+    total = sum_copies(s_ref)
+    sub = lax.broadcasted_iota(jnp.int32, (8, COLS), 0)
+    rows = jnp.where(sub < 4, jnp.broadcast_to(total[0:1], (8, COLS)), jnp.broadcast_to(total[1:2], (8, COLS)))
+    sums = rows
+    for m in range(1, 4):
+        sums = jnp.where((sub & 3) == m, roll_lanes(rows, -32 * m), sums)
     for lb in range(G):
         diag = lane_iota((8, LEV)) == (lax.broadcasted_iota(jnp.int32, (8, LEV), 0) + 8 * lb)
         a = 4.0 + jnp.sum(jnp.where(diag, jnp.broadcast_to(shift_ref[...], (8, LEV)), 0.0), axis=1, keepdims=True)
@@ -442,29 +523,36 @@
 def relay(parts, copies):
     return pl.pallas_call(
         relay_kernel,
-        out_shape=jax.ShapeDtypeStruct((copies, 8, COLS), F32),
+        out_shape=jax.ShapeDtypeStruct((copies, 2, COLS), F32),
         compiler_params=params(),
         name="relay",
     )(parts)
 
 
+def in_squares(slots, begin):
+    lats, lons = lax.axis_size("lat"), lax.axis_size("lon")
+    groups = [
+        [((i + a) % lats) * lons + (j + b) % lons for a in (0, 1) for b in (0, 1)]
+        for i in range(begin, lats, 2)
+        for j in range(begin, lons, 2)
+    ]
+    return lax.all_to_all(slots, ("lat", "lon"), 0, 0, axis_index_groups=groups)
+
+
 def per_device(fields, frac, shift, mix, proj, mode_shift, cells, source, weight):
     fields = fields[0]
-    west, east = pack(shift[0], fields)
-    west = send(west, "lon", 1)
-    east = send(east, "lon", -1)
+    lists = tables(cells[0], source[0, 0].T, weight[0, 0].T, proj)
+    east = send(pack_east(fields), "lon", -1)
+    west = send(pack(shift[0], fields), "lon", 1)
     adv, rhs, half = advect(mix, shift[0], frac[0], fields, west, east)
     both = lax.all_gather(half, "panel")
-    b, top, bottom = margin(rhs, both, cells[0], source[0, 0].T, weight[0, 0].T, proj)
-    north = send(bottom, "lat", 1)
-    south = send(top, "lat", -1)
-    columns = pack_columns(b, north, south)
-    from_west = send(columns, "lon", 1)
-    from_east = send(columns, "lon", -1)
+    b, first = margin(rhs, both, lists)
+    got_first = in_squares(first, 0)
+    got_second = in_squares(second(b, first, got_first), 1)
     shifts = mode_shift.reshape(1, LEV)
     count = lax.axis_size("lon")
     rest = lax.axis_size("panel") * lax.axis_size("lat")
-    c, u1, u2, sums = images(shifts, b, north, south, from_west, from_east, count)
+    c, u1, u2, sums = images(shifts, b, got_first, got_second, count)
     sums = relay(lax.all_to_all(sums, "lon", 0, 0), rest)
     sums = lax.all_to_all(sums, ("panel", "lat"), 0, 0)
     sol, res = iterate(shifts, sums, b, c, u1, u2)

time: 88.9 us -> 87.1 us (0.980)
  blocking collectives: 54.6 us -> 64.5 us
  starting transfers between devices: 13.1 us -> 5.39 us
  waiting for transfers between devices: 7.34 us -> 2.27 us
    all_to_all x0 -> x2, blocking collectives: none -> 23.1 us  [in_squares(): return lax.all_to_all(slots, ('lat', 'lon'), 0, 0, axis_index_groups=groups)]
    all_to_all x1, blocking collectives: 28.6 us -> 17.1 us  [per_device(): sums = relay(lax.all_to_all(sums, 'lon', 0, 0), rest)]
    ppermute x6 -> x2, starting transfers between devices: 13.1 us -> 5.39 us  [send(): lax.ppermute(block, axis, [(i, i + by) for i in range(count) if 0 <= i +...]
    ppermute x6 -> x2, waiting for transfers between devices: 7.34 us -> 2.27 us  [send(): lax.ppermute(block, axis, [(i, i + by) for i in range(count) if 0 <= i +...]
    all_to_all x1, blocking collectives: 18.9 us -> 17.3 us  [per_device(): sums = lax.all_to_all(sums, ('panel', 'lat'), 0, 0)]
    unnamed x18 -> x22, local copies, waits for them, and re-layouts: 2.48 us -> 3.09 us
  transfers between devices with their start and end apart: 6 -> 2, of which waited for: 3 -> 1; matrix products, arithmetic and copies ran while one was open for 0% -> 0% of each run, Pallas kernels for 0% -> 1%
where the time goes in v4:
time: 87.1 us; the launch traced here: 86.7 us
  blocking collectives  64.5 us (74%)
  Pallas kernels  10.7 us (12%)
  starting transfers between devices  5.39 us (6%)
  local copies, waits for them, and re-layouts  3.09 us (4%)
  waiting for transfers between devices  2.27 us (3%)
    all_to_all x2, blocking collectives, in_squares(): return lax.all_to_all(slots, ('lat', 'lon'), 0, 0, axis_index_groups=groups)  23.1 us
    all_to_all x1, blocking collectives, per_device(): sums = lax.all_to_all(sums, ('panel', 'lat'), 0, 0)  17.3 us
    all_to_all x1, blocking collectives, per_device(): sums = relay(lax.all_to_all(sums, 'lon', 0, 0), rest)  17.1 us
    all_gather x1, blocking collectives, per_device(): both = lax.all_gather(half, 'panel')  6.95 us
    ppermute x2, starting transfers between devices, send(): lax.ppermute(block, axis, [(i, i + by) for i in range(count) if 0 <= i +...  5.39 us
    pallas_call x1, Pallas kernels, advect(): pl.pallas_call(advect_kernel, grid=(G,), in_specs=[pl.BlockSpec(memory_sp...  3.76 us
    unnamed x22, local copies, waits for them, and re-layouts  3.09 us
    ppermute x2, waiting for transfers between devices, send(): lax.ppermute(block, axis, [(i, i + by) for i in range(count) if 0 <= i +...  2.27 us
  transfers between devices with their start and end apart: 2, of which 1 were waited for; matrix products, arithmetic and copies ran while one was open for 0% of the time, Pallas kernels for 1%

profile of v4, /device:TPU:1, one launch (start us, length us, event | category | flops | bytes accessed | tf_op | source)
XLA Modules:
  0.0 86.7 jit_solution(2493632425937623496)
XLA Ops:
  0.6 1.1 %copy-done = bf16[1,6,24,16,128]{4,3,2,1,0:T(8,128)(2,1)S(1)} copy-done((bf16[1,6,24,16,128]{4,3,2,1,0:T(8,128)(2,1)S(1)}, bf16[1,6,24,16,128]{4,3,2,1,0:T(8,128)(2,1)}, u32[]{:S(2)}) %copy-start) | copy-done | bytes 589848
  1.7 0.7 copy-done.3
  2.4 1.6 %pack.1 = bf16[3,24,16,128]{3,2,1,0:T(8,128)(2,1)S(1)} custom-call(s32[16,32]{1,0:T(8,128)S(1)} %bitcast.20, bf16[6,24,16,128]{3,2,1,0:T(8,128)(2,1)S(1)} %bitcast.15), custom_call_target="tpu_custom_call" | custom-call | tf_op jit(solution)/shard_map/pack/pallas_call | solution.py:106
  4.1 0.0 copy-start.2
  4.1 4.1 %collective-permute-start = (bf16[3,24,16,128]{3,2,1,0:T(8,128)(2,1)S(1)}, bf16[3,24,16,128]{3,2,1,0:T(8,128)(2,1)S(1)}, u32[]{:S(2)}, u32[]{:S(2)}) collective-permute-start(bf16[3,24,16,128]{3,2,1,0:T(8,128)(2,1)S(1)} %pack.1), channel_id=1, source_target_pairs={{0,1},{1,2},{2,3},{3,4},{4,5},{5,6},{6,7},{7,8},{8,9},{9,10},{10,1... | collective-permute-start | bytes 884744 | tf_op jit(solution)/shard_map/ppermute | solution.py:514
  8.2 0.0 copy-start.5
  8.2 0.0 copy-start.8
  8.2 0.5 pack_east.1
  8.7 0.0 copy-start.7
  8.7 1.3 %collective-permute-start.1 = (bf16[3,16,128]{2,1,0:T(8,128)(2,1)S(1)}, bf16[3,16,128]{2,1,0:T(8,128)(2,1)S(1)}, u32[]{:S(2)}, u32[]{:S(2)}) collective-permute-start(bf16[3,16,128]{2,1,0:T(8,128)(2,1)S(1)} %pack_east.1), channel_id=1, source_target_pairs={{1,0},{2,1},{3,2},{4,3},{5,4},{6,5},{7,6},{8,7},{9,8},{10,9},{11,1... | collective-permute-start | bytes 36872 | tf_op jit(solution)/shard_map/ppermute | solution.py:514
  10.0 0.6 copy-done.10
  10.7 0.2 tables.1
  10.9 2.3 %collective-permute-done.1.east_ref = bf16[3,16,128]{2,1,0:T(8,128)(2,1)S(1)} collective-permute-done((bf16[3,16,128]{2,1,0:T(8,128)(2,1)S(1)}, bf16[3,16,128]{2,1,0:T(8,128)(2,1)S(1)}, u32[]{:S(2)}, u32[]{:S(2)}) %collective-permute-start.1) | collective-permute-done | bytes 12320 | tf_op jit(solution)/shard_map/ppermute | solution.py:514
  13.1 3.8 %advect.1 = (bf16[6,24,16,128]{3,2,1,0:T(8,128)(2,1)}, f32[3,128,128]{2,1,0:T(8,128)S(1)}, bf16[3,128,128]{2,1,0:T(8,128)(2,1)S(1)}) custom-call(f32[6,24]{1,0:T(8,128)S(1)} %copy-done.6, s32[16,32]{1,0:T(8,128)S(1)} %bitcast.21, f32[24,16,128]{2,1,0:T(8,128)S(1)} %bitcast.19, bf16[6,24,16,128]{3,2,1,0:T(8,128)(2,1)S(1)} %bitcast.17, ...), custom_call_target="tpu_custom_call" | custom-call | tf_op jit(solution)/shard_map/advect/pallas_call | solution.py:194
  16.9 7.0 %all-gather = bf16[6,128,128]{2,1,0:T(8,128)(2,1)S(1)} all-gather(bf16[3,128,128]{2,1,0:T(8,128)(2,1)S(1)} %get-tuple-element.23), channel_id=2, replica_groups=mesh['panel'=2,'lat'=8,'lon'=32] {'panel'}, dimensions={0}, use_global_device_ids=true | all-gather | bytes 294912 | tf_op jit(solution)/shard_map/all_gather | solution.py:548
  23.9 1.4 %margin.1 = (f32[3,128,128]{2,1,0:T(8,128)S(1)}, f32[4,3,24,128]{3,2,1,0:T(8,128)S(1)}) custom-call(f32[3,128,128]{2,1,0:T(8,128)S(1)} %get-tuple-element.22.rhs_ref, bf16[2,3,128,128]{3,2,1,0:T(8,128)(2,1)S(1)} %bitcast.18, bf16[128,1024]{1,0:T(8,128)(2,1)S(1)} %get-tuple-element.24.pick_ref, bf16[128,256]{1,0:T(8,128)(2,1)S(1)} %get-tuple-element.25.place_ref, ...), custom_call_target="tpu_custom_call" | custom-call | tf_op jit(solution)/shard_map/margin/pallas_call | solution.py:314
  25.2 6.6 %all_to_all.20.got_ref.first_ref = f32[4,3,24,128]{3,2,1,0:T(8,128)S(1)} all-to-all(f32[4,3,24,128]{3,2,1,0:T(8,128)S(1)} %get-tuple-element.32.first_ref), channel_id=1, replica_groups={{0,1,32,33},{2,3,34,35},{4,5,36,37},{6,7,38,39},{8,9,40,41},{10,11,42,4..., dimensions={0} | all-to-all | bytes 294912 | tf_op jit(solution)/shard_map/all_to_all | solution.py:539
  31.9 0.1 second.1
  32.0 16.5 %all_to_all.21.second_ref = f32[4,3,32,128]{3,2,1,0:T(8,128)S(1)} all-to-all(f32[4,3,32,128]{3,2,1,0:T(8,128)S(1)} %second.1), channel_id=1, replica_groups={{33,34,65,66},{35,36,67,68},{37,38,69,70},{39,40,71,72},{41,42,73,74},{..., dimensions={0} | all-to-all | bytes 393216 | tf_op jit(solution)/shard_map/all_to_all | solution.py:539
  48.4 0.7 copy-done.9
  49.1 2.1 %images.1 = (f32[3,128,128]{2,1,0:T(8,128)S(1)}, f32[3,128,128]{2,1,0:T(8,128)S(1)}, f32[3,128,128]{2,1,0:T(8,128)S(1)}, f32[32,2,128]{2,1,0:T(2,128)S(1)}) custom-call(f32[1,24]{1,0:T(1,128)S(1)} %bitcast.24, f32[3,128,128]{2,1,0:T(8,128)S(1)} %get-tuple-element.31.b_ref, f32[4,3,24,128]{3,2,1,0:T(8,128)S(1)} %all_to_all.20.got_ref.first_ref, ...), custom_call_target="tpu_custom_call" | custom-call | tf_op jit(solution)/shard_map/images/pallas_call | solution.py:446
  51.2 17.1 %all_to_all.22.in_ref = f32[32,2,128]{2,1,0:T(2,128)S(1)} all-to-all(f32[32,2,128]{2,1,0:T(2,128)S(1)} %get-tuple-element.33), channel_id=1, replica_groups=mesh['panel'=2,'lat'=8,'lon'=32] {'lon'}, dimensions={0} | all-to-all | bytes 65536 | tf_op jit(solution)/shard_map/all_to_all | solution.py:556
  68.3 17.3 %all_to_all.23.s_ref = f32[16,2,128]{2,1,0:T(2,128)S(1)} all-to-all(f32[16,2,128]{2,1,0:T(2,128)S(1)} %relay.1), channel_id=1, replica_groups=mesh['panel'=2,'lat'=8,'lon'=32] {'panel','lat'}, dimensions={0} | all-to-all | bytes 32768 | tf_op jit(solution)/shard_map/all_to_all | solution.py:557
  85.6 1.1 %iterate.1 = (f32[384,128]{1,0:T(8,128)}, f32[384,128]{1,0:T(8,128)}) custom-call(f32[1,24]{1,0:T(1,128)S(1)} %bitcast.25, f32[16,2,128]{2,1,0:T(2,128)S(1)} %all_to_all.23.s_ref, f32[3,128,128]{2,1,0:T(8,128)S(1)} %get-tuple-element.31.b_ref, f32[3,128,128]{2,1,0:T(8,128)S(1)} %get-tuple-element.34.c_ref, f32[3,128,128]{2,1,0:T(8,128)S(1)} %get-tuple-element.35.u1_ref, ...), custom_call_target="tpu_custom_call" | custom-call | tf_op jit(solution)/shard_map/iterate/pallas_call | solution.py:504
  (16 shorter events, 0.0 us)
Async XLA Ops:
  0.6 1.1 %copy-start = (bf16[1,6,24,16,128]{4,3,2,1,0:T(8,128)(2,1)S(1)}, bf16[1,6,24,16,128]{4,3,2,1,0:T(8,128)(2,1)}, u32[]{:S(2)}) copy-start(bf16[1,6,24,16,128]{4,3,2,1,0:T(8,128)(2,1)} %param.9) | copy-start | bytes 1769476
  1.7 0.7 copy-start.3
  2.4 5.8 %copy-start.1 = (bf16[1,6,24,16,128]{4,3,2,1,0:T(8,128)(2,1)S(1)}, bf16[1,6,24,16,128]{4,3,2,1,0:T(8,128)(2,1)}, u32[]{:S(2)}) copy-start(bf16[1,6,24,16,128]{4,3,2,1,0:T(8,128)(2,1)} %param.9) | copy-start | bytes 1769476
  4.1 9.1 %copy-start.2 = (f32[1,24,16,128]{3,2,1,0:T(8,128)S(1)}, f32[1,24,16,128]{3,2,1,0:T(8,128)}, u32[]{:S(2)}) copy-start(f32[1,24,16,128]{3,2,1,0:T(8,128)} %param.10) | copy-start | bytes 589828
  4.1 9.1 %collective-permute-start = (bf16[3,24,16,128]{3,2,1,0:T(8,128)(2,1)S(1)}, bf16[3,24,16,128]{3,2,1,0:T(8,128)(2,1)S(1)}, u32[]{:S(2)}, u32[]{:S(2)}) collective-permute-start(bf16[3,24,16,128]{3,2,1,0:T(8,128)(2,1)S(1)} %pack.1), channel_id=1, source_target_pairs={{0,1},{1,2},{2,3},{3,4},{4,5},{5,6},{6,7},{7,8},{8,9},{9,10},{10,1... | collective-permute-start | bytes 884744 | tf_op jit(solution)/shard_map/ppermute | solution.py:514
  8.2 1.8 %copy-start.5 = (f32[24,24]{1,0:T(8,128)S(1)}, f32[24,24]{1,0:T(8,128)}, u32[]{:S(2)}) copy-start(f32[24,24]{1,0:T(8,128)} %proj_ref.1) | copy-start | bytes 6916
  8.2 1.8 %copy-start.8 = (f32[1,1,256,4]{2,3,1,0:T(4,128)S(1)}, f32[1,1,256,4]{2,3,1,0:T(4,128)}, u32[]{:S(2)}) copy-start(f32[1,1,256,4]{2,3,1,0:T(4,128)} %param.17) | copy-start | bytes 12292
  8.7 1.3 %copy-start.7 = (s32[1,1,256,4]{2,3,1,0:T(4,128)S(1)}, s32[1,1,256,4]{2,3,1,0:T(4,128)}, u32[]{:S(2)}) copy-start(s32[1,1,256,4]{2,3,1,0:T(4,128)} %param.16) | copy-start | bytes 12292
  8.7 4.4 %collective-permute-start.1 = (bf16[3,16,128]{2,1,0:T(8,128)(2,1)S(1)}, bf16[3,16,128]{2,1,0:T(8,128)(2,1)S(1)}, u32[]{:S(2)}, u32[]{:S(2)}) collective-permute-start(bf16[3,16,128]{2,1,0:T(8,128)(2,1)S(1)} %pack_east.1), channel_id=1, source_target_pairs={{1,0},{2,1},{3,2},{4,3},{5,4},{6,5},{7,6},{8,7},{9,8},{10,9},{11,1... | collective-permute-start | bytes 36872 | tf_op jit(solution)/shard_map/ppermute | solution.py:514
  10.0 0.7 copy-start.10
  10.7 2.5 %copy-start.4 = (s32[1,16,32]{2,1,0:T(8,128)S(1)}, s32[1,16,32]{2,1,0:T(8,128)}, u32[]{:S(2)}) copy-start(s32[1,16,32]{2,1,0:T(8,128)} %param.11) | copy-start | bytes 6148
  10.7 2.5 %copy-start.6 = (f32[6,24]{1,0:T(8,128)S(1)}, f32[6,24]{1,0:T(8,128)}, u32[]{:S(2)}) copy-start(f32[6,24]{1,0:T(8,128)} %mix_ref.1) | copy-start | bytes 1732
  48.4 0.7 copy-start.9

commit v5 on v4

--- a/solution.py
+++ b/solution.py
@@ -37,8 +37,8 @@
     return jnp.broadcast_to(own, (ROWS, COLS))
 
 
-def half_mask(mask):
-    return jnp.where(mask, 1, 0).astype(jnp.int16) == jnp.int16(1)
+def half_bits(mask):
+    return jnp.where(mask, 1, 0).astype(jnp.int16)
 
 
 def lane_matrix(rule):
@@ -74,135 +74,169 @@
     )(fields)
 
 
-def pack_kernel(shift_ref, fields_ref, west_ref, scratch):
+def pack_kernel(shift_hbm, fields_hbm, west_ref, kept_ref, shift_ref, scratch, mask_ref, matrix_ref, sems):
+    table = pltpu.make_async_copy(shift_hbm, shift_ref, sems.at[G])
+    table.start()
+    copies = []
+    for g in range(G):
+        part = (slice(None), pl.ds(8 * g, 8))
+        copies.append(pltpu.make_async_copy(fields_hbm.at[part], kept_ref.at[part], sems.at[g]))
+        copies[-1].start()
+    table.wait()
+    pack_plan(shift_ref, mask_ref, matrix_ref)
+    masks = [mask_ref[n] == 1 for n in range(4)]
+    zero = jnp.zeros((ROWS, COLS), BF16)
+    for g in range(G):
+        copies[g].wait()
+        for l8 in range(8):
+            level = 8 * g + l8
+            parts = [
+                jnp.concatenate([jnp.where(m, kept_ref[f, level], zero) for m in masks], axis=1) for f in range(NF)
+            ]
+            wide = jnp.dot(jnp.concatenate(parts, axis=0), matrix_ref[...], preferred_element_type=F32)
+            scratch[l8] = wide
+            pairs = scratch[l8, pl.ds(0, 8 * NF, stride=2), :] + scratch[l8, pl.ds(1, 8 * NF, stride=2), :]
+            pairs = pairs.astype(BF16)
+            for n in range(NF // 2):
+                west_ref[n, level] = pairs[ROWS * n : ROWS * n + ROWS]
+
+
+def pack_plan(shift_ref, mask_ref, matrix_ref):
     shift = own_shift(shift_ref, lax.axis_index("lon") + 1)
     lane = lane_iota((ROWS, COLS))
     low = (lax.broadcasted_iota(jnp.int32, (ROWS, COLS), 0) & 1) == 0
     block = lane >= COLS - 32 * shift
     single = lane == COLS - 1 - 32 * shift
-    masks = [half_mask(m & row) for row in (low, ~low) for m in (block, single)]
-    matrix = jnp.concatenate(
-        [
-            lane_matrix(lambda s, t: s == t),
-            lane_matrix(lambda s, t: ((s & 31) == 31) & (t == 31)),
-            lane_matrix(mirrored),
-            lane_matrix(lambda s, t: ((s & 31) == 31) & (t == 30)),
+    for n, mask in enumerate([m & row for row in (low, ~low) for m in (block, single)]):
+        mask_ref[n] = half_bits(mask)
+    rules = (
+        lambda s, t: s == t,
+        lambda s, t: ((s & 31) == 31) & (t == 31),
+        mirrored,
+        lambda s, t: ((s & 31) == 31) & (t == 30),
+    )
+    for n, rule in enumerate(rules):
+        matrix_ref[COLS * n : COLS * n + COLS, :] = lane_matrix(rule)
+
+
+def pack(shift, fields):
+    return pl.pallas_call(
+        pack_kernel,
+        in_specs=[pl.BlockSpec(memory_space=pltpu.HBM)] * 2,
+        out_specs=[pl.BlockSpec(memory_space=pltpu.VMEM)] * 2,
+        out_shape=[
+            jax.ShapeDtypeStruct((NF // 2, LEV, ROWS, COLS), BF16),
+            jax.ShapeDtypeStruct((NF, LEV, ROWS, COLS), BF16),
         ],
-        axis=0,
-    )
-    zero = jnp.zeros((ROWS, COLS), BF16)
-    for l8 in range(8):
-        parts = [
-            jnp.concatenate([jnp.where(m, fields_ref[f, l8], zero) for m in masks], axis=1) for f in range(NF)
-        ]
-        scratch[l8] = jnp.dot(jnp.concatenate(parts, axis=0), matrix, preferred_element_type=F32)
-        pairs = scratch[l8, pl.ds(0, 8 * NF, stride=2), :] + scratch[l8, pl.ds(1, 8 * NF, stride=2), :]
-        pairs = pairs.astype(BF16)
-        for n in range(NF // 2):
-            west_ref[n, l8] = pairs[ROWS * n : ROWS * n + ROWS]
-
-
-def pack(shift, fields):
-    return pl.pallas_call(
-        pack_kernel,
-        grid=(G,),
-        in_specs=[
-            pl.BlockSpec((ROWS, 32), lambda g: (0, 0)),
-            pl.BlockSpec((NF, 8, ROWS, COLS), lambda g: (0, g, 0, 0)),
+        scratch_shapes=[
+            pltpu.VMEM((ROWS, 32), jnp.int32),
+            pltpu.VMEM((8, NF * ROWS, COLS), F32),
+            pltpu.VMEM((4, ROWS, COLS), jnp.int16),
+            pltpu.VMEM((4 * COLS, COLS), BF16),
+            pltpu.SemaphoreType.DMA((G + 1,)),
         ],
-        out_specs=pl.BlockSpec((NF // 2, 8, ROWS, COLS), lambda g: (0, g, 0, 0)),
-        out_shape=jax.ShapeDtypeStruct((NF // 2, LEV, ROWS, COLS), BF16),
-        scratch_shapes=[pltpu.VMEM((8, NF * ROWS, COLS), F32)],
         compiler_params=params(),
         name="pack",
-    )(shift, fields)
-
-
-def advect_kernel(mix_ref, shift_ref, frac_ref, fields_ref, west_ref, east_ref, adv_ref, rhs_ref, half_ref, scratch):
-    g = pl.program_id(0)
+    )(*(pltpu.with_memory_space_constraint(x, pltpu.HBM) for x in (shift, fields)))
+
+
+TAPS = (-1, 0, 1, 2)
+
+
+def turn(x, sign, odd, two):
+    x = jnp.where(odd, roll_lanes(x, 32 * sign), x)
+    return jnp.where(two, roll_lanes(x, 64), x)
+
+
+def advect_plan(mix_ref, shift_ref, frac_ref, mix_out_ref, mask_ref, shift_out_ref, matrix_ref, weight_ref):
+    for f in range(NF):
+        for level in range(LEV):
+            mix_out_ref[f, level] = jnp.full((8, COLS), mix_ref[f, level], F32)
     shift = own_shift(shift_ref, lax.axis_index("lon"))
+    shift_out_ref[...] = shift
     lane = lane_iota((ROWS, COLS))
     low = (lax.broadcasted_iota(jnp.int32, (ROWS, COLS), 0) & 1) == 0
-    swap16 = half_mask(~low & ((lane >> 5) != 2))
-    single16 = half_mask(lane == jnp.where(low, 31, 30))
-    single_at = jnp.concatenate([lane == ((COLS - 32 * shift) & (COLS - 1))] * NF, axis=0)
-    single_to = lane_matrix(lambda s, t: ((s == 30) | (s == 31)) & ((t & 31) == 0))
-    zero = jnp.zeros((ROWS, COLS), BF16)
     odd, two = (shift & 1) == 1, (shift & 2) == 2
-    odd16, two16 = half_mask(odd), half_mask(two)
-    edge16 = half_mask(lane < 2)
-
-    def turn(x, sign, odd, two):
-        x = jnp.where(odd, roll_lanes(x, 32 * sign), x)
-        return jnp.where(two, roll_lanes(x, 64), x)
 
     def beyond(j):
         at = ((lane - j + 32 * shift) & (COLS - 1)) - 32 * shift + j
         return (at < 0) | (at >= COLS)
 
-    taps = (-1, 0, 1, 2)
-    masks = [half_mask(beyond(j)) for j in taps]
-    shifts = [lane_matrix(lambda s, t, j=j: s == ((t + j) & (COLS - 1))) for j in taps]
-    east = east_ref[0]
-    for l8 in range(8):
-        t = turn(frac_ref[l8], -1, odd, two)
+    masks = [beyond(j) for j in TAPS]
+    masks += [odd, two, lane < 2, ~low & ((lane >> 5) != 2), lane == jnp.where(low, 31, 30)]
+    for n, mask in enumerate(masks):
+        mask_ref[n] = half_bits(mask)
+    rules = [lambda s, t, j=j: s == ((t + j) & (COLS - 1)) for j in TAPS if j]
+    rules.append(lambda s, t: ((s == 30) | (s == 31)) & ((t & 31) == 0))
+    for n, rule in enumerate(rules):
+        matrix_ref[n] = lane_matrix(rule)
+    for level in range(LEV):
+        t = turn(frac_ref[level], -1, odd, two)
         tm1, tm2, tp1 = t - 1.0, t - 2.0, t + 1.0
-        weights = (
-            -t * tm1 * tm2 * (1.0 / 6.0),
-            tp1 * tm1 * tm2 * 0.5,
-            -tp1 * t * tm2 * 0.5,
-            tp1 * t * tm1 * (1.0 / 6.0),
-        )
-        shared = jnp.concatenate([west_ref[n, l8] for n in range(NF // 2)], axis=0).astype(F32)
-        scratch[l8, pl.ds(0, 8 * NF, stride=2), :] = shared
-        scratch[l8, pl.ds(1, 8 * NF, stride=2), :] = shared
-        west = scratch[l8].astype(BF16)
-        chosen = [[] for _ in taps]
-        singles = []
-        for f in range(NF):
-            other = west[ROWS * f : ROWS * f + ROWS]
-            singles.append(jnp.where(single16, other, zero))
-            other = jnp.where(swap16, roll_lanes(other, 64), other)
-            other = jnp.where(edge16, roll_lanes(east, -2 * (f * 8 + l8)), other)
-            for n, mask in enumerate(masks):
-                chosen[n].append(jnp.where(mask, other, fields_ref[f, l8]))
-        moved = []
-        for j, parts, matrix in zip(taps, chosen, shifts):
-            if j == 0:
-                moved.append([part.astype(F32) for part in parts])
-            else:
-                wide = jnp.dot(jnp.concatenate(parts, axis=0), matrix, preferred_element_type=F32)
-                if j == -1:
-                    column = jnp.dot(jnp.concatenate(singles, axis=0), single_to, preferred_element_type=F32)
+        weight_ref[0, level] = -t * tm1 * tm2 * (1.0 / 6.0)
+        weight_ref[1, level] = tp1 * tm1 * tm2 * 0.5
+        weight_ref[2, level] = -tp1 * t * tm2 * 0.5
+        weight_ref[3, level] = tp1 * t * tm1 * (1.0 / 6.0)
+
+
+def advect_kernel(
+    mix_ref, mask_ref, shift_ref, matrix_ref, weight_ref, fields_ref, west_ref, east_ref, adv_ref, rhs_ref, half_ref, scratch
+):
+    shift = shift_ref[...]
+    lane = lane_iota((ROWS, COLS))
+    odd, two = (shift & 1) == 1, (shift & 2) == 2
+    bits = [mask_ref[n] == 1 for n in range(9)]
+    masks, (odd16, two16, edge16, swap16, single16) = bits[:4], bits[4:]
+    single_at = jnp.concatenate([lane == ((COLS - 32 * shift) & (COLS - 1))] * NF, axis=0)
+    zero = jnp.zeros((ROWS, COLS), BF16)
+
+    @pl.loop(0, G)
+    def _(g):
+        east = east_ref[g]
+        for l8 in range(8):
+            level = g * 8 + l8
+            shared = jnp.concatenate([west_ref[n, level] for n in range(NF // 2)], axis=0).astype(F32)
+            scratch[l8, pl.ds(0, 8 * NF, stride=2), :] = shared
+            scratch[l8, pl.ds(1, 8 * NF, stride=2), :] = shared
+            west = scratch[l8].astype(BF16)
+            chosen = [[] for _ in TAPS]
+            singles = []
+            for f in range(NF):
+                other = west[ROWS * f : ROWS * f + ROWS]
+                singles.append(jnp.where(single16, other, zero))
+                other = jnp.where(swap16, roll_lanes(other, 64), other)
+                other = jnp.where(edge16, roll_lanes(east, -2 * (f * 8 + l8)), other)
+                own = fields_ref[f, level]
+                for n, mask in enumerate(masks):
+                    chosen[n].append(jnp.where(mask, other, own))
+            moved = [None] * 4
+            moved[1] = [part.astype(F32) for part in chosen[1]]
+            for n, tap in ((0, 0), (1, 2), (2, 3)):
+                wide = jnp.dot(jnp.concatenate(chosen[tap], axis=0), matrix_ref[n], preferred_element_type=F32)
+                if tap == 0:
+                    column = jnp.dot(jnp.concatenate(singles, axis=0), matrix_ref[3], preferred_element_type=F32)
                     wide = jnp.where(single_at, column, wide)
-                moved.append([wide[ROWS * f : ROWS * f + ROWS] for f in range(NF)])
-        total = jnp.zeros((ROWS, COLS), F32)
-        for f in range(NF):
-            acc = weights[0] * moved[0][f]
-            for n in range(1, 4):
-                acc = acc + weights[n] * moved[n][f]
-            rounded = acc.astype(BF16)
-            adv_ref[f, l8] = turn(rounded, 1, odd16, two16)
-            total = total + mix_ref[f, g * 8 + l8] * rounded.astype(F32)
-        rhs_ref[0, pl.ds(l8, ROWS, stride=8), :] = turn(total, 1, odd, two)
-    half_ref[0] = rhs_ref[0].astype(BF16)
-
-
-def advect(mix, shift, frac, fields, west, east):
-    block = pl.BlockSpec((NF, 8, ROWS, COLS), lambda g: (0, g, 0, 0))
-    group = pl.BlockSpec((1, 128, COLS), lambda g: (g, 0, 0))
+                moved[tap] = [wide[ROWS * f : ROWS * f + ROWS] for f in range(NF)]
+            weights = [weight_ref[n, level] for n in range(4)]
+            total = jnp.zeros((ROWS, COLS), F32)
+            for f in range(NF):
+                acc = weights[0] * moved[0][f]
+                for n in range(1, 4):
+                    acc = acc + weights[n] * moved[n][f]
+                rounded = acc.astype(BF16)
+                adv_ref[f, level] = turn(rounded, 1, odd16, two16)
+                mix = mix_ref[f, level]
+                total = total + jnp.concatenate([mix, mix], axis=0) * rounded.astype(F32)
+            rhs_ref[g, pl.ds(l8, ROWS, stride=8), :] = turn(total, 1, odd, two)
+        half_ref[g] = rhs_ref[g].astype(BF16)
+
+
+def advect(plan, fields, west, east):
+    whole = pl.BlockSpec(memory_space=pltpu.VMEM)
     return pl.pallas_call(
         advect_kernel,
-        grid=(G,),
-        in_specs=[
-            pl.BlockSpec(memory_space=pltpu.SMEM),
-            pl.BlockSpec((ROWS, 32), lambda g: (0, 0)),
-            pl.BlockSpec((8, ROWS, COLS), lambda g: (g, 0, 0)),
-            block,
-            pl.BlockSpec((NF // 2, 8, ROWS, COLS), lambda g: (0, g, 0, 0)),
-            pl.BlockSpec((1, ROWS, COLS), lambda g: (g, 0, 0)),
-        ],
-        out_specs=[block, group, group],
+        in_specs=[whole] * 8,
+        out_specs=[whole] * 3,
         out_shape=[
             jax.ShapeDtypeStruct((NF, LEV, ROWS, COLS), BF16),
             jax.ShapeDtypeStruct((G, 128, COLS), F32),
@@ -211,7 +245,7 @@
         scratch_shapes=[pltpu.VMEM((8, NF * ROWS, COLS), F32)],
         compiler_params=params(),
         name="advect",
-    )(mix, shift, frac, fields, west, east)
+    )(*plan, fields, west, east)
 
 
 SLOTS = 20
@@ -229,9 +263,13 @@
     return a, b, c
 
 
-def tables_kernel(
-    cells_ref, source_ref, weight_ref, proj_ref, pick_ref, place_ref, in_row_ref, covered_ref, src_row_ref, wgt_ref, proj_out_ref
+def prepare_kernel(
+    mix_ref, shift_ref, frac_ref, mode_ref, cells_ref, source_ref, weight_ref, proj_ref,
+    mix_out_ref, mask_ref, own_ref, matrix_ref, taps_ref, mode_out_ref,
+    pick_ref, place_ref, in_row_ref, covered_ref, src_row_ref, wgt_ref, proj_out_ref,
 ):
+    advect_plan(mix_ref, shift_ref, frac_ref, mix_out_ref, mask_ref, own_ref, matrix_ref, taps_ref)
+    mode_out_ref[...] = mode_ref[...]
     proj_out_ref[...] = proj_ref[...]
     src = jnp.concatenate([source_ref[q : q + 1, :] for q in range(4)], axis=1)
     wgt = jnp.concatenate([weight_ref[q : q + 1, :] for q in range(4)], axis=1)
@@ -250,22 +288,31 @@
     covered_ref[...] = lax.dot_general(in_row, place, nt, preferred_element_type=F32)
 
 
-def tables(cells, source, weight, proj):
-    return pl.pallas_call(
-        tables_kernel,
-        out_shape=[
-            jax.ShapeDtypeStruct((COLS, 4 * OV), BF16),
-            jax.ShapeDtypeStruct((128, OV), BF16),
-            jax.ShapeDtypeStruct((128, OV), BF16),
-            jax.ShapeDtypeStruct((128, COLS), F32),
-            jax.ShapeDtypeStruct((8, 4 * OV), jnp.int32),
-            jax.ShapeDtypeStruct((8, 4 * OV), F32),
-            jax.ShapeDtypeStruct((LEV, LEV), F32),
-        ],
-        compiler_params=params(),
-        cost_estimate=pl.CostEstimate(flops=4_000_000, bytes_accessed=500_000, transcendentals=0),
-        name="tables",
-    )(cells, source, weight, proj)
+def prepare(*args):
+    shapes = [
+        ((NF, LEV, 8, COLS), F32),
+        ((9, ROWS, COLS), jnp.int16),
+        ((ROWS, COLS), jnp.int32),
+        ((4, COLS, COLS), BF16),
+        ((4, LEV, ROWS, COLS), F32),
+        ((1, LEV), F32),
+        ((COLS, 4 * OV), BF16),
+        ((128, OV), BF16),
+        ((128, OV), BF16),
+        ((128, COLS), F32),
+        ((8, 4 * OV), jnp.int32),
+        ((8, 4 * OV), F32),
+        ((LEV, LEV), F32),
+    ]
+    made = pl.pallas_call(
+        prepare_kernel,
+        in_specs=[pl.BlockSpec(memory_space=pltpu.SMEM)] + [pl.BlockSpec(memory_space=pltpu.VMEM)] * 7,
+        out_shape=[jax.ShapeDtypeStruct(shape, dtype) for shape, dtype in shapes],
+        compiler_params=params(),
+        cost_estimate=pl.CostEstimate(flops=4_000_000, bytes_accessed=2_000_000, transcendentals=0),
+        name="prepare",
+    )(*args)
+    return made[:5], made[5], made[6:]
 
 
 def margin_kernel(
@@ -348,7 +395,9 @@
     )(b, first, got)
 
 
-def images_kernel(shift_ref, b_ref, first_ref, second_ref, c_ref, u1_ref, u2_ref, s_ref):
+def images_kernel(shift_ref, b_ref, first_ref, second_ref, adv_ref, c_ref, u1_ref, u2_ref, s_ref, adv_hbm, sem):
+    leaving = pltpu.make_async_copy(adv_ref, adv_hbm, sem)
+    leaving.start()
     lat, lon = lax.axis_index("lat"), lax.axis_index("lon")
     one = jnp.float32(1.0)
     zero = jnp.float32(0.0)
@@ -439,16 +488,26 @@
     folded = jnp.concatenate([jnp.sum(spread[4 * h : 4 * h + 4], axis=0, keepdims=True) for h in range(2)], axis=0)
     for n in range(s_ref.shape[0]):
         s_ref[n] = folded
-
-
-def images(mode_shift, b, got_first, got_second, copies):
+    leaving.wait()
+
+
+def images(mode_shift, b, got_first, got_second, adv, copies):
     full = jax.ShapeDtypeStruct((G, 128, COLS), F32)
     return pl.pallas_call(
         images_kernel,
-        out_shape=[full, full, full, jax.ShapeDtypeStruct((copies, 2, COLS), F32)],
+        in_specs=[pl.BlockSpec(memory_space=pltpu.VMEM)] * 5,
+        out_specs=[pl.BlockSpec(memory_space=pltpu.VMEM)] * 4 + [pl.BlockSpec(memory_space=pltpu.HBM)],
+        out_shape=[
+            full,
+            full,
+            full,
+            jax.ShapeDtypeStruct((copies, 2, COLS), F32),
+            jax.ShapeDtypeStruct(adv.shape, adv.dtype),
+        ],
+        scratch_shapes=[pltpu.SemaphoreType.DMA(())],
         compiler_params=params(),
         name="images",
-    )(mode_shift, b, got_first, got_second)
+    )(mode_shift, b, got_first, got_second, adv)
 
 
 def sum_copies(ref):
@@ -541,21 +600,24 @@
 
 def per_device(fields, frac, shift, mix, proj, mode_shift, cells, source, weight):
     fields = fields[0]
-    lists = tables(cells[0], source[0, 0].T, weight[0, 0].T, proj)
+    table = shift[0]
+    plan, modes, lists = prepare(
+        mix, table, frac[0], mode_shift.reshape(1, LEV), cells[0], source[0, 0].T, weight[0, 0].T, proj
+    )
+    packed, fields = pack(table, fields)
+    west = send(packed, "lon", 1)
     east = send(pack_east(fields), "lon", -1)
-    west = send(pack(shift[0], fields), "lon", 1)
-    adv, rhs, half = advect(mix, shift[0], frac[0], fields, west, east)
+    adv, rhs, half = advect(plan, fields, west, east)
     both = lax.all_gather(half, "panel")
     b, first = margin(rhs, both, lists)
     got_first = in_squares(first, 0)
     got_second = in_squares(second(b, first, got_first), 1)
-    shifts = mode_shift.reshape(1, LEV)
     count = lax.axis_size("lon")
     rest = lax.axis_size("panel") * lax.axis_size("lat")
-    c, u1, u2, sums = images(shifts, b, got_first, got_second, count)
+    c, u1, u2, sums, adv = images(modes, b, got_first, got_second, adv, count)
     sums = relay(lax.all_to_all(sums, "lon", 0, 0), rest)
     sums = lax.all_to_all(sums, ("panel", "lat"), 0, 0)
-    sol, res = iterate(shifts, sums, b, c, u1, u2)
+    sol, res = iterate(modes, sums, b, c, u1, u2)
     shape = (1, LEV, ROWS, COLS)
     return adv[None], sol.reshape(shape), res.reshape(shape)
 

time: 87.1 us -> 84.4 us (0.969)
  local copies, waits for them, and re-layouts: 3.09 us -> 0.65 us
    unnamed x22 -> x16, local copies, waits for them, and re-layouts: 3.09 us -> 0.65 us
  transfers between devices with their start and end apart: 2 -> 2, of which waited for: 1 -> 1; matrix products, arithmetic and copies ran while one was open for 0% -> 0% of each run, Pallas kernels for 1% -> 2%
where the time goes in v5:
time: 84.4 us; the launch traced here: 84 us
  blocking collectives  64.4 us (76%)
  Pallas kernels  11.3 us (13%)
  starting transfers between devices  5.26 us (6%)
  waiting for transfers between devices  1.53 us (2%)
    all_to_all x2, blocking collectives, in_squares(): return lax.all_to_all(slots, ('lat', 'lon'), 0, 0, axis_index_groups=groups)  23.1 us
    all_to_all x1, blocking collectives, per_device(): sums = lax.all_to_all(sums, ('panel', 'lat'), 0, 0)  17.3 us
    all_to_all x1, blocking collectives, per_device(): sums = relay(lax.all_to_all(sums, 'lon', 0, 0), rest)  17.1 us
    all_gather x1, blocking collectives, per_device(): both = lax.all_gather(half, 'panel')  6.96 us
    ppermute x2, starting transfers between devices, send(): lax.ppermute(block, axis, [(i, i + by) for i in range(count) if 0 <= i +...  5.26 us
    pallas_call x1, Pallas kernels, images(): pl.pallas_call(images_kernel, in_specs=[pl.BlockSpec(memory_space=pltpu.V...  2.7 us
    pallas_call x1, Pallas kernels, advect(): pl.pallas_call(advect_kernel, in_specs=[whole] * 8, out_specs=[whole] * 3...  2.36 us
    pallas_call x1, Pallas kernels, pack(): pl.pallas_call(pack_kernel, in_specs=[pl.BlockSpec(memory_space=pltpu.HBM...  2.32 us
  transfers between devices with their start and end apart: 2, of which 1 were waited for; matrix products, arithmetic and copies ran while one was open for 0% of the time, Pallas kernels for 2%

profile of v5, /device:TPU:1, one launch (start us, length us, event | category | flops | bytes accessed | tf_op | source)
XLA Modules:
  0.0 84.0 jit_solution(8686401636723454404)
XLA Ops:
  0.6 2.3 %pack.1 = (bf16[3,24,16,128]{3,2,1,0:T(8,128)(2,1)S(1)}, bf16[6,24,16,128]{3,2,1,0:T(8,128)(2,1)S(1)}) custom-call(s32[16,32]{1,0:T(8,128)} %bitcast.17, bf16[6,24,16,128]{3,2,1,0:T(8,128)(2,1)} %bitcast.23), custom_call_target="tpu_custom_call" | custom-call | tf_op jit(solution)/shard_map/pack/pallas_call | solution.py:123
  3.0 4.0 %collective-permute-start = (bf16[3,24,16,128]{3,2,1,0:T(8,128)(2,1)S(1)}, bf16[3,24,16,128]{3,2,1,0:T(8,128)(2,1)S(1)}, u32[]{:S(2)}, u32[]{:S(2)}) collective-permute-start(bf16[3,24,16,128]{3,2,1,0:T(8,128)(2,1)S(1)} %get-tuple-element.37), channel_id=1, source_target_pairs={{0,1},{1,2},{2,3},{3,4},{4,5},{5,6},{6,7},{7,8},{8,9},{9,10},{10,1... | collective-permute-start | bytes 884744 | tf_op jit(solution)/shard_map/ppermute | solution.py:573
  6.9 0.0 copy-start
  6.9 0.0 copy-start.2
  6.9 0.0 copy-start.3
  7.0 0.0 copy-start.4
  7.0 0.0 copy-start.5
  7.0 0.0 copy-start.7
  7.0 0.5 pack_east.1
  7.5 1.3 %collective-permute-start.1 = (bf16[3,16,128]{2,1,0:T(8,128)(2,1)S(1)}, bf16[3,16,128]{2,1,0:T(8,128)(2,1)S(1)}, u32[]{:S(2)}, u32[]{:S(2)}) collective-permute-start(bf16[3,16,128]{2,1,0:T(8,128)(2,1)S(1)} %pack_east.1), channel_id=1, source_target_pairs={{1,0},{2,1},{3,2},{4,3},{5,4},{6,5},{7,6},{8,7},{9,8},{10,9},{11,1... | collective-permute-start | bytes 36872 | tf_op jit(solution)/shard_map/ppermute | solution.py:573
  8.8 0.0 copy-start.6
  8.9 0.6 copy-done.6
  9.5 0.9 %prepare.1 = (f32[6,24,8,128]{3,2,1,0:T(8,128)S(1)}, s16[9,16,128]{2,1,0:T(8,128)(2,1)S(1)}, s32[16,128]{1,0:T(8,128)S(1)}, bf16[4,128,128]{2,1,0:T(8,128)(2,1)S...) custom-call(f32[6,24]{1,0:T(8,128)S(1)} %copy-done.3, ...), custom_call_target="tpu_custom_call" | custom-call | flops 4000000 | bytes 2000000 | tf_op jit(solution)/shard_map/prepare/pallas_call | solution.py:307
  10.4 1.5 %collective-permute-done.1.east_ref = bf16[3,16,128]{2,1,0:T(8,128)(2,1)S(1)} collective-permute-done((bf16[3,16,128]{2,1,0:T(8,128)(2,1)S(1)}, bf16[3,16,128]{2,1,0:T(8,128)(2,1)S(1)}, u32[]{:S(2)}, u32[]{:S(2)}) %collective-permute-start.1) | collective-permute-done | bytes 12320 | tf_op jit(solution)/shard_map/ppermute | solution.py:573
  11.9 2.4 %advect.1 = (bf16[6,24,16,128]{3,2,1,0:T(8,128)(2,1)S(1)}, f32[3,128,128]{2,1,0:T(8,128)S(1)}, bf16[3,128,128]{2,1,0:T(8,128)(2,1)S(1)}) custom-call(f32[6,24,8,128]{3,2,1,0:T(8,128)S(1)} %get-tuple-element.31.mix_ref, s16[9,16,128]{2,1,0:T(8,128)(2,1)S(1)} %get-tuple-element.32.mask_ref, s32[16,128]{1,0:T(8,128)S(1)} %get-tuple-element.33.shift_ref, ...), custom_call_target="tpu_custom_call" | custom-call | tf_op jit(solution)/shard_map/advect/pallas_call | solution.py:236
  14.3 7.0 %all-gather = bf16[6,128,128]{2,1,0:T(8,128)(2,1)S(1)} all-gather(bf16[3,128,128]{2,1,0:T(8,128)(2,1)S(1)} %get-tuple-element.39), channel_id=2, replica_groups=mesh['panel'=2,'lat'=8,'lon'=32] {'panel'}, dimensions={0}, use_global_device_ids=true | all-gather | bytes 294912 | tf_op jit(solution)/shard_map/all_gather | solution.py:611
  21.3 1.4 %margin.1 = (f32[3,128,128]{2,1,0:T(8,128)S(1)}, f32[4,3,24,128]{3,2,1,0:T(8,128)S(1)}) custom-call(f32[3,128,128]{2,1,0:T(8,128)S(1)} %get-tuple-element.38.rhs_ref, bf16[2,3,128,128]{3,2,1,0:T(8,128)(2,1)S(1)} %bitcast.15, bf16[128,1024]{1,0:T(8,128)(2,1)S(1)} %get-tuple-element.40.pick_ref, bf16[128,256]{1,0:T(8,128)(2,1)S(1)} %get-tuple-element.41.place_ref, ...), custom_call_target="tpu_custom_call" | custom-call | tf_op jit(solution)/shard_map/margin/pallas_call | solution.py:361
  22.6 6.6 %all_to_all.20.got_ref.first_ref = f32[4,3,24,128]{3,2,1,0:T(8,128)S(1)} all-to-all(f32[4,3,24,128]{3,2,1,0:T(8,128)S(1)} %get-tuple-element.48.first_ref), channel_id=1, replica_groups={{0,1,32,33},{2,3,34,35},{4,5,36,37},{6,7,38,39},{8,9,40,41},{10,11,42,4..., dimensions={0} | all-to-all | bytes 294912 | tf_op jit(solution)/shard_map/all_to_all | solution.py:598
  29.3 0.1 second.1
  29.4 16.5 %all_to_all.21.second_ref = f32[4,3,32,128]{3,2,1,0:T(8,128)S(1)} all-to-all(f32[4,3,32,128]{3,2,1,0:T(8,128)S(1)} %second.1), channel_id=1, replica_groups={{33,34,65,66},{35,36,67,68},{37,38,69,70},{39,40,71,72},{41,42,73,74},{..., dimensions={0} | all-to-all | bytes 393216 | tf_op jit(solution)/shard_map/all_to_all | solution.py:598
  45.8 2.7 %images.1 = (f32[3,128,128]{2,1,0:T(8,128)S(1)}, f32[3,128,128]{2,1,0:T(8,128)S(1)}, f32[3,128,128]{2,1,0:T(8,128)S(1)}, f32[32,2,128]{2,1,0:T(2,128)S(1)}, bf16[6,24,16,128]{3,2,1,0:T(8,128)(2,1)}) custom-call(f32[1,24]{1,0:T(1,128)S(1)} %get-tuple-element.30.shift_ref, f32[3,128,128]{2,1,0:T(8,128)S(1)} %get-tuple-element.47.b_ref, ...), custom_call_target="tpu_custom_call" | custom-call | tf_op jit(solution)/shard_map/images/pallas_call | solution.py:496
  48.5 17.1 %all_to_all.22.in_ref = f32[32,2,128]{2,1,0:T(2,128)S(1)} all-to-all(f32[32,2,128]{2,1,0:T(2,128)S(1)} %get-tuple-element.51), channel_id=1, replica_groups=mesh['panel'=2,'lat'=8,'lon'=32] {'lon'}, dimensions={0} | all-to-all | bytes 65536 | tf_op jit(solution)/shard_map/all_to_all | solution.py:618
  65.7 17.3 %all_to_all.23.s_ref = f32[16,2,128]{2,1,0:T(2,128)S(1)} all-to-all(f32[16,2,128]{2,1,0:T(2,128)S(1)} %relay.1), channel_id=1, replica_groups=mesh['panel'=2,'lat'=8,'lon'=32] {'panel','lat'}, dimensions={0} | all-to-all | bytes 32768 | tf_op jit(solution)/shard_map/all_to_all | solution.py:619
  82.9 1.1 %iterate.1 = (f32[384,128]{1,0:T(8,128)}, f32[384,128]{1,0:T(8,128)}) custom-call(f32[1,24]{1,0:T(1,128)S(1)} %get-tuple-element.30.shift_ref, f32[16,2,128]{2,1,0:T(2,128)S(1)} %all_to_all.23.s_ref, f32[3,128,128]{2,1,0:T(8,128)S(1)} %get-tuple-element.47.b_ref, f32[3,128,128]{2,1,0:T(8,128)S(1)} %get-tuple-element.52.c_ref, ...), custom_call_target="tpu_custom_call" | custom-call | tf_op jit(solution)/shard_map/iterate/pallas_call | solution.py:563
  (10 shorter events, 0.0 us)
Async XLA Ops:
  3.0 9.0 %collective-permute-start = (bf16[3,24,16,128]{3,2,1,0:T(8,128)(2,1)S(1)}, bf16[3,24,16,128]{3,2,1,0:T(8,128)(2,1)S(1)}, u32[]{:S(2)}, u32[]{:S(2)}) collective-permute-start(bf16[3,24,16,128]{3,2,1,0:T(8,128)(2,1)S(1)} %get-tuple-element.37), channel_id=1, source_target_pairs={{0,1},{1,2},{2,3},{3,4},{4,5},{5,6},{6,7},{7,8},{8,9},{9,10},{10,1... | collective-permute-start | bytes 884744 | tf_op jit(solution)/shard_map/ppermute | solution.py:573
  6.9 1.9 %copy-start = (f32[1,24,16,128]{3,2,1,0:T(8,128)S(1)}, f32[1,24,16,128]{3,2,1,0:T(8,128)}, u32[]{:S(2)}) copy-start(f32[1,24,16,128]{3,2,1,0:T(8,128)} %param.10) | copy-start | bytes 589828
  6.9 1.9 %copy-start.2 = (f32[24,24]{1,0:T(8,128)S(1)}, f32[24,24]{1,0:T(8,128)}, u32[]{:S(2)}) copy-start(f32[24,24]{1,0:T(8,128)} %proj_ref.1) | copy-start | bytes 6916
  6.9 1.9 %copy-start.3 = (f32[6,24]{1,0:T(8,128)S(1)}, f32[6,24]{1,0:T(8,128)}, u32[]{:S(2)}) copy-start(f32[6,24]{1,0:T(8,128)} %mix_ref.1) | copy-start | bytes 1732
  7.0 1.9 %copy-start.4 = (s32[1,1,256,4]{2,3,1,0:T(4,128)S(1)}, s32[1,1,256,4]{2,3,1,0:T(4,128)}, u32[]{:S(2)}) copy-start(s32[1,1,256,4]{2,3,1,0:T(4,128)} %param.16) | copy-start | bytes 12292
  7.0 1.9 %copy-start.5 = (f32[1,1,256,4]{2,3,1,0:T(4,128)S(1)}, f32[1,1,256,4]{2,3,1,0:T(4,128)}, u32[]{:S(2)}) copy-start(f32[1,1,256,4]{2,3,1,0:T(4,128)} %param.17) | copy-start | bytes 12292
  7.0 1.9 %copy-start.7 = (f32[24]{0:T(128)S(1)}, f32[24]{0:T(128)}, u32[]{:S(2)}) copy-start(f32[24]{0:T(128)} %param.14) | copy-start | bytes 292
  7.5 1.4 %copy-start.1 = (s32[1,16,32]{2,1,0:T(8,128)S(1)}, s32[1,16,32]{2,1,0:T(8,128)}, u32[]{:S(2)}) copy-start(s32[1,16,32]{2,1,0:T(8,128)} %param.11) | copy-start | bytes 6148
  7.5 4.4 %collective-permute-start.1 = (bf16[3,16,128]{2,1,0:T(8,128)(2,1)S(1)}, bf16[3,16,128]{2,1,0:T(8,128)(2,1)S(1)}, u32[]{:S(2)}, u32[]{:S(2)}) collective-permute-start(bf16[3,16,128]{2,1,0:T(8,128)(2,1)S(1)} %pack_east.1), channel_id=1, source_target_pairs={{1,0},{2,1},{3,2},{4,3},{5,4},{6,5},{7,6},{8,7},{9,8},{10,9},{11,1... | collective-permute-start | bytes 36872 | tf_op jit(solution)/shard_map/ppermute | solution.py:573
  8.8 0.7 copy-start.6

commit v6 on v5

--- a/solution.py
+++ b/solution.py
@@ -52,22 +52,21 @@
 
 
 def pack_east_kernel(fields_ref, out_ref):
-    lane = lane_iota((ROWS, COLS))
-    acc = jnp.zeros((ROWS, COLS), F32)
-    for f in range(NF):
-        for l8 in range(8):
-            i = f * 8 + l8
-            x = roll_lanes(fields_ref[f, l8].astype(F32), 2 * i)
-            acc = jnp.where((lane >> 1) == i, x, acc)
-    out_ref[0] = acc.astype(BF16)
+    pair = (lane_iota((ROWS, COLS)) >> 1).astype(jnp.int16)
+    for g in range(G):
+        acc = jnp.zeros((ROWS, COLS), BF16)
+        for f in range(NF):
+            for l8 in range(8):
+                i = f * 8 + l8
+                acc = jnp.where(pair == jnp.int16(i), roll_lanes(fields_ref[f, 8 * g + l8], 2 * i), acc)
+        out_ref[g] = acc
 
 
 def pack_east(fields):
     return pl.pallas_call(
         pack_east_kernel,
-        grid=(G,),
-        in_specs=[pl.BlockSpec((NF, 8, ROWS, COLS), lambda g: (0, g, 0, 0))],
-        out_specs=pl.BlockSpec((1, ROWS, COLS), lambda g: (g, 0, 0)),
+        in_specs=[pl.BlockSpec(memory_space=pltpu.VMEM)],
+        out_specs=pl.BlockSpec(memory_space=pltpu.VMEM),
         out_shape=jax.ShapeDtypeStruct((G, ROWS, COLS), BF16),
         compiler_params=params(),
         name="pack_east",
@@ -84,7 +83,7 @@
         copies[-1].start()
     table.wait()
     pack_plan(shift_ref, mask_ref, matrix_ref)
-    masks = [mask_ref[n] == 1 for n in range(4)]
+    masks = [mask_ref[n] == 1 for n in range(2)]
     zero = jnp.zeros((ROWS, COLS), BF16)
     for g in range(G):
         copies[g].wait()
@@ -94,8 +93,9 @@
                 jnp.concatenate([jnp.where(m, kept_ref[f, level], zero) for m in masks], axis=1) for f in range(NF)
             ]
             wide = jnp.dot(jnp.concatenate(parts, axis=0), matrix_ref[...], preferred_element_type=F32)
-            scratch[l8] = wide
-            pairs = scratch[l8, pl.ds(0, 8 * NF, stride=2), :] + scratch[l8, pl.ds(1, 8 * NF, stride=2), :]
+            scratch[l8, 0] = wide[:, :COLS]
+            scratch[l8, 1] = wide[:, COLS:]
+            pairs = scratch[l8, 0, pl.ds(0, 8 * NF, stride=2), :] + scratch[l8, 1, pl.ds(1, 8 * NF, stride=2), :]
             pairs = pairs.astype(BF16)
             for n in range(NF // 2):
                 west_ref[n, level] = pairs[ROWS * n : ROWS * n + ROWS]
@@ -104,19 +104,15 @@
 def pack_plan(shift_ref, mask_ref, matrix_ref):
     shift = own_shift(shift_ref, lax.axis_index("lon") + 1)
     lane = lane_iota((ROWS, COLS))
-    low = (lax.broadcasted_iota(jnp.int32, (ROWS, COLS), 0) & 1) == 0
-    block = lane >= COLS - 32 * shift
-    single = lane == COLS - 1 - 32 * shift
-    for n, mask in enumerate([m & row for row in (low, ~low) for m in (block, single)]):
-        mask_ref[n] = half_bits(mask)
+    mask_ref[0] = half_bits(lane >= COLS - 32 * shift)
+    mask_ref[1] = half_bits(lane == COLS - 1 - 32 * shift)
     rules = (
-        lambda s, t: s == t,
-        lambda s, t: ((s & 31) == 31) & (t == 31),
-        mirrored,
-        lambda s, t: ((s & 31) == 31) & (t == 30),
+        (lambda s, t: s == t, mirrored),
+        (lambda s, t: ((s & 31) == 31) & (t == 31), lambda s, t: ((s & 31) == 31) & (t == 30)),
     )
-    for n, rule in enumerate(rules):
-        matrix_ref[COLS * n : COLS * n + COLS, :] = lane_matrix(rule)
+    for m, pair in enumerate(rules):
+        for n, rule in enumerate(pair):
+            matrix_ref[COLS * m : COLS * m + COLS, COLS * n : COLS * n + COLS] = lane_matrix(rule)
 
 
 def pack(shift, fields):
@@ -130,9 +126,9 @@
         ],
         scratch_shapes=[
             pltpu.VMEM((ROWS, 32), jnp.int32),
-            pltpu.VMEM((8, NF * ROWS, COLS), F32),
-            pltpu.VMEM((4, ROWS, COLS), jnp.int16),
-            pltpu.VMEM((4 * COLS, COLS), BF16),
+            pltpu.VMEM((8, 2, NF * ROWS, COLS), F32),
+            pltpu.VMEM((2, ROWS, COLS), jnp.int16),
+            pltpu.VMEM((2 * COLS, 2 * COLS), BF16),
             pltpu.SemaphoreType.DMA((G + 1,)),
         ],
         compiler_params=params(),
@@ -251,8 +247,8 @@
 SLOTS = 20
 
 
-def slot_of_lane():
-    return ((lane_iota((8, COLS)) + 3) & (COLS - 1)) // 6
+def slot_of_lane(shape=(8, COLS)):
+    return ((lane_iota(shape) + 3) & (COLS - 1)) // 6
 
 
 def split3(x):
@@ -324,27 +320,25 @@
     in_row = in_row_ref[...].astype(F32)
     covered = covered_ref[...] > 0.5
     nt = (((1,), (1,)), ((), ()))
-    joined = []
-    for lb in range(G):
-        cols = jnp.dot(both_ref[other, lb], pick, preferred_element_type=F32)
-        rep = jnp.zeros((8, 4 * OV), F32)
-        for r in range(ROWS):
-            rep = rep + jnp.where(src_row == r, wgt, 0.0) * cols[8 * r : 8 * r + 8, :]
-        rep = rep[:, :OV] + rep[:, OV : 2 * OV] + rep[:, 2 * OV : 3 * OV] + rep[:, 3 * OV :]
-        spread = in_row * jnp.concatenate([rep] * ROWS, axis=0)
-        values = None
-        for part in split3(spread):
-            value = lax.dot_general(part, place, nt, preferred_element_type=F32)
-            values = value if values is None else values + value
-        joined.append(jnp.where(covered, values, rhs_ref[lb]))
+    halves = jnp.concatenate([both_ref[other, lb] for lb in range(G)], axis=0)
+    cols = jnp.dot(halves, pick, preferred_element_type=F32)
+    rep = jnp.zeros((8 * G, 4 * OV), F32)
+    for r in range(ROWS):
+        weight = jnp.where(src_row == r, wgt, 0.0)
+        rows = [cols[128 * lb + 8 * r : 128 * lb + 8 * r + 8] for lb in range(G)]
+        rep = rep + jnp.concatenate([weight] * G, axis=0) * jnp.concatenate(rows, axis=0)
+    rep = rep[:, :OV] + rep[:, OV : 2 * OV] + rep[:, 2 * OV : 3 * OV] + rep[:, 3 * OV :]
+    spread = jnp.concatenate([in_row * jnp.concatenate([rep[8 * lb : 8 * lb + 8]] * ROWS, axis=0) for lb in range(G)], axis=0)
+    placed = lax.dot_general(jnp.concatenate(split3(spread), axis=0), place, nt, preferred_element_type=F32)
+    placed = placed[:384] + placed[384:768] + placed[768:]
+    joined = [jnp.where(covered, placed[128 * lb : 128 * lb + 128], rhs_ref[lb]) for lb in range(G)]
     levels = jnp.concatenate(
         [jnp.concatenate([joined[lb][8 * r : 8 * r + 8] for lb in range(G)], axis=0) for r in range(ROWS)], axis=1
     )
     modal = jnp.dot(proj_ref[...], levels, precision=lax.Precision.HIGHEST, preferred_element_type=F32)
     for lb in range(G):
         for r in range(ROWS):
-            tile = modal[8 * lb : 8 * lb + 8, COLS * r : COLS * r + COLS]
-            b_ref[lb, 8 * r : 8 * r + 8, :] = tile
+            b_ref[lb, 8 * r : 8 * r + 8, :] = modal[8 * lb : 8 * lb + 8, COLS * r : COLS * r + COLS]
     lat, lon = lax.axis_index("lat"), lax.axis_index("lon")
     place_in_square = 2 * (lat & 1) + (lon & 1)
     for lb in range(G):
@@ -405,20 +399,28 @@
     has_s = jnp.where(lat < lax.axis_size("lat") - 1, one, zero)
     has_w = jnp.where(lon > 0, one, zero)
     has_e = jnp.where(lon < lax.axis_size("lon") - 1, one, zero)
-    lane = lane_iota((8, COLS))
+    shape = (8 * G, COLS)
+    lane = lane_iota(shape)
     first, last = lane == 0, lane == COLS - 1
     side = jnp.where(lane < 64, has_e, has_w)
     here = 2 * (lat & 1) + (lon & 1)
     there = 3 - here
-    lat_even = jnp.broadcast_to(lat & 1, (8, COLS)) == 0
-    slot = slot_of_lane()
+    lat_even = jnp.broadcast_to(lat & 1, shape) == 0
+    slot = slot_of_lane(shape)
     from_east = ((lane % 6) < 3) & (lane < 120)
     north_slot, south_slot = slot < 2, (slot == 18) | (slot == 19)
     inside = jnp.where(from_east, has_e, has_w)
     inside = jnp.where(north_slot, inside * has_n, jnp.where(south_slot, inside * has_s, inside)) > 0.5
     first_side = (lat_even & south_slot) | (~lat_even & north_slot)
     second_side = (lat_even & north_slot) | (~lat_even & south_slot)
-    east_first = jnp.where(from_east, 1, 0) == jnp.broadcast_to(1 - (lon & 1), (8, COLS))
+    east_first = jnp.where(from_east, 1, 0) == jnp.broadcast_to(1 - (lon & 1), shape)
+
+    def rows_of(ref, *at):
+        return jnp.concatenate([ref[(*at[:-1], lb, at[-1])] for lb in range(G)], axis=0)
+
+    def store(ref, j, value):
+        for lb in range(G):
+            ref[lb, 8 * j : 8 * j + 8, :] = value[8 * lb : 8 * lb + 8]
 
     def line(main, ext):
         return roll_lanes(jnp.where(last, ext, main), 1) + roll_lanes(jnp.where(first, ext, main), -1)
@@ -426,62 +428,63 @@
     def row_scale(j):
         return has_n if j < 0 else has_s if j >= ROWS else None
 
+    modes = jnp.broadcast_to(shift_ref[...], (8 * G, LEV))
+    diag = lane_iota((8 * G, LEV)) == lax.broadcasted_iota(jnp.int32, (8 * G, LEV), 0)
+    a = jnp.broadcast_to(4.0 + jnp.sum(jnp.where(diag, modes, 0.0), axis=1, keepdims=True), shape)
+    columns, forwarded = slice(0, 8), slice(24, 32)
+    near = jnp.where(first_side, rows_of(first_ref, here ^ 3, columns), rows_of(first_ref, here ^ 1, columns))
+    near = jnp.where(second_side, rows_of(second_ref, there ^ 2, forwarded), near)
+    far = jnp.where(second_side, rows_of(second_ref, there ^ 3, forwarded), rows_of(second_ref, there ^ 1, forwarded))
+    packed = jnp.where(inside, jnp.where(east_first, near, far), 0.0)
+
+    def b_main(j):
+        if 0 <= j < ROWS:
+            return rows_of(b_ref, slice(8 * j, 8 * j + 8))
+        n = j + 3 if j < 0 else j - ROWS
+        rows = slice(8 * n, 8 * n + 8)
+        one, two = rows_of(first_ref, here ^ 2, rows), rows_of(second_ref, there ^ 2, rows)
+        if j < 0:
+            return jnp.where(has_n > 0.5, jnp.where(lat_even, two, one), 0.0)
+        return jnp.where(has_s > 0.5, jnp.where(lat_even, one, two), 0.0)
+
+    bm = {j: b_main(j) for j in (-3, -2)}
+    bx = {-2: packed}
+    cm, cx, um, ux = {}, {}, {}, {}
+    sums = [jnp.zeros(shape, F32) for _ in range(8)]
+    for j in range(-2, ROWS + 4):
+        if j <= ROWS + 1:
+            bm[j + 1] = b_main(j + 1)
+            if j + 1 <= ROWS + 1:
+                bx[j + 1] = roll_lanes(packed, -6 * (j + 3))
+            value = a * bm[j] - (bm[j - 1] + bm[j + 1] + line(bm[j], bx[j]))
+            scale = row_scale(j)
+            cm[j] = value if scale is None else value * scale
+            if -1 <= j <= ROWS:
+                value = (a * bx[j] - (bx[j - 1] + bx[j + 1] + line(bx[j], bm[j]))) * side
+                cx[j] = value if scale is None else value * scale
+            if 0 <= j < ROWS:
+                store(c_ref, j, cm[j])
+        i = j - 1
+        if -1 <= i <= ROWS:
+            value = 0.25 * (cm[i - 1] + cm[i + 1] + line(cm[i], cx[i]))
+            scale = row_scale(i)
+            um[i] = value if scale is None else value * scale
+            if 0 <= i < ROWS:
+                ux[i] = 0.25 * (cx[i - 1] + cx[i + 1] + line(cx[i], cm[i])) * side
+                store(u1_ref, i, um[i])
+        i = j - 2
+        if 0 <= i < ROWS:
+            u2 = 0.5 * (um[i - 1] + um[i + 1] + line(um[i], ux[i])) - cm[i]
+            store(u2_ref, i, u2)
+            b, c, u1 = b_main(i), cm[i], um[i]
+            pairs = ((b, c), (b, u1), (b, u2), (c, c), (c, u1), (u1, u1), (u1, u2), (u2, u2))
+            sums = [s + x * y for s, (x, y) in zip(sums, pairs)]
+    lane, sub = lane_iota((8, COLS)), lax.broadcasted_iota(jnp.int32, (8, COLS), 0)
     sums_out = jnp.zeros((8, COLS), F32)
-    for lb in range(G):
-        diag = lane_iota((8, LEV)) == (lax.broadcasted_iota(jnp.int32, (8, LEV), 0) + 8 * lb)
-        a = 4.0 + jnp.sum(jnp.where(diag, jnp.broadcast_to(shift_ref[...], (8, LEV)), 0.0), axis=1, keepdims=True)
-        a = jnp.broadcast_to(a, (8, COLS))
-        near = jnp.where(first_side, first_ref[here ^ 3, lb, 0:8, :], first_ref[here ^ 1, lb, 0:8, :])
-        near = jnp.where(second_side, second_ref[there ^ 2, lb, 24:32, :], near)
-        far = jnp.where(second_side, second_ref[there ^ 3, lb, 24:32, :], second_ref[there ^ 1, lb, 24:32, :])
-        packed = jnp.where(inside, jnp.where(east_first, near, far), 0.0)
-
-        def b_main(j):
-            if 0 <= j < ROWS:
-                return b_ref[lb, 8 * j : 8 * j + 8, :]
-            n = j + 3 if j < 0 else j - ROWS
-            rows = slice(8 * n, 8 * n + 8)
-            one, two = first_ref[here ^ 2, lb, rows, :], second_ref[there ^ 2, lb, rows, :]
-            if j < 0:
-                return jnp.where(has_n > 0.5, jnp.where(lat_even, two, one), 0.0)
-            return jnp.where(has_s > 0.5, jnp.where(lat_even, one, two), 0.0)
-
-        bm = {j: b_main(j) for j in (-3, -2)}
-        bx = {-2: packed}
-        cm, cx, um, ux = {}, {}, {}, {}
-        sums = [jnp.zeros((8, COLS), F32) for _ in range(8)]
-        for j in range(-2, ROWS + 4):
-            if j <= ROWS + 1:
-                bm[j + 1] = b_main(j + 1)
-                if j + 1 <= ROWS + 1:
-                    bx[j + 1] = roll_lanes(packed, -6 * (j + 3))
-                value = a * bm[j] - (bm[j - 1] + bm[j + 1] + line(bm[j], bx[j]))
-                scale = row_scale(j)
-                cm[j] = value if scale is None else value * scale
-                if -1 <= j <= ROWS:
-                    value = (a * bx[j] - (bx[j - 1] + bx[j + 1] + line(bx[j], bm[j]))) * side
-                    cx[j] = value if scale is None else value * scale
-                if 0 <= j < ROWS:
-                    c_ref[lb, 8 * j : 8 * j + 8, :] = cm[j]
-            i = j - 1
-            if -1 <= i <= ROWS:
-                value = 0.25 * (cm[i - 1] + cm[i + 1] + line(cm[i], cx[i]))
-                scale = row_scale(i)
-                um[i] = value if scale is None else value * scale
-                if 0 <= i < ROWS:
-                    ux[i] = 0.25 * (cx[i - 1] + cx[i + 1] + line(cx[i], cm[i])) * side
-                    u1_ref[lb, 8 * i : 8 * i + 8, :] = um[i]
-            i = j - 2
-            if 0 <= i < ROWS:
-                u2 = 0.5 * (um[i - 1] + um[i + 1] + line(um[i], ux[i])) - cm[i]
-                u2_ref[lb, 8 * i : 8 * i + 8, :] = u2
-                b, c, u1 = b_main(i), cm[i], um[i]
-                pairs = ((b, c), (b, u1), (b, u2), (c, c), (c, u1), (u1, u1), (u1, u2), (u2, u2))
-                sums = [s + x * y for s, (x, y) in zip(sums, pairs)]
-        for q in range(8):
-            total = jnp.sum(sums[q], axis=1, keepdims=True)
-            sums_out = jnp.where(lane == 8 * lb + q, total, sums_out)
-    sub = lax.broadcasted_iota(jnp.int32, (8, COLS), 0)
+    for q in range(8):
+        total = jnp.sum(sums[q], axis=1, keepdims=True)
+        for lb in range(G):
+            sums_out = jnp.where(lane == 8 * lb + q, total[8 * lb : 8 * lb + 8], sums_out)
     spread = jnp.zeros((8, COLS), F32)
     for m in range(4):
         spread = jnp.where((sub & 3) == m, roll_lanes(sums_out, 32 * m), spread)

time: 84.4 us -> 82.5 us (0.977)
  Pallas kernels: 11.3 us -> 9.23 us
    pallas_call x1, Pallas kernels: 2.7 us -> 1.27 us  [images(): pl.pallas_call(images_kernel, in_specs=[pl.BlockSpec(memory_space=pltpu.V...]
  transfers between devices with their start and end apart: 2 -> 2, of which waited for: 1 -> 1; matrix products, arithmetic and copies ran while one was open for 0% -> 0% of each run, Pallas kernels for 2% -> 1%
where the time goes in v6:
time: 82.5 us; the launch traced here: 82.2 us
  blocking collectives  64.7 us (78%)
  Pallas kernels  9.23 us (11%)
  starting transfers between devices  5.26 us (6%)
  waiting for transfers between devices  1.53 us (2%)
    all_to_all x2, blocking collectives, in_squares(): return lax.all_to_all(slots, ('lat', 'lon'), 0, 0, axis_index_groups=groups)  23.3 us
    all_to_all x1, blocking collectives, per_device(): sums = lax.all_to_all(sums, ('panel', 'lat'), 0, 0)  17.3 us
    all_to_all x1, blocking collectives, per_device(): sums = relay(lax.all_to_all(sums, 'lon', 0, 0), rest)  17.1 us
    all_gather x1, blocking collectives, per_device(): both = lax.all_gather(half, 'panel')  6.96 us
    ppermute x2, starting transfers between devices, send(): lax.ppermute(block, axis, [(i, i + by) for i in range(count) if 0 <= i +...  5.26 us
    pallas_call x1, Pallas kernels, advect(): pl.pallas_call(advect_kernel, in_specs=[whole] * 8, out_specs=[whole] * 3...  2.36 us
    pallas_call x1, Pallas kernels, pack(): pl.pallas_call(pack_kernel, in_specs=[pl.BlockSpec(memory_space=pltpu.HBM...  2.03 us
  transfers between devices with their start and end apart: 2, of which 1 were waited for; matrix products, arithmetic and copies ran while one was open for 0% of the time, Pallas kernels for 1%

profile of v6, /device:TPU:1, one launch (start us, length us, event | category | flops | bytes accessed | tf_op | source)
XLA Modules:
  0.0 82.2 jit_solution(8646757720719669126)
XLA Ops:
  0.6 2.0 %pack.1 = (bf16[3,24,16,128]{3,2,1,0:T(8,128)(2,1)S(1)}, bf16[6,24,16,128]{3,2,1,0:T(8,128)(2,1)S(1)}) custom-call(s32[16,32]{1,0:T(8,128)} %bitcast.17, bf16[6,24,16,128]{3,2,1,0:T(8,128)(2,1)} %bitcast.23), custom_call_target="tpu_custom_call" | custom-call | tf_op jit(solution)/shard_map/pack/pallas_call | solution.py:119
  2.7 4.0 %collective-permute-start = (bf16[3,24,16,128]{3,2,1,0:T(8,128)(2,1)S(1)}, bf16[3,24,16,128]{3,2,1,0:T(8,128)(2,1)S(1)}, u32[]{:S(2)}, u32[]{:S(2)}) collective-permute-start(bf16[3,24,16,128]{3,2,1,0:T(8,128)(2,1)S(1)} %get-tuple-element.37), channel_id=1, source_target_pairs={{0,1},{1,2},{2,3},{3,4},{4,5},{5,6},{6,7},{7,8},{8,9},{9,10},{10,1... | collective-permute-start | bytes 884744 | tf_op jit(solution)/shard_map/ppermute | solution.py:576
  6.6 0.0 copy-start
  6.6 0.0 copy-start.2
  6.7 0.0 copy-start.3
  6.7 0.0 copy-start.4
  6.7 0.0 copy-start.5
  6.7 0.0 copy-start.7
  6.7 0.2 pack_east.1
  6.9 0.0 copy-start.1
  6.9 1.3 %collective-permute-start.1 = (bf16[3,16,128]{2,1,0:T(8,128)(2,1)S(1)}, bf16[3,16,128]{2,1,0:T(8,128)(2,1)S(1)}, u32[]{:S(2)}, u32[]{:S(2)}) collective-permute-start(bf16[3,16,128]{2,1,0:T(8,128)(2,1)S(1)} %pack_east.1), channel_id=1, source_target_pairs={{1,0},{2,1},{3,2},{4,3},{5,4},{6,5},{7,6},{8,7},{9,8},{10,9},{11,1... | collective-permute-start | bytes 36872 | tf_op jit(solution)/shard_map/ppermute | solution.py:576
  8.3 0.6 copy-done.6
  8.9 0.9 %prepare.1 = (f32[6,24,8,128]{3,2,1,0:T(8,128)S(1)}, s16[9,16,128]{2,1,0:T(8,128)(2,1)S(1)}, s32[16,128]{1,0:T(8,128)S(1)}, bf16[4,128,128]{2,1,0:T(8,128)(2,1)S...) custom-call(f32[6,24]{1,0:T(8,128)S(1)} %copy-done.3, ...), custom_call_target="tpu_custom_call" | custom-call | flops 4000000 | bytes 2000000 | tf_op jit(solution)/shard_map/prepare/pallas_call | solution.py:303
  9.8 1.5 %collective-permute-done.1.east_ref = bf16[3,16,128]{2,1,0:T(8,128)(2,1)S(1)} collective-permute-done((bf16[3,16,128]{2,1,0:T(8,128)(2,1)S(1)}, bf16[3,16,128]{2,1,0:T(8,128)(2,1)S(1)}, u32[]{:S(2)}, u32[]{:S(2)}) %collective-permute-start.1) | collective-permute-done | bytes 12320 | tf_op jit(solution)/shard_map/ppermute | solution.py:576
  11.4 2.4 %advect.1 = (bf16[6,24,16,128]{3,2,1,0:T(8,128)(2,1)S(1)}, f32[3,128,128]{2,1,0:T(8,128)S(1)}, bf16[3,128,128]{2,1,0:T(8,128)(2,1)S(1)}) custom-call(f32[6,24,8,128]{3,2,1,0:T(8,128)S(1)} %get-tuple-element.31.mix_ref, s16[9,16,128]{2,1,0:T(8,128)(2,1)S(1)} %get-tuple-element.32.mask_ref, s32[16,128]{1,0:T(8,128)S(1)} %get-tuple-element.33.shift_ref, ...), custom_call_target="tpu_custom_call" | custom-call | tf_op jit(solution)/shard_map/advect/pallas_call | solution.py:232
  13.7 7.0 %all-gather = bf16[6,128,128]{2,1,0:T(8,128)(2,1)S(1)} all-gather(bf16[3,128,128]{2,1,0:T(8,128)(2,1)S(1)} %get-tuple-element.39), channel_id=2, replica_groups=mesh['panel'=2,'lat'=8,'lon'=32] {'panel'}, dimensions={0}, use_global_device_ids=true | all-gather | bytes 294912 | tf_op jit(solution)/shard_map/all_gather | solution.py:614
  20.7 1.3 %margin.1 = (f32[3,128,128]{2,1,0:T(8,128)S(1)}, f32[4,3,24,128]{3,2,1,0:T(8,128)S(1)}) custom-call(f32[3,128,128]{2,1,0:T(8,128)S(1)} %get-tuple-element.38.rhs_ref, bf16[2,3,128,128]{3,2,1,0:T(8,128)(2,1)S(1)} %bitcast.15, bf16[128,1024]{1,0:T(8,128)(2,1)S(1)} %get-tuple-element.40.pick_ref, bf16[128,256]{1,0:T(8,128)(2,1)S(1)} %get-tuple-element.41.place_ref, ...), custom_call_target="tpu_custom_call" | custom-call | tf_op jit(solution)/shard_map/margin/pallas_call | solution.py:355
  22.0 6.6 %all_to_all.20.got_ref.first_ref = f32[4,3,24,128]{3,2,1,0:T(8,128)S(1)} all-to-all(f32[4,3,24,128]{3,2,1,0:T(8,128)S(1)} %get-tuple-element.48.first_ref), channel_id=1, replica_groups={{0,1,32,33},{2,3,34,35},{4,5,36,37},{6,7,38,39},{8,9,40,41},{10,11,42,4..., dimensions={0} | all-to-all | bytes 294912 | tf_op jit(solution)/shard_map/all_to_all | solution.py:601
  28.6 0.1 second.1
  28.7 16.7 %all_to_all.21.second_ref = f32[4,3,32,128]{3,2,1,0:T(8,128)S(1)} all-to-all(f32[4,3,32,128]{3,2,1,0:T(8,128)S(1)} %second.1), channel_id=1, replica_groups={{33,34,65,66},{35,36,67,68},{37,38,69,70},{39,40,71,72},{41,42,73,74},{..., dimensions={0} | all-to-all | bytes 393216 | tf_op jit(solution)/shard_map/all_to_all | solution.py:601
  45.4 1.3 %images.1 = (f32[3,128,128]{2,1,0:T(8,128)S(1)}, f32[3,128,128]{2,1,0:T(8,128)S(1)}, f32[3,128,128]{2,1,0:T(8,128)S(1)}, f32[32,2,128]{2,1,0:T(2,128)S(1)}, bf16[6,24,16,128]{3,2,1,0:T(8,128)(2,1)}) custom-call(f32[1,24]{1,0:T(1,128)S(1)} %get-tuple-element.30.shift_ref, f32[3,128,128]{2,1,0:T(8,128)S(1)} %get-tuple-element.47.b_ref, ...), custom_call_target="tpu_custom_call" | custom-call | tf_op jit(solution)/shard_map/images/pallas_call | solution.py:499
  46.7 17.1 %all_to_all.22.in_ref = f32[32,2,128]{2,1,0:T(2,128)S(1)} all-to-all(f32[32,2,128]{2,1,0:T(2,128)S(1)} %get-tuple-element.51), channel_id=1, replica_groups=mesh['panel'=2,'lat'=8,'lon'=32] {'lon'}, dimensions={0} | all-to-all | bytes 65536 | tf_op jit(solution)/shard_map/all_to_all | solution.py:621
  63.8 17.3 %all_to_all.23.s_ref = f32[16,2,128]{2,1,0:T(2,128)S(1)} all-to-all(f32[16,2,128]{2,1,0:T(2,128)S(1)} %relay.1), channel_id=1, replica_groups=mesh['panel'=2,'lat'=8,'lon'=32] {'panel','lat'}, dimensions={0} | all-to-all | bytes 32768 | tf_op jit(solution)/shard_map/all_to_all | solution.py:622
  81.1 1.1 %iterate.1 = (f32[384,128]{1,0:T(8,128)}, f32[384,128]{1,0:T(8,128)}) custom-call(f32[1,24]{1,0:T(1,128)S(1)} %get-tuple-element.30.shift_ref, f32[16,2,128]{2,1,0:T(2,128)S(1)} %all_to_all.23.s_ref, f32[3,128,128]{2,1,0:T(8,128)S(1)} %get-tuple-element.47.b_ref, f32[3,128,128]{2,1,0:T(8,128)S(1)} %get-tuple-element.52.c_ref, ...), custom_call_target="tpu_custom_call" | custom-call | tf_op jit(solution)/shard_map/iterate/pallas_call | solution.py:566
  (10 shorter events, 0.0 us)
Async XLA Ops:
  2.7 8.7 %collective-permute-start = (bf16[3,24,16,128]{3,2,1,0:T(8,128)(2,1)S(1)}, bf16[3,24,16,128]{3,2,1,0:T(8,128)(2,1)S(1)}, u32[]{:S(2)}, u32[]{:S(2)}) collective-permute-start(bf16[3,24,16,128]{3,2,1,0:T(8,128)(2,1)S(1)} %get-tuple-element.37), channel_id=1, source_target_pairs={{0,1},{1,2},{2,3},{3,4},{4,5},{5,6},{6,7},{7,8},{8,9},{9,10},{10,1... | collective-permute-start | bytes 884744 | tf_op jit(solution)/shard_map/ppermute | solution.py:576
  6.6 1.6 %copy-start = (f32[1,24,16,128]{3,2,1,0:T(8,128)S(1)}, f32[1,24,16,128]{3,2,1,0:T(8,128)}, u32[]{:S(2)}) copy-start(f32[1,24,16,128]{3,2,1,0:T(8,128)} %param.10) | copy-start | bytes 589828
  6.6 1.6 %copy-start.2 = (f32[24,24]{1,0:T(8,128)S(1)}, f32[24,24]{1,0:T(8,128)}, u32[]{:S(2)}) copy-start(f32[24,24]{1,0:T(8,128)} %proj_ref.1) | copy-start | bytes 6916
  6.7 1.6 %copy-start.3 = (f32[6,24]{1,0:T(8,128)S(1)}, f32[6,24]{1,0:T(8,128)}, u32[]{:S(2)}) copy-start(f32[6,24]{1,0:T(8,128)} %mix_ref.1) | copy-start | bytes 1732
  6.7 1.6 %copy-start.4 = (s32[1,1,256,4]{2,3,1,0:T(4,128)S(1)}, s32[1,1,256,4]{2,3,1,0:T(4,128)}, u32[]{:S(2)}) copy-start(s32[1,1,256,4]{2,3,1,0:T(4,128)} %param.16) | copy-start | bytes 12292
  6.7 1.6 %copy-start.5 = (f32[1,1,256,4]{2,3,1,0:T(4,128)S(1)}, f32[1,1,256,4]{2,3,1,0:T(4,128)}, u32[]{:S(2)}) copy-start(f32[1,1,256,4]{2,3,1,0:T(4,128)} %param.17) | copy-start | bytes 12292
  6.7 1.6 %copy-start.7 = (f32[24]{0:T(128)S(1)}, f32[24]{0:T(128)}, u32[]{:S(2)}) copy-start(f32[24]{0:T(128)} %param.14) | copy-start | bytes 292
  6.9 1.4 %copy-start.1 = (s32[1,16,32]{2,1,0:T(8,128)S(1)}, s32[1,16,32]{2,1,0:T(8,128)}, u32[]{:S(2)}) copy-start(s32[1,16,32]{2,1,0:T(8,128)} %param.11) | copy-start | bytes 6148
  6.9 4.4 %collective-permute-start.1 = (bf16[3,16,128]{2,1,0:T(8,128)(2,1)S(1)}, bf16[3,16,128]{2,1,0:T(8,128)(2,1)S(1)}, u32[]{:S(2)}, u32[]{:S(2)}) collective-permute-start(bf16[3,16,128]{2,1,0:T(8,128)(2,1)S(1)} %pack_east.1), channel_id=1, source_target_pairs={{1,0},{2,1},{3,2},{4,3},{5,4},{6,5},{7,6},{8,7},{9,8},{10,9},{11,1... | collective-permute-start | bytes 36872 | tf_op jit(solution)/shard_map/ppermute | solution.py:576
  8.2 0.7 copy-start.6

commit v7 on v6

--- a/solution.py
+++ b/solution.py
@@ -73,32 +73,35 @@
     )(fields)
 
 
+CHUNKS = 1
+PER_CHUNK = LEV // CHUNKS
+
+
 def pack_kernel(shift_hbm, fields_hbm, west_ref, kept_ref, shift_ref, scratch, mask_ref, matrix_ref, sems):
-    table = pltpu.make_async_copy(shift_hbm, shift_ref, sems.at[G])
+    table = pltpu.make_async_copy(shift_hbm, shift_ref, sems.at[CHUNKS])
     table.start()
     copies = []
-    for g in range(G):
-        part = (slice(None), pl.ds(8 * g, 8))
-        copies.append(pltpu.make_async_copy(fields_hbm.at[part], kept_ref.at[part], sems.at[g]))
+    for n in range(CHUNKS):
+        part = (slice(None), pl.ds(PER_CHUNK * n, PER_CHUNK))
+        copies.append(pltpu.make_async_copy(fields_hbm.at[part], kept_ref.at[part], sems.at[n]))
         copies[-1].start()
     table.wait()
     pack_plan(shift_ref, mask_ref, matrix_ref)
     masks = [mask_ref[n] == 1 for n in range(2)]
     zero = jnp.zeros((ROWS, COLS), BF16)
-    for g in range(G):
-        copies[g].wait()
-        for l8 in range(8):
-            level = 8 * g + l8
+    low = (lax.broadcasted_iota(jnp.int32, (NF * ROWS, COLS), 0) & 1) == 0
+    for n in range(CHUNKS):
+        copies[n].wait()
+        for level in range(PER_CHUNK * n, PER_CHUNK * n + PER_CHUNK):
             parts = [
                 jnp.concatenate([jnp.where(m, kept_ref[f, level], zero) for m in masks], axis=1) for f in range(NF)
             ]
             wide = jnp.dot(jnp.concatenate(parts, axis=0), matrix_ref[...], preferred_element_type=F32)
-            scratch[l8, 0] = wide[:, :COLS]
-            scratch[l8, 1] = wide[:, COLS:]
-            pairs = scratch[l8, 0, pl.ds(0, 8 * NF, stride=2), :] + scratch[l8, 1, pl.ds(1, 8 * NF, stride=2), :]
+            scratch[level % 8] = jnp.where(low, wide[:, :COLS], wide[:, COLS:])
+            pairs = scratch[level % 8, pl.ds(0, 8 * NF, stride=2), :] + scratch[level % 8, pl.ds(1, 8 * NF, stride=2), :]
             pairs = pairs.astype(BF16)
-            for n in range(NF // 2):
-                west_ref[n, level] = pairs[ROWS * n : ROWS * n + ROWS]
+            for m in range(NF // 2):
+                west_ref[m, level] = pairs[ROWS * m : ROWS * m + ROWS]
 
 
 def pack_plan(shift_ref, mask_ref, matrix_ref):
@@ -126,10 +129,10 @@
         ],
         scratch_shapes=[
             pltpu.VMEM((ROWS, 32), jnp.int32),
-            pltpu.VMEM((8, 2, NF * ROWS, COLS), F32),
+            pltpu.VMEM((8, NF * ROWS, COLS), F32),
             pltpu.VMEM((2, ROWS, COLS), jnp.int16),
             pltpu.VMEM((2 * COLS, 2 * COLS), BF16),
-            pltpu.SemaphoreType.DMA((G + 1,)),
+            pltpu.SemaphoreType.DMA((CHUNKS + 1,)),
         ],
         compiler_params=params(),
         name="pack",
@@ -183,47 +186,52 @@
     odd, two = (shift & 1) == 1, (shift & 2) == 2
     bits = [mask_ref[n] == 1 for n in range(9)]
     masks, (odd16, two16, edge16, swap16, single16) = bits[:4], bits[4:]
-    single_at = jnp.concatenate([lane == ((COLS - 32 * shift) & (COLS - 1))] * NF, axis=0)
+    single_at = lane == ((COLS - 32 * shift) & (COLS - 1))
     zero = jnp.zeros((ROWS, COLS), BF16)
 
     @pl.loop(0, G)
     def _(g):
         east = east_ref[g]
-        for l8 in range(8):
-            level = g * 8 + l8
-            shared = jnp.concatenate([west_ref[n, level] for n in range(NF // 2)], axis=0).astype(F32)
-            scratch[l8, pl.ds(0, 8 * NF, stride=2), :] = shared
-            scratch[l8, pl.ds(1, 8 * NF, stride=2), :] = shared
-            west = scratch[l8].astype(BF16)
+        for batch in (range(8),):
             chosen = [[] for _ in TAPS]
             singles = []
-            for f in range(NF):
-                other = west[ROWS * f : ROWS * f + ROWS]
-                singles.append(jnp.where(single16, other, zero))
-                other = jnp.where(swap16, roll_lanes(other, 64), other)
-                other = jnp.where(edge16, roll_lanes(east, -2 * (f * 8 + l8)), other)
-                own = fields_ref[f, level]
-                for n, mask in enumerate(masks):
-                    chosen[n].append(jnp.where(mask, other, own))
-            moved = [None] * 4
-            moved[1] = [part.astype(F32) for part in chosen[1]]
-            for n, tap in ((0, 0), (1, 2), (2, 3)):
-                wide = jnp.dot(jnp.concatenate(chosen[tap], axis=0), matrix_ref[n], preferred_element_type=F32)
-                if tap == 0:
-                    column = jnp.dot(jnp.concatenate(singles, axis=0), matrix_ref[3], preferred_element_type=F32)
-                    wide = jnp.where(single_at, column, wide)
-                moved[tap] = [wide[ROWS * f : ROWS * f + ROWS] for f in range(NF)]
-            weights = [weight_ref[n, level] for n in range(4)]
-            total = jnp.zeros((ROWS, COLS), F32)
-            for f in range(NF):
-                acc = weights[0] * moved[0][f]
-                for n in range(1, 4):
-                    acc = acc + weights[n] * moved[n][f]
-                rounded = acc.astype(BF16)
-                adv_ref[f, level] = turn(rounded, 1, odd16, two16)
-                mix = mix_ref[f, level]
-                total = total + jnp.concatenate([mix, mix], axis=0) * rounded.astype(F32)
-            rhs_ref[g, pl.ds(l8, ROWS, stride=8), :] = turn(total, 1, odd, two)
+            for l8 in batch:
+                level = g * 8 + l8
+                shared = jnp.concatenate([west_ref[n, level] for n in range(NF // 2)], axis=0).astype(F32)
+                scratch[l8, pl.ds(0, 8 * NF, stride=2), :] = shared
+                scratch[l8, pl.ds(1, 8 * NF, stride=2), :] = shared
+            for l8 in batch:
+                level = g * 8 + l8
+                west = scratch[l8].astype(BF16)
+                for f in range(NF):
+                    other = west[ROWS * f : ROWS * f + ROWS]
+                    singles.append(jnp.where(single16, other, zero))
+                    other = jnp.where(swap16, roll_lanes(other, 64), other)
+                    other = jnp.where(edge16, roll_lanes(east, -2 * (f * 8 + l8)), other)
+                    own = fields_ref[f, level]
+                    for n, mask in enumerate(masks):
+                        chosen[n].append(jnp.where(mask, other, own))
+            wide = [
+                jnp.dot(jnp.concatenate(chosen[tap], axis=0), matrix_ref[n], preferred_element_type=F32)
+                for n, tap in ((0, 0), (1, 2), (2, 3))
+            ]
+            column = jnp.dot(jnp.concatenate(singles, axis=0), matrix_ref[3], preferred_element_type=F32)
+            for k, l8 in enumerate(batch):
+                level = g * 8 + l8
+                weights = [weight_ref[n, level] for n in range(4)]
+                total = jnp.zeros((ROWS, COLS), F32)
+                for f in range(NF):
+                    i = k * NF + f
+                    at = slice(ROWS * i, ROWS * i + ROWS)
+                    acc = weights[0] * jnp.where(single_at, column[at], wide[0][at])
+                    acc = acc + weights[1] * chosen[1][i].astype(F32)
+                    acc = acc + weights[2] * wide[1][at]
+                    acc = acc + weights[3] * wide[2][at]
+                    rounded = acc.astype(BF16)
+                    adv_ref[f, level] = turn(rounded, 1, odd16, two16)
+                    mix = mix_ref[f, level]
+                    total = total + jnp.concatenate([mix, mix], axis=0) * rounded.astype(F32)
+                rhs_ref[g, pl.ds(l8, ROWS, stride=8), :] = turn(total, 1, odd, two)
         half_ref[g] = rhs_ref[g].astype(BF16)
 
 

time: 82.5 us -> 82.1 us (level)
  no operation moved by 1% of the time
where the time goes in v7:
time: 82.1 us; the launch traced here: 81.8 us
  blocking collectives  64.7 us (79%)
  Pallas kernels  8.82 us (11%)
  starting transfers between devices  5.25 us (6%)
  waiting for transfers between devices  1.53 us (2%)
    all_to_all x2, blocking collectives, in_squares(): return lax.all_to_all(slots, ('lat', 'lon'), 0, 0, axis_index_groups=groups)  23.3 us
    all_to_all x1, blocking collectives, per_device(): sums = lax.all_to_all(sums, ('panel', 'lat'), 0, 0)  17.3 us
    all_to_all x1, blocking collectives, per_device(): sums = relay(lax.all_to_all(sums, 'lon', 0, 0), rest)  17.1 us
    all_gather x1, blocking collectives, per_device(): both = lax.all_gather(half, 'panel')  6.96 us
    ppermute x2, starting transfers between devices, send(): lax.ppermute(block, axis, [(i, i + by) for i in range(count) if 0 <= i +...  5.25 us
    pallas_call x1, Pallas kernels, advect(): pl.pallas_call(advect_kernel, in_specs=[whole] * 8, out_specs=[whole] * 3...  2.12 us
    pallas_call x1, Pallas kernels, pack(): pl.pallas_call(pack_kernel, in_specs=[pl.BlockSpec(memory_space=pltpu.HBM...  1.87 us
  transfers between devices with their start and end apart: 2, of which 1 were waited for; matrix products, arithmetic and copies ran while one was open for 0% of the time, Pallas kernels for 1%

profile of v7, /device:TPU:1, one launch (start us, length us, event | category | flops | bytes accessed | tf_op | source)
XLA Modules:
  0.0 81.8 jit_solution(3873303984469024696)
XLA Ops:
  0.6 1.9 %pack.1 = (bf16[3,24,16,128]{3,2,1,0:T(8,128)(2,1)S(1)}, bf16[6,24,16,128]{3,2,1,0:T(8,128)(2,1)S(1)}) custom-call(s32[16,32]{1,0:T(8,128)} %bitcast.17, bf16[6,24,16,128]{3,2,1,0:T(8,128)(2,1)} %bitcast.23), custom_call_target="tpu_custom_call" | custom-call | tf_op jit(solution)/shard_map/pack/pallas_call | solution.py:122
  2.5 4.0 %collective-permute-start = (bf16[3,24,16,128]{3,2,1,0:T(8,128)(2,1)S(1)}, bf16[3,24,16,128]{3,2,1,0:T(8,128)(2,1)S(1)}, u32[]{:S(2)}, u32[]{:S(2)}) collective-permute-start(bf16[3,24,16,128]{3,2,1,0:T(8,128)(2,1)S(1)} %get-tuple-element.37), channel_id=1, source_target_pairs={{0,1},{1,2},{2,3},{3,4},{4,5},{5,6},{6,7},{7,8},{8,9},{9,10},{10,1... | collective-permute-start | bytes 884744 | tf_op jit(solution)/shard_map/ppermute | solution.py:584
  6.5 0.0 copy-start
  6.5 0.0 copy-start.2
  6.5 0.0 copy-start.3
  6.5 0.0 copy-start.4
  6.5 0.0 copy-start.5
  6.6 0.2 pack_east.1
  6.8 0.0 copy-start.1
  6.8 1.3 %collective-permute-start.1 = (bf16[3,16,128]{2,1,0:T(8,128)(2,1)S(1)}, bf16[3,16,128]{2,1,0:T(8,128)(2,1)S(1)}, u32[]{:S(2)}, u32[]{:S(2)}) collective-permute-start(bf16[3,16,128]{2,1,0:T(8,128)(2,1)S(1)} %pack_east.1), channel_id=1, source_target_pairs={{1,0},{2,1},{3,2},{4,3},{5,4},{6,5},{7,6},{8,7},{9,8},{10,9},{11,1... | collective-permute-start | bytes 36872 | tf_op jit(solution)/shard_map/ppermute | solution.py:584
  8.1 0.0 copy-start.6
  8.2 0.6 copy-done.6
  8.8 0.9 %prepare.1 = (f32[6,24,8,128]{3,2,1,0:T(8,128)S(1)}, s16[9,16,128]{2,1,0:T(8,128)(2,1)S(1)}, s32[16,128]{1,0:T(8,128)S(1)}, bf16[4,128,128]{2,1,0:T(8,128)(2,1)S...) custom-call(f32[6,24]{1,0:T(8,128)S(1)} %copy-done.3, ...), custom_call_target="tpu_custom_call" | custom-call | flops 4000000 | bytes 2000000 | tf_op jit(solution)/shard_map/prepare/pallas_call | solution.py:311
  9.7 1.5 %collective-permute-done.1.east_ref = bf16[3,16,128]{2,1,0:T(8,128)(2,1)S(1)} collective-permute-done((bf16[3,16,128]{2,1,0:T(8,128)(2,1)S(1)}, bf16[3,16,128]{2,1,0:T(8,128)(2,1)S(1)}, u32[]{:S(2)}, u32[]{:S(2)}) %collective-permute-start.1) | collective-permute-done | bytes 12320 | tf_op jit(solution)/shard_map/ppermute | solution.py:584
  11.2 2.1 %advect.1 = (bf16[6,24,16,128]{3,2,1,0:T(8,128)(2,1)S(1)}, f32[3,128,128]{2,1,0:T(8,128)S(1)}, bf16[3,128,128]{2,1,0:T(8,128)(2,1)S(1)}) custom-call(f32[6,24,8,128]{3,2,1,0:T(8,128)S(1)} %get-tuple-element.31.mix_ref, s16[9,16,128]{2,1,0:T(8,128)(2,1)S(1)} %get-tuple-element.32.mask_ref, s32[16,128]{1,0:T(8,128)S(1)} %get-tuple-element.33.shift_ref, ...), custom_call_target="tpu_custom_call" | custom-call | tf_op jit(solution)/shard_map/advect/pallas_call | solution.py:240
  13.3 7.0 %all-gather = bf16[6,128,128]{2,1,0:T(8,128)(2,1)S(1)} all-gather(bf16[3,128,128]{2,1,0:T(8,128)(2,1)S(1)} %get-tuple-element.39), channel_id=2, replica_groups=mesh['panel'=2,'lat'=8,'lon'=32] {'panel'}, dimensions={0}, use_global_device_ids=true | all-gather | bytes 294912 | tf_op jit(solution)/shard_map/all_gather | solution.py:622
  20.3 1.3 %margin.1 = (f32[3,128,128]{2,1,0:T(8,128)S(1)}, f32[4,3,24,128]{3,2,1,0:T(8,128)S(1)}) custom-call(f32[3,128,128]{2,1,0:T(8,128)S(1)} %get-tuple-element.38.rhs_ref, bf16[2,3,128,128]{3,2,1,0:T(8,128)(2,1)S(1)} %bitcast.15, bf16[128,1024]{1,0:T(8,128)(2,1)S(1)} %get-tuple-element.40.pick_ref, bf16[128,256]{1,0:T(8,128)(2,1)S(1)} %get-tuple-element.41.place_ref, ...), custom_call_target="tpu_custom_call" | custom-call | tf_op jit(solution)/shard_map/margin/pallas_call | solution.py:363
  21.6 6.6 %all_to_all.20.got_ref.first_ref = f32[4,3,24,128]{3,2,1,0:T(8,128)S(1)} all-to-all(f32[4,3,24,128]{3,2,1,0:T(8,128)S(1)} %get-tuple-element.48.first_ref), channel_id=1, replica_groups={{0,1,32,33},{2,3,34,35},{4,5,36,37},{6,7,38,39},{8,9,40,41},{10,11,42,4..., dimensions={0} | all-to-all | bytes 294912 | tf_op jit(solution)/shard_map/all_to_all | solution.py:609
  28.2 0.1 second.1
  28.3 16.7 %all_to_all.21.second_ref = f32[4,3,32,128]{3,2,1,0:T(8,128)S(1)} all-to-all(f32[4,3,32,128]{3,2,1,0:T(8,128)S(1)} %second.1), channel_id=1, replica_groups={{33,34,65,66},{35,36,67,68},{37,38,69,70},{39,40,71,72},{41,42,73,74},{..., dimensions={0} | all-to-all | bytes 393216 | tf_op jit(solution)/shard_map/all_to_all | solution.py:609
  45.0 1.3 %images.1 = (f32[3,128,128]{2,1,0:T(8,128)S(1)}, f32[3,128,128]{2,1,0:T(8,128)S(1)}, f32[3,128,128]{2,1,0:T(8,128)S(1)}, f32[32,2,128]{2,1,0:T(2,128)S(1)}, bf16[6,24,16,128]{3,2,1,0:T(8,128)(2,1)}) custom-call(f32[1,24]{1,0:T(1,128)S(1)} %get-tuple-element.30.shift_ref, f32[3,128,128]{2,1,0:T(8,128)S(1)} %get-tuple-element.47.b_ref, ...), custom_call_target="tpu_custom_call" | custom-call | tf_op jit(solution)/shard_map/images/pallas_call | solution.py:507
  46.3 17.1 %all_to_all.22.in_ref = f32[32,2,128]{2,1,0:T(2,128)S(1)} all-to-all(f32[32,2,128]{2,1,0:T(2,128)S(1)} %get-tuple-element.51), channel_id=1, replica_groups=mesh['panel'=2,'lat'=8,'lon'=32] {'lon'}, dimensions={0} | all-to-all | bytes 65536 | tf_op jit(solution)/shard_map/all_to_all | solution.py:629
  63.4 17.3 %all_to_all.23.s_ref = f32[16,2,128]{2,1,0:T(2,128)S(1)} all-to-all(f32[16,2,128]{2,1,0:T(2,128)S(1)} %relay.1), channel_id=1, replica_groups=mesh['panel'=2,'lat'=8,'lon'=32] {'panel','lat'}, dimensions={0} | all-to-all | bytes 32768 | tf_op jit(solution)/shard_map/all_to_all | solution.py:630
  80.7 1.1 %iterate.1 = (f32[384,128]{1,0:T(8,128)}, f32[384,128]{1,0:T(8,128)}) custom-call(f32[1,24]{1,0:T(1,128)S(1)} %get-tuple-element.30.shift_ref, f32[16,2,128]{2,1,0:T(2,128)S(1)} %all_to_all.23.s_ref, f32[3,128,128]{2,1,0:T(8,128)S(1)} %get-tuple-element.47.b_ref, f32[3,128,128]{2,1,0:T(8,128)S(1)} %get-tuple-element.52.c_ref, ...), custom_call_target="tpu_custom_call" | custom-call | tf_op jit(solution)/shard_map/iterate/pallas_call | solution.py:574
  (10 shorter events, 0.0 us)
Async XLA Ops:
  2.5 8.7 %collective-permute-start = (bf16[3,24,16,128]{3,2,1,0:T(8,128)(2,1)S(1)}, bf16[3,24,16,128]{3,2,1,0:T(8,128)(2,1)S(1)}, u32[]{:S(2)}, u32[]{:S(2)}) collective-permute-start(bf16[3,24,16,128]{3,2,1,0:T(8,128)(2,1)S(1)} %get-tuple-element.37), channel_id=1, source_target_pairs={{0,1},{1,2},{2,3},{3,4},{4,5},{5,6},{6,7},{7,8},{8,9},{9,10},{10,1... | collective-permute-start | bytes 884744 | tf_op jit(solution)/shard_map/ppermute | solution.py:584
  6.5 1.6 %copy-start = (f32[1,24,16,128]{3,2,1,0:T(8,128)S(1)}, f32[1,24,16,128]{3,2,1,0:T(8,128)}, u32[]{:S(2)}) copy-start(f32[1,24,16,128]{3,2,1,0:T(8,128)} %param.10) | copy-start | bytes 589828
  6.5 1.6 %copy-start.2 = (f32[24,24]{1,0:T(8,128)S(1)}, f32[24,24]{1,0:T(8,128)}, u32[]{:S(2)}) copy-start(f32[24,24]{1,0:T(8,128)} %proj_ref.1) | copy-start | bytes 6916
  6.5 1.6 %copy-start.3 = (f32[6,24]{1,0:T(8,128)S(1)}, f32[6,24]{1,0:T(8,128)}, u32[]{:S(2)}) copy-start(f32[6,24]{1,0:T(8,128)} %mix_ref.1) | copy-start | bytes 1732
  6.5 1.6 %copy-start.4 = (s32[1,1,256,4]{2,3,1,0:T(4,128)S(1)}, s32[1,1,256,4]{2,3,1,0:T(4,128)}, u32[]{:S(2)}) copy-start(s32[1,1,256,4]{2,3,1,0:T(4,128)} %param.16) | copy-start | bytes 12292
  6.5 1.6 %copy-start.5 = (f32[1,1,256,4]{2,3,1,0:T(4,128)S(1)}, f32[1,1,256,4]{2,3,1,0:T(4,128)}, u32[]{:S(2)}) copy-start(f32[1,1,256,4]{2,3,1,0:T(4,128)} %param.17) | copy-start | bytes 12292
  6.5 1.6 %copy-start.7 = (f32[24]{0:T(128)S(1)}, f32[24]{0:T(128)}, u32[]{:S(2)}) copy-start(f32[24]{0:T(128)} %param.14) | copy-start | bytes 292
  6.8 1.4 %copy-start.1 = (s32[1,16,32]{2,1,0:T(8,128)S(1)}, s32[1,16,32]{2,1,0:T(8,128)}, u32[]{:S(2)}) copy-start(s32[1,16,32]{2,1,0:T(8,128)} %param.11) | copy-start | bytes 6148
  6.8 4.4 %collective-permute-start.1 = (bf16[3,16,128]{2,1,0:T(8,128)(2,1)S(1)}, bf16[3,16,128]{2,1,0:T(8,128)(2,1)S(1)}, u32[]{:S(2)}, u32[]{:S(2)}) collective-permute-start(bf16[3,16,128]{2,1,0:T(8,128)(2,1)S(1)} %pack_east.1), channel_id=1, source_target_pairs={{1,0},{2,1},{3,2},{4,3},{5,4},{6,5},{7,6},{8,7},{9,8},{10,9},{11,1... | collective-permute-start | bytes 36872 | tf_op jit(solution)/shard_map/ppermute | solution.py:584
  8.1 0.7 copy-start.6

commit v8 on v7

--- a/solution.py
+++ b/solution.py
@@ -625,9 +625,9 @@
     got_second = in_squares(second(b, first, got_first), 1)
     count = lax.axis_size("lon")
     rest = lax.axis_size("panel") * lax.axis_size("lat")
-    c, u1, u2, sums, adv = images(modes, b, got_first, got_second, adv, count)
-    sums = relay(lax.all_to_all(sums, "lon", 0, 0), rest)
-    sums = lax.all_to_all(sums, ("panel", "lat"), 0, 0)
+    c, u1, u2, sums, adv = images(modes, b, got_first, got_second, adv, rest)
+    sums = relay(lax.all_to_all(sums, ("panel", "lat"), 0, 0), count)
+    sums = lax.all_to_all(sums, "lon", 0, 0)
     sol, res = iterate(modes, sums, b, c, u1, u2)
     shape = (1, LEV, ROWS, COLS)
     return adv[None], sol.reshape(shape), res.reshape(shape)

time: 82.1 us -> 80.7 us (0.983)
  blocking collectives: 64.7 us -> 63.3 us
    all_to_all x2, blocking collectives: 34.4 us -> 33 us  [the longest x1 18.4 us: per_device(): sums = lax.all_to_all(sums, 'lon', 0, 0)]
where the time goes in v8:
time: 80.7 us; the launch traced here: 80.3 us
  blocking collectives  63.3 us (78%)
  Pallas kernels  8.82 us (11%)
  starting transfers between devices  5.25 us (7%)
  waiting for transfers between devices  1.53 us (2%)
  between operations  0.81 us (1%)
    all_to_all x2, blocking collectives, in_squares(): return lax.all_to_all(slots, ('lat', 'lon'), 0, 0, axis_index_groups=groups)  23.3 us
    all_to_all x1, blocking collectives, per_device(): sums = lax.all_to_all(sums, 'lon', 0, 0)  18.4 us
    all_to_all x1, blocking collectives, per_device(): sums = relay(lax.all_to_all(sums, ('panel', 'lat'), 0, 0), count)  14.5 us
    all_gather x1, blocking collectives, per_device(): both = lax.all_gather(half, 'panel')  6.96 us
    ppermute x2, starting transfers between devices, send(): lax.ppermute(block, axis, [(i, i + by) for i in range(count) if 0 <= i +...  5.25 us
    pallas_call x1, Pallas kernels, advect(): pl.pallas_call(advect_kernel, in_specs=[whole] * 8, out_specs=[whole] * 3...  2.12 us
    pallas_call x1, Pallas kernels, pack(): pl.pallas_call(pack_kernel, in_specs=[pl.BlockSpec(memory_space=pltpu.HBM...  1.87 us
  transfers between devices with their start and end apart: 2, of which 1 were waited for; matrix products, arithmetic and copies ran while one was open for 0% of the time, Pallas kernels for 1%

profile of v8, /device:TPU:1, one launch (start us, length us, event | category | flops | bytes accessed | tf_op | source)
XLA Modules:
  0.0 80.3 jit_solution(18254955839372444560)
XLA Ops:
  0.6 1.9 %pack.1 = (bf16[3,24,16,128]{3,2,1,0:T(8,128)(2,1)S(1)}, bf16[6,24,16,128]{3,2,1,0:T(8,128)(2,1)S(1)}) custom-call(s32[16,32]{1,0:T(8,128)} %bitcast.17, bf16[6,24,16,128]{3,2,1,0:T(8,128)(2,1)} %bitcast.23), custom_call_target="tpu_custom_call" | custom-call | tf_op jit(solution)/shard_map/pack/pallas_call | solution.py:122
  2.5 4.0 %collective-permute-start = (bf16[3,24,16,128]{3,2,1,0:T(8,128)(2,1)S(1)}, bf16[3,24,16,128]{3,2,1,0:T(8,128)(2,1)S(1)}, u32[]{:S(2)}, u32[]{:S(2)}) collective-permute-start(bf16[3,24,16,128]{3,2,1,0:T(8,128)(2,1)S(1)} %get-tuple-element.37), channel_id=1, source_target_pairs={{0,1},{1,2},{2,3},{3,4},{4,5},{5,6},{6,7},{7,8},{8,9},{9,10},{10,1... | collective-permute-start | bytes 884744 | tf_op jit(solution)/shard_map/ppermute | solution.py:584
  6.5 0.0 copy-start
  6.5 0.0 copy-start.2
  6.5 0.0 copy-start.3
  6.5 0.0 copy-start.4
  6.5 0.0 copy-start.5
  6.6 0.2 pack_east.1
  6.8 0.0 copy-start.1
  6.8 1.3 %collective-permute-start.1 = (bf16[3,16,128]{2,1,0:T(8,128)(2,1)S(1)}, bf16[3,16,128]{2,1,0:T(8,128)(2,1)S(1)}, u32[]{:S(2)}, u32[]{:S(2)}) collective-permute-start(bf16[3,16,128]{2,1,0:T(8,128)(2,1)S(1)} %pack_east.1), channel_id=1, source_target_pairs={{1,0},{2,1},{3,2},{4,3},{5,4},{6,5},{7,6},{8,7},{9,8},{10,9},{11,1... | collective-permute-start | bytes 36872 | tf_op jit(solution)/shard_map/ppermute | solution.py:584
  8.1 0.0 copy-start.6
  8.2 0.6 copy-done.6
  8.8 0.9 %prepare.1 = (f32[6,24,8,128]{3,2,1,0:T(8,128)S(1)}, s16[9,16,128]{2,1,0:T(8,128)(2,1)S(1)}, s32[16,128]{1,0:T(8,128)S(1)}, bf16[4,128,128]{2,1,0:T(8,128)(2,1)S...) custom-call(f32[6,24]{1,0:T(8,128)S(1)} %copy-done.3, ...), custom_call_target="tpu_custom_call" | custom-call | flops 4000000 | bytes 2000000 | tf_op jit(solution)/shard_map/prepare/pallas_call | solution.py:311
  9.7 1.5 %collective-permute-done.1.east_ref = bf16[3,16,128]{2,1,0:T(8,128)(2,1)S(1)} collective-permute-done((bf16[3,16,128]{2,1,0:T(8,128)(2,1)S(1)}, bf16[3,16,128]{2,1,0:T(8,128)(2,1)S(1)}, u32[]{:S(2)}, u32[]{:S(2)}) %collective-permute-start.1) | collective-permute-done | bytes 12320 | tf_op jit(solution)/shard_map/ppermute | solution.py:584
  11.2 2.1 %advect.1 = (bf16[6,24,16,128]{3,2,1,0:T(8,128)(2,1)S(1)}, f32[3,128,128]{2,1,0:T(8,128)S(1)}, bf16[3,128,128]{2,1,0:T(8,128)(2,1)S(1)}) custom-call(f32[6,24,8,128]{3,2,1,0:T(8,128)S(1)} %get-tuple-element.31.mix_ref, s16[9,16,128]{2,1,0:T(8,128)(2,1)S(1)} %get-tuple-element.32.mask_ref, s32[16,128]{1,0:T(8,128)S(1)} %get-tuple-element.33.shift_ref, ...), custom_call_target="tpu_custom_call" | custom-call | tf_op jit(solution)/shard_map/advect/pallas_call | solution.py:240
  13.3 7.0 %all-gather = bf16[6,128,128]{2,1,0:T(8,128)(2,1)S(1)} all-gather(bf16[3,128,128]{2,1,0:T(8,128)(2,1)S(1)} %get-tuple-element.39), channel_id=2, replica_groups=mesh['panel'=2,'lat'=8,'lon'=32] {'panel'}, dimensions={0}, use_global_device_ids=true | all-gather | bytes 294912 | tf_op jit(solution)/shard_map/all_gather | solution.py:622
  20.3 1.3 %margin.1 = (f32[3,128,128]{2,1,0:T(8,128)S(1)}, f32[4,3,24,128]{3,2,1,0:T(8,128)S(1)}) custom-call(f32[3,128,128]{2,1,0:T(8,128)S(1)} %get-tuple-element.38.rhs_ref, bf16[2,3,128,128]{3,2,1,0:T(8,128)(2,1)S(1)} %bitcast.15, bf16[128,1024]{1,0:T(8,128)(2,1)S(1)} %get-tuple-element.40.pick_ref, bf16[128,256]{1,0:T(8,128)(2,1)S(1)} %get-tuple-element.41.place_ref, ...), custom_call_target="tpu_custom_call" | custom-call | tf_op jit(solution)/shard_map/margin/pallas_call | solution.py:363
  21.6 6.6 %all_to_all.20.got_ref.first_ref = f32[4,3,24,128]{3,2,1,0:T(8,128)S(1)} all-to-all(f32[4,3,24,128]{3,2,1,0:T(8,128)S(1)} %get-tuple-element.48.first_ref), channel_id=1, replica_groups={{0,1,32,33},{2,3,34,35},{4,5,36,37},{6,7,38,39},{8,9,40,41},{10,11,42,4..., dimensions={0} | all-to-all | bytes 294912 | tf_op jit(solution)/shard_map/all_to_all | solution.py:609
  28.2 0.1 second.1
  28.3 16.7 %all_to_all.21.second_ref = f32[4,3,32,128]{3,2,1,0:T(8,128)S(1)} all-to-all(f32[4,3,32,128]{3,2,1,0:T(8,128)S(1)} %second.1), channel_id=1, replica_groups={{33,34,65,66},{35,36,67,68},{37,38,69,70},{39,40,71,72},{41,42,73,74},{..., dimensions={0} | all-to-all | bytes 393216 | tf_op jit(solution)/shard_map/all_to_all | solution.py:609
  45.0 1.3 %images.1 = (f32[3,128,128]{2,1,0:T(8,128)S(1)}, f32[3,128,128]{2,1,0:T(8,128)S(1)}, f32[3,128,128]{2,1,0:T(8,128)S(1)}, f32[16,2,128]{2,1,0:T(2,128)S(1)}, bf16[6,24,16,128]{3,2,1,0:T(8,128)(2,1)}) custom-call(f32[1,24]{1,0:T(1,128)S(1)} %get-tuple-element.30.shift_ref, f32[3,128,128]{2,1,0:T(8,128)S(1)} %get-tuple-element.47.b_ref, ...), custom_call_target="tpu_custom_call" | custom-call | tf_op jit(solution)/shard_map/images/pallas_call | solution.py:507
  46.3 14.5 %all_to_all.22.in_ref = f32[16,2,128]{2,1,0:T(2,128)S(1)} all-to-all(f32[16,2,128]{2,1,0:T(2,128)S(1)} %get-tuple-element.51), channel_id=1, replica_groups=mesh['panel'=2,'lat'=8,'lon'=32] {'panel','lat'}, dimensions={0} | all-to-all | bytes 32768 | tf_op jit(solution)/shard_map/all_to_all | solution.py:629
  60.8 18.4 %all_to_all.23.s_ref = f32[32,2,128]{2,1,0:T(2,128)S(1)} all-to-all(f32[32,2,128]{2,1,0:T(2,128)S(1)} %relay.1), channel_id=1, replica_groups=mesh['panel'=2,'lat'=8,'lon'=32] {'lon'}, dimensions={0} | all-to-all | bytes 65536 | tf_op jit(solution)/shard_map/all_to_all | solution.py:630
  79.3 1.1 %iterate.1 = (f32[384,128]{1,0:T(8,128)}, f32[384,128]{1,0:T(8,128)}) custom-call(f32[1,24]{1,0:T(1,128)S(1)} %get-tuple-element.30.shift_ref, f32[32,2,128]{2,1,0:T(2,128)S(1)} %all_to_all.23.s_ref, f32[3,128,128]{2,1,0:T(8,128)S(1)} %get-tuple-element.47.b_ref, f32[3,128,128]{2,1,0:T(8,128)S(1)} %get-tuple-element.52.c_ref, ...), custom_call_target="tpu_custom_call" | custom-call | tf_op jit(solution)/shard_map/iterate/pallas_call | solution.py:574
  (10 shorter events, 0.0 us)
Async XLA Ops:
  2.5 8.7 %collective-permute-start = (bf16[3,24,16,128]{3,2,1,0:T(8,128)(2,1)S(1)}, bf16[3,24,16,128]{3,2,1,0:T(8,128)(2,1)S(1)}, u32[]{:S(2)}, u32[]{:S(2)}) collective-permute-start(bf16[3,24,16,128]{3,2,1,0:T(8,128)(2,1)S(1)} %get-tuple-element.37), channel_id=1, source_target_pairs={{0,1},{1,2},{2,3},{3,4},{4,5},{5,6},{6,7},{7,8},{8,9},{9,10},{10,1... | collective-permute-start | bytes 884744 | tf_op jit(solution)/shard_map/ppermute | solution.py:584
  6.5 1.6 %copy-start = (f32[1,24,16,128]{3,2,1,0:T(8,128)S(1)}, f32[1,24,16,128]{3,2,1,0:T(8,128)}, u32[]{:S(2)}) copy-start(f32[1,24,16,128]{3,2,1,0:T(8,128)} %param.10) | copy-start | bytes 589828
  6.5 1.6 %copy-start.2 = (f32[24,24]{1,0:T(8,128)S(1)}, f32[24,24]{1,0:T(8,128)}, u32[]{:S(2)}) copy-start(f32[24,24]{1,0:T(8,128)} %proj_ref.1) | copy-start | bytes 6916
  6.5 1.6 %copy-start.3 = (f32[6,24]{1,0:T(8,128)S(1)}, f32[6,24]{1,0:T(8,128)}, u32[]{:S(2)}) copy-start(f32[6,24]{1,0:T(8,128)} %mix_ref.1) | copy-start | bytes 1732
  6.5 1.6 %copy-start.4 = (s32[1,1,256,4]{2,3,1,0:T(4,128)S(1)}, s32[1,1,256,4]{2,3,1,0:T(4,128)}, u32[]{:S(2)}) copy-start(s32[1,1,256,4]{2,3,1,0:T(4,128)} %param.16) | copy-start | bytes 12292
  6.5 1.6 %copy-start.5 = (f32[1,1,256,4]{2,3,1,0:T(4,128)S(1)}, f32[1,1,256,4]{2,3,1,0:T(4,128)}, u32[]{:S(2)}) copy-start(f32[1,1,256,4]{2,3,1,0:T(4,128)} %param.17) | copy-start | bytes 12292
  6.5 1.6 %copy-start.7 = (f32[24]{0:T(128)S(1)}, f32[24]{0:T(128)}, u32[]{:S(2)}) copy-start(f32[24]{0:T(128)} %param.14) | copy-start | bytes 292
  6.8 1.4 %copy-start.1 = (s32[1,16,32]{2,1,0:T(8,128)S(1)}, s32[1,16,32]{2,1,0:T(8,128)}, u32[]{:S(2)}) copy-start(s32[1,16,32]{2,1,0:T(8,128)} %param.11) | copy-start | bytes 6148
  6.8 4.4 %collective-permute-start.1 = (bf16[3,16,128]{2,1,0:T(8,128)(2,1)S(1)}, bf16[3,16,128]{2,1,0:T(8,128)(2,1)S(1)}, u32[]{:S(2)}, u32[]{:S(2)}) collective-permute-start(bf16[3,16,128]{2,1,0:T(8,128)(2,1)S(1)} %pack_east.1), channel_id=1, source_target_pairs={{1,0},{2,1},{3,2},{4,3},{5,4},{6,5},{7,6},{8,7},{9,8},{10,9},{11,1... | collective-permute-start | bytes 36872 | tf_op jit(solution)/shard_map/ppermute | solution.py:584
  8.1 0.7 copy-start.6

commit v9 on v8

--- a/solution.py
+++ b/solution.py
@@ -73,35 +73,34 @@
     )(fields)
 
 
-CHUNKS = 1
-PER_CHUNK = LEV // CHUNKS
+CHUNKS = NF // 2
 
 
 def pack_kernel(shift_hbm, fields_hbm, west_ref, kept_ref, shift_ref, scratch, mask_ref, matrix_ref, sems):
     table = pltpu.make_async_copy(shift_hbm, shift_ref, sems.at[CHUNKS])
     table.start()
-    copies = []
-    for n in range(CHUNKS):
-        part = (slice(None), pl.ds(PER_CHUNK * n, PER_CHUNK))
-        copies.append(pltpu.make_async_copy(fields_hbm.at[part], kept_ref.at[part], sems.at[n]))
-        copies[-1].start()
+    whole = pltpu.make_async_copy(fields_hbm, kept_ref, sems.at[0])
+    whole.start()
     table.wait()
     pack_plan(shift_ref, mask_ref, matrix_ref)
     masks = [mask_ref[n] == 1 for n in range(2)]
     zero = jnp.zeros((ROWS, COLS), BF16)
-    low = (lax.broadcasted_iota(jnp.int32, (NF * ROWS, COLS), 0) & 1) == 0
+    whole.wait()
+    rows = 8 * 2 * ROWS
+    low = (lax.broadcasted_iota(jnp.int32, (rows, COLS), 0) & 1) == 0
     for n in range(CHUNKS):
-        copies[n].wait()
-        for level in range(PER_CHUNK * n, PER_CHUNK * n + PER_CHUNK):
+        for g in range(G):
             parts = [
-                jnp.concatenate([jnp.where(m, kept_ref[f, level], zero) for m in masks], axis=1) for f in range(NF)
+                jnp.concatenate([jnp.where(m, kept_ref[2 * n + f, 8 * g + l8], zero) for m in masks], axis=1)
+                for l8 in range(8)
+                for f in range(2)
             ]
             wide = jnp.dot(jnp.concatenate(parts, axis=0), matrix_ref[...], preferred_element_type=F32)
-            scratch[level % 8] = jnp.where(low, wide[:, :COLS], wide[:, COLS:])
-            pairs = scratch[level % 8, pl.ds(0, 8 * NF, stride=2), :] + scratch[level % 8, pl.ds(1, 8 * NF, stride=2), :]
+            scratch[g] = jnp.where(low, wide[:, :COLS], wide[:, COLS:])
+            pairs = scratch[g, pl.ds(0, rows // 2, stride=2), :] + scratch[g, pl.ds(1, rows // 2, stride=2), :]
             pairs = pairs.astype(BF16)
-            for m in range(NF // 2):
-                west_ref[m, level] = pairs[ROWS * m : ROWS * m + ROWS]
+            for l8 in range(8):
+                west_ref[n, 8 * g + l8] = pairs[ROWS * l8 : ROWS * l8 + ROWS]
 
 
 def pack_plan(shift_ref, mask_ref, matrix_ref):
@@ -129,7 +128,7 @@
         ],
         scratch_shapes=[
             pltpu.VMEM((ROWS, 32), jnp.int32),
-            pltpu.VMEM((8, NF * ROWS, COLS), F32),
+            pltpu.VMEM((G, 16 * ROWS, COLS), F32),
             pltpu.VMEM((2, ROWS, COLS), jnp.int16),
             pltpu.VMEM((2 * COLS, 2 * COLS), BF16),
             pltpu.SemaphoreType.DMA((CHUNKS + 1,)),

time: 80.7 us -> 80.5 us (level)
  no operation moved by 1% of the time
where the time goes in v9:
time: 80.5 us; the launch traced here: 80.2 us
  blocking collectives  63.3 us (79%)
  Pallas kernels  8.66 us (11%)
  starting transfers between devices  5.25 us (7%)
  waiting for transfers between devices  1.53 us (2%)
  between operations  0.81 us (1%)
    all_to_all x2, blocking collectives, in_squares(): return lax.all_to_all(slots, ('lat', 'lon'), 0, 0, axis_index_groups=groups)  23.3 us
    all_to_all x1, blocking collectives, per_device(): sums = lax.all_to_all(sums, 'lon', 0, 0)  18.4 us
    all_to_all x1, blocking collectives, per_device(): sums = relay(lax.all_to_all(sums, ('panel', 'lat'), 0, 0), count)  14.5 us
    all_gather x1, blocking collectives, per_device(): both = lax.all_gather(half, 'panel')  6.96 us
    ppermute x2, starting transfers between devices, send(): lax.ppermute(block, axis, [(i, i + by) for i in range(count) if 0 <= i +...  5.25 us
    pallas_call x1, Pallas kernels, advect(): pl.pallas_call(advect_kernel, in_specs=[whole] * 8, out_specs=[whole] * 3...  2.12 us
    pallas_call x1, Pallas kernels, pack(): pl.pallas_call(pack_kernel, in_specs=[pl.BlockSpec(memory_space=pltpu.HBM...  1.71 us
  transfers between devices with their start and end apart: 2, of which 1 were waited for; matrix products, arithmetic and copies ran while one was open for 0% of the time, Pallas kernels for 1%

profile of v9, /device:TPU:1, one launch (start us, length us, event | category | flops | bytes accessed | tf_op | source)
XLA Modules:
  0.0 80.2 jit_solution(4053667095559457025)
XLA Ops:
  0.6 1.7 %pack.1 = (bf16[3,24,16,128]{3,2,1,0:T(8,128)(2,1)S(1)}, bf16[6,24,16,128]{3,2,1,0:T(8,128)(2,1)S(1)}) custom-call(s32[16,32]{1,0:T(8,128)} %bitcast.17, bf16[6,24,16,128]{3,2,1,0:T(8,128)(2,1)} %bitcast.23), custom_call_target="tpu_custom_call" | custom-call | tf_op jit(solution)/shard_map/pack/pallas_call | solution.py:121
  2.3 4.0 %collective-permute-start = (bf16[3,24,16,128]{3,2,1,0:T(8,128)(2,1)S(1)}, bf16[3,24,16,128]{3,2,1,0:T(8,128)(2,1)S(1)}, u32[]{:S(2)}, u32[]{:S(2)}) collective-permute-start(bf16[3,24,16,128]{3,2,1,0:T(8,128)(2,1)S(1)} %get-tuple-element.37), channel_id=1, source_target_pairs={{0,1},{1,2},{2,3},{3,4},{4,5},{5,6},{6,7},{7,8},{8,9},{9,10},{10,1... | collective-permute-start | bytes 884744 | tf_op jit(solution)/shard_map/ppermute | solution.py:583
  6.3 0.0 copy-start
  6.3 0.0 copy-start.2
  6.3 0.0 copy-start.3
  6.3 0.0 copy-start.4
  6.4 0.0 copy-start.5
  6.4 0.0 copy-start.7
  6.4 0.2 pack_east.1
  6.6 0.0 copy-start.1
  6.6 1.3 %collective-permute-start.1 = (bf16[3,16,128]{2,1,0:T(8,128)(2,1)S(1)}, bf16[3,16,128]{2,1,0:T(8,128)(2,1)S(1)}, u32[]{:S(2)}, u32[]{:S(2)}) collective-permute-start(bf16[3,16,128]{2,1,0:T(8,128)(2,1)S(1)} %pack_east.1), channel_id=1, source_target_pairs={{1,0},{2,1},{3,2},{4,3},{5,4},{6,5},{7,6},{8,7},{9,8},{10,9},{11,1... | collective-permute-start | bytes 36872 | tf_op jit(solution)/shard_map/ppermute | solution.py:583
  8.0 0.6 copy-done.6
  8.6 0.9 %prepare.1 = (f32[6,24,8,128]{3,2,1,0:T(8,128)S(1)}, s16[9,16,128]{2,1,0:T(8,128)(2,1)S(1)}, s32[16,128]{1,0:T(8,128)S(1)}, bf16[4,128,128]{2,1,0:T(8,128)(2,1)S...) custom-call(f32[6,24]{1,0:T(8,128)S(1)} %copy-done.3, ...), custom_call_target="tpu_custom_call" | custom-call | flops 4000000 | bytes 2000000 | tf_op jit(solution)/shard_map/prepare/pallas_call | solution.py:310
  9.5 1.5 %collective-permute-done.1.east_ref = bf16[3,16,128]{2,1,0:T(8,128)(2,1)S(1)} collective-permute-done((bf16[3,16,128]{2,1,0:T(8,128)(2,1)S(1)}, bf16[3,16,128]{2,1,0:T(8,128)(2,1)S(1)}, u32[]{:S(2)}, u32[]{:S(2)}) %collective-permute-start.1) | collective-permute-done | bytes 12320 | tf_op jit(solution)/shard_map/ppermute | solution.py:583
  11.1 2.1 %advect.1 = (bf16[6,24,16,128]{3,2,1,0:T(8,128)(2,1)S(1)}, f32[3,128,128]{2,1,0:T(8,128)S(1)}, bf16[3,128,128]{2,1,0:T(8,128)(2,1)S(1)}) custom-call(f32[6,24,8,128]{3,2,1,0:T(8,128)S(1)} %get-tuple-element.31.mix_ref, s16[9,16,128]{2,1,0:T(8,128)(2,1)S(1)} %get-tuple-element.32.mask_ref, s32[16,128]{1,0:T(8,128)S(1)} %get-tuple-element.33.shift_ref, ...), custom_call_target="tpu_custom_call" | custom-call | tf_op jit(solution)/shard_map/advect/pallas_call | solution.py:239
  13.2 7.0 %all-gather = bf16[6,128,128]{2,1,0:T(8,128)(2,1)S(1)} all-gather(bf16[3,128,128]{2,1,0:T(8,128)(2,1)S(1)} %get-tuple-element.39), channel_id=2, replica_groups=mesh['panel'=2,'lat'=8,'lon'=32] {'panel'}, dimensions={0}, use_global_device_ids=true | all-gather | bytes 294912 | tf_op jit(solution)/shard_map/all_gather | solution.py:621
  20.1 1.3 %margin.1 = (f32[3,128,128]{2,1,0:T(8,128)S(1)}, f32[4,3,24,128]{3,2,1,0:T(8,128)S(1)}) custom-call(f32[3,128,128]{2,1,0:T(8,128)S(1)} %get-tuple-element.38.rhs_ref, bf16[2,3,128,128]{3,2,1,0:T(8,128)(2,1)S(1)} %bitcast.15, bf16[128,1024]{1,0:T(8,128)(2,1)S(1)} %get-tuple-element.40.pick_ref, bf16[128,256]{1,0:T(8,128)(2,1)S(1)} %get-tuple-element.41.place_ref, ...), custom_call_target="tpu_custom_call" | custom-call | tf_op jit(solution)/shard_map/margin/pallas_call | solution.py:362
  21.4 6.6 %all_to_all.20.got_ref.first_ref = f32[4,3,24,128]{3,2,1,0:T(8,128)S(1)} all-to-all(f32[4,3,24,128]{3,2,1,0:T(8,128)S(1)} %get-tuple-element.48.first_ref), channel_id=1, replica_groups={{0,1,32,33},{2,3,34,35},{4,5,36,37},{6,7,38,39},{8,9,40,41},{10,11,42,4..., dimensions={0} | all-to-all | bytes 294912 | tf_op jit(solution)/shard_map/all_to_all | solution.py:608
  28.0 0.1 second.1
  28.1 16.7 %all_to_all.21.second_ref = f32[4,3,32,128]{3,2,1,0:T(8,128)S(1)} all-to-all(f32[4,3,32,128]{3,2,1,0:T(8,128)S(1)} %second.1), channel_id=1, replica_groups={{33,34,65,66},{35,36,67,68},{37,38,69,70},{39,40,71,72},{41,42,73,74},{..., dimensions={0} | all-to-all | bytes 393216 | tf_op jit(solution)/shard_map/all_to_all | solution.py:608
  44.8 1.3 %images.1 = (f32[3,128,128]{2,1,0:T(8,128)S(1)}, f32[3,128,128]{2,1,0:T(8,128)S(1)}, f32[3,128,128]{2,1,0:T(8,128)S(1)}, f32[16,2,128]{2,1,0:T(2,128)S(1)}, bf16[6,24,16,128]{3,2,1,0:T(8,128)(2,1)}) custom-call(f32[1,24]{1,0:T(1,128)S(1)} %get-tuple-element.30.shift_ref, f32[3,128,128]{2,1,0:T(8,128)S(1)} %get-tuple-element.47.b_ref, ...), custom_call_target="tpu_custom_call" | custom-call | tf_op jit(solution)/shard_map/images/pallas_call | solution.py:506
  46.1 14.5 %all_to_all.22.in_ref = f32[16,2,128]{2,1,0:T(2,128)S(1)} all-to-all(f32[16,2,128]{2,1,0:T(2,128)S(1)} %get-tuple-element.51), channel_id=1, replica_groups=mesh['panel'=2,'lat'=8,'lon'=32] {'panel','lat'}, dimensions={0} | all-to-all | bytes 32768 | tf_op jit(solution)/shard_map/all_to_all | solution.py:628
  60.7 18.4 %all_to_all.23.s_ref = f32[32,2,128]{2,1,0:T(2,128)S(1)} all-to-all(f32[32,2,128]{2,1,0:T(2,128)S(1)} %relay.1), channel_id=1, replica_groups=mesh['panel'=2,'lat'=8,'lon'=32] {'lon'}, dimensions={0} | all-to-all | bytes 65536 | tf_op jit(solution)/shard_map/all_to_all | solution.py:629
  79.1 1.1 %iterate.1 = (f32[384,128]{1,0:T(8,128)}, f32[384,128]{1,0:T(8,128)}) custom-call(f32[1,24]{1,0:T(1,128)S(1)} %get-tuple-element.30.shift_ref, f32[32,2,128]{2,1,0:T(2,128)S(1)} %all_to_all.23.s_ref, f32[3,128,128]{2,1,0:T(8,128)S(1)} %get-tuple-element.47.b_ref, f32[3,128,128]{2,1,0:T(8,128)S(1)} %get-tuple-element.52.c_ref, ...), custom_call_target="tpu_custom_call" | custom-call | tf_op jit(solution)/shard_map/iterate/pallas_call | solution.py:573
  (10 shorter events, 0.0 us)
Async XLA Ops:
  2.3 8.7 %collective-permute-start = (bf16[3,24,16,128]{3,2,1,0:T(8,128)(2,1)S(1)}, bf16[3,24,16,128]{3,2,1,0:T(8,128)(2,1)S(1)}, u32[]{:S(2)}, u32[]{:S(2)}) collective-permute-start(bf16[3,24,16,128]{3,2,1,0:T(8,128)(2,1)S(1)} %get-tuple-element.37), channel_id=1, source_target_pairs={{0,1},{1,2},{2,3},{3,4},{4,5},{5,6},{6,7},{7,8},{8,9},{9,10},{10,1... | collective-permute-start | bytes 884744 | tf_op jit(solution)/shard_map/ppermute | solution.py:583
  6.3 1.6 %copy-start = (f32[1,24,16,128]{3,2,1,0:T(8,128)S(1)}, f32[1,24,16,128]{3,2,1,0:T(8,128)}, u32[]{:S(2)}) copy-start(f32[1,24,16,128]{3,2,1,0:T(8,128)} %param.10) | copy-start | bytes 589828
  6.3 1.6 %copy-start.2 = (f32[24,24]{1,0:T(8,128)S(1)}, f32[24,24]{1,0:T(8,128)}, u32[]{:S(2)}) copy-start(f32[24,24]{1,0:T(8,128)} %proj_ref.1) | copy-start | bytes 6916
  6.3 1.6 %copy-start.3 = (f32[6,24]{1,0:T(8,128)S(1)}, f32[6,24]{1,0:T(8,128)}, u32[]{:S(2)}) copy-start(f32[6,24]{1,0:T(8,128)} %mix_ref.1) | copy-start | bytes 1732
  6.3 1.6 %copy-start.4 = (s32[1,1,256,4]{2,3,1,0:T(4,128)S(1)}, s32[1,1,256,4]{2,3,1,0:T(4,128)}, u32[]{:S(2)}) copy-start(s32[1,1,256,4]{2,3,1,0:T(4,128)} %param.16) | copy-start | bytes 12292
  6.4 1.6 %copy-start.5 = (f32[1,1,256,4]{2,3,1,0:T(4,128)S(1)}, f32[1,1,256,4]{2,3,1,0:T(4,128)}, u32[]{:S(2)}) copy-start(f32[1,1,256,4]{2,3,1,0:T(4,128)} %param.17) | copy-start | bytes 12292
  6.4 1.6 %copy-start.7 = (f32[24]{0:T(128)S(1)}, f32[24]{0:T(128)}, u32[]{:S(2)}) copy-start(f32[24]{0:T(128)} %param.14) | copy-start | bytes 292
  6.6 1.4 %copy-start.1 = (s32[1,16,32]{2,1,0:T(8,128)S(1)}, s32[1,16,32]{2,1,0:T(8,128)}, u32[]{:S(2)}) copy-start(s32[1,16,32]{2,1,0:T(8,128)} %param.11) | copy-start | bytes 6148
  6.6 4.4 %collective-permute-start.1 = (bf16[3,16,128]{2,1,0:T(8,128)(2,1)S(1)}, bf16[3,16,128]{2,1,0:T(8,128)(2,1)S(1)}, u32[]{:S(2)}, u32[]{:S(2)}) collective-permute-start(bf16[3,16,128]{2,1,0:T(8,128)(2,1)S(1)} %pack_east.1), channel_id=1, source_target_pairs={{1,0},{2,1},{3,2},{4,3},{5,4},{6,5},{7,6},{8,7},{9,8},{10,9},{11,1... | collective-permute-start | bytes 36872 | tf_op jit(solution)/shard_map/ppermute | solution.py:583
  7.9 0.7 copy-start.6
